TPU v7x, 256 devices: a whole 4x4x8 slice. The times are simulated.
256 devices in a mesh: seq: 16 (over y, x), grp: 8 (over z), store: 2 (over core).
Axes of the slice: x: 4, y: 4, z: 8, core: 2. Of those that a mesh axis runs over, the one named last changes fastest.
Arguments:
- query: bfloat16 [8, 2, 32, 2048, 128], P('grp', 'store', None, 'seq')
- kv_store: bfloat16 [256, 2, 2, 32, 128, 128], P(('grp', 'store'), None, None, 'seq'), may hold values from -6 to 6
- nbr_owner: int32 [8, 32, 2], P('grp'), may hold values from 0 to 15, all different within a row; in each aligned block of 32 rows (0 to 31, 32 to 63, ..., all dimensions but the last counted through in order) at most 6 rows name the same one
- nbr_block: int32 [8, 32, 2], P('grp'), may hold values from 0 to 15
- d_out: bfloat16 [8, 2, 32, 2048, 128], P('grp', 'store', None, 'seq'), may hold values from -6 to 6
Outputs:
- attn_out: bfloat16 [8, 2, 32, 2048, 128], P('grp', 'store', None, 'seq')
- d_query: bfloat16 [8, 2, 32, 2048, 128], P('grp', 'store', None, 'seq')
- d_kv: bfloat16 [256, 2, 2, 32, 128, 128], P(('grp', 'store'), None, None, 'seq')
Inputs may be any that keep to these rules, and one draw needn't show every extreme that they name: `nbr_owner`: among one group's 32 spans no store shard is named more than 6 times, a bound that some block reaches; the 2 neighbours of a span lie in different shards; every shard is named somewhere.
All inputs are finite; a program needn't handle non-finite values.
Results may differ from a plain program's by a relative error of at most 0.027.
Values may be sent and summed in bfloat16 or wider, within the bound.
No kernel may reach another device: no remote copies, remote signals or barrier semaphores. Data moves between devices by JAX's collectives and lax.ppermute only.
A program may use at most 128 MiB of HBM per device.

v0:
```python
import math

import jax
import jax.numpy as jnp
from jax import lax
from jax.sharding import PartitionSpec as P

SPAN = 64
NBRS = 2


def on_device(query, kv_store, nbr_owner, nbr_block, d_out):
    grp_count = lax.axis_size("grp")
    nstore = lax.axis_size("store")
    owners = grp_count * nstore
    heads_query = lax.all_to_all(query, "seq", split_axis=2, concat_axis=3, tiled=True)
    heads_grad = lax.all_to_all(d_out, "seq", split_axis=2, concat_axis=3, tiled=True)
    pair_count = heads_query.shape[2]
    group_tokens = heads_query.shape[3]
    head_dim = heads_query.shape[4]
    group_spans = group_tokens // SPAN
    capacity = 3 * NBRS * group_spans // (2 * owners)
    slot_count = owners * capacity
    score_scale = 1.0 / math.sqrt(head_dim)
    query_rows = heads_query.reshape(pair_count, group_spans, SPAN, head_dim)
    grad_rows = heads_grad.reshape(pair_count, group_spans, SPAN, head_dim)
    owner_flat = nbr_owner.reshape(-1)
    block_flat = nbr_block.reshape(-1)
    instances = owner_flat.shape[0]
    position = jnp.arange(instances, dtype=jnp.int32)
    earlier = (owner_flat[:, None] == owner_flat[None, :]) & (position[None, :] < position[:, None])
    owner_rank = jnp.sum(earlier.astype(jnp.int32), axis=1)
    slot_index = owner_flat * capacity + owner_rank
    places = jnp.arange(slot_count, dtype=jnp.int32)
    slot_hits = (slot_index[:, None] == places[None, :]).astype(jnp.int32)
    wanted = jnp.sum(slot_hits * block_flat[:, None], axis=0).reshape(owners, capacity)
    asked_ids = lax.all_to_all(wanted, ("grp", "store"), split_axis=0, concat_axis=0, tiled=True)
    asked_count = asked_ids.shape[1]
    asked_grid = asked_ids.reshape(grp_count, nstore, asked_count)
    half_index = jnp.arange(nstore, dtype=jnp.int32).reshape(1, nstore, 1)
    picked = kv_store[asked_grid, :, half_index]
    served = picked.reshape(owners, asked_count, 2, pair_count, picked.shape[5], head_dim)
    replied = lax.all_to_all(served, ("grp", "store"), split_axis=0, concat_axis=0, tiled=True)
    block_len = replied.shape[4]
    slot_rows = replied.reshape(slot_count, 2, pair_count, block_len, head_dim)
    instance = slot_rows[slot_index].reshape(group_spans, NBRS, 2, pair_count, block_len, head_dim)
    context = jnp.transpose(instance, (2, 3, 0, 1, 4, 5)).reshape(
        2, pair_count, group_spans, NBRS * block_len, head_dim
    )
    key_rows = context[0]
    value_rows = context[1]
    scores = (
        jnp.einsum("hcqd,hckd->hcqk", query_rows, key_rows, preferred_element_type=jnp.float32)
        * score_scale
    )
    row_top = jnp.max(scores, axis=-1, keepdims=True)
    weights = jnp.exp(scores - row_top)
    attn_prob = weights / jnp.sum(weights, axis=-1, keepdims=True)
    prob_bf = attn_prob.astype(jnp.bfloat16)
    attended = jnp.einsum(
        "hcqk,hckd->hcqd", prob_bf, value_rows, preferred_element_type=jnp.float32
    ).astype(jnp.bfloat16)
    row_delta = jnp.sum(grad_rows.astype(jnp.float32) * attended.astype(jnp.float32), axis=-1)
    grad_prob = jnp.einsum(
        "hcqd,hckd->hcqk", grad_rows, value_rows, preferred_element_type=jnp.float32
    )
    dscore = attn_prob * (grad_prob - row_delta[..., None])
    dscore_bf = dscore.astype(jnp.bfloat16)
    grad_query = (
        jnp.einsum("hcqk,hckd->hcqd", dscore_bf, key_rows, preferred_element_type=jnp.float32)
        * score_scale
    ).astype(jnp.bfloat16)
    grad_keys = (
        jnp.einsum("hcqk,hcqd->hckd", dscore_bf, query_rows, preferred_element_type=jnp.float32)
        * score_scale
    ).astype(jnp.bfloat16)
    grad_values = jnp.einsum(
        "hcqk,hcqd->hckd", prob_bf, grad_rows, preferred_element_type=jnp.float32
    ).astype(jnp.bfloat16)
    block_grad = jnp.stack((grad_keys, grad_values), axis=0).reshape(
        2, pair_count, group_spans, NBRS, block_len, head_dim
    )
    block_grad = jnp.transpose(block_grad, (2, 3, 0, 1, 4, 5)).reshape(
        instances, 2, pair_count, block_len, head_dim
    )
    grad_slots = jnp.zeros((slot_count, 2, pair_count, block_len, head_dim), jnp.bfloat16)
    grad_slots = (
        grad_slots.at[slot_index]
        .set(block_grad)
        .reshape(owners, capacity, 2, pair_count, block_len, head_dim)
    )
    returned = lax.all_to_all(grad_slots, ("grp", "store"), split_axis=0, concat_axis=0, tiled=True)
    block_len = kv_store.shape[4]
    blocks = kv_store.shape[0]
    ret_grid = returned.reshape(grp_count, nstore, capacity, -1)
    ids_grid = asked_ids.reshape(grp_count, nstore, capacity)
    block_range = jnp.arange(blocks, dtype=jnp.int32)
    half_sums = []
    for store_half in range(nstore):
        half_ids = ids_grid[:, store_half].reshape(-1)
        onehot = (block_range[:, None] == half_ids[None, :]).astype(jnp.bfloat16)
        half_grads = ret_grid[:, store_half].reshape(grp_count * capacity, -1)
        summed = jnp.dot(onehot, half_grads, preferred_element_type=jnp.float32)
        half_sums.append(summed.reshape(blocks, 2, pair_count, block_len, head_dim))
    d_kv = jnp.stack(half_sums, axis=2).astype(jnp.bfloat16)
    out_heads = attended.reshape(1, 1, pair_count, group_tokens, head_dim)
    grad_heads_out = grad_query.reshape(1, 1, pair_count, group_tokens, head_dim)
    attn_out = lax.all_to_all(out_heads, "seq", split_axis=3, concat_axis=2, tiled=True)
    d_query = lax.all_to_all(grad_heads_out, "seq", split_axis=3, concat_axis=2, tiled=True)
    return (attn_out, d_query, d_kv)


def solution(mesh):
    in_specs = (
        P("grp", "store", None, "seq", None),
        P(("grp", "store"), None, None, "seq", None, None),
        P("grp", None, None),
        P("grp", None, None),
        P("grp", "store", None, "seq", None),
    )
    out_specs = (
        P("grp", "store", None, "seq", None),
        P("grp", "store", None, "seq", None),
        P(("grp", "store"), None, None, "seq", None, None),
    )
    return jax.shard_map(
        on_device, mesh=mesh, in_specs=in_specs, out_specs=out_specs, check_vma=False
    )
```

profile of v0, /device:TPU:2, one launch (start us, length us, event | category | flops | bytes accessed | tf_op | source)
XLA Modules:
  0.0 891.6 jit_solution(6365892472241093906)
XLA Ops:
  2.7 15.9 %all_to_all.85 = s32[16,1,6]{2,1,0:T(1,128)S(1)} all-to-all(s32[16,1,6]{2,1,0:T(1,128)S(1)} %bitcast.156), channel_id=1, replica_groups=mesh['seq'=16,'grp'=8,'store'=2] {'grp','store'}, dimensions={0} | all-to-all | bytes 768 | tf_op jit(solution)/shard_map/all_to_all | solution.py:37
  18.7 23.4 %all_to_all.86 = bf16[1,1,32,128,128]{4,3,1,0,2:T(8,128)(2,1)} all-to-all(bf16[1,1,32,128,128]{4,3,1,0,2:T(8,128)(2,1)} %bitcast.146), channel_id=1, replica_groups=mesh['seq'=16,'grp'=8,'store'=2] {'seq'}, dimensions={2} | all-to-all | bytes 2097152 | tf_op jit(solution)/shard_map/all_to_all | solution.py:16
  42.1 4.9 all-to-all-start.4
  47.1 9.3 %gather_fusion = bf16[96,2,2,128,128]{4,3,2,1,0:T(8,128)(2,1)} fusion(bf16[16,2,2,2,128,128]{5,4,3,2,1,0:T(8,128)(2,1)} %param.6, s32[96]{0:T(128)S(1)} %reshape.165), kind=kCustom, calls=%fused_computation | custom fusion | bytes 25166592 | tf_op jit(solution)/shard_map/gather | solution.py:41
  56.4 5.8 all-to-all-done.4
  62.2 5.2 all-to-all-start.1
  70.0 271.4 %all-to-all-done.1 = bf16[16,6,2,2,128,128]{5,4,3,2,1,0:T(8,128)(2,1)} async-done(((bf16[16,6,2,2,128,128]{5,4,3,2,1,0:T(8,128)(2,1)}), bf16[16,6,2,2,128,128]{5,4,3,2,1,0:T(8,128)(2,1)}, u32[]{:S(2)}, u32[]{:S(2)}) %all-to-all-start.1) | async-done | bytes 12582944 | tf_op jit(solution)/shard_map/all_to_all | solution.py:43
  341.5 10.1 %gather_fusion.1 = bf16[64,2,2,128,128]{4,3,2,1,0:T(8,128)(2,1)} fusion(bf16[96,2,2,128,128]{4,3,2,1,0:T(8,128)(2,1)} %bitcast.3, s32[1024]{0:T(1024)S(1)} %pad_clamp_fusion), kind=kCustom, calls=%fused_computation.1 | custom fusion | bytes 16777472 | tf_op jit(solution)/shard_map/gather | solution.py:46
  351.6 10.3 %copy.84 = bf16[32,2,2,2,128,128]{5,4,1,0,3,2:T(8,128)(2,1)} copy(bf16[32,2,2,2,128,128]{5,4,3,2,1,0:T(8,128)(2,1)} %bitcast.129) | data formatting | bytes 16777216 | tf_op jit(solution)/shard_map/reshape | solution.py:46
  361.9 5.2 fusion.40
  372.3 13.0 %multiply_reduce_fusion = (f32[2,32,64]{2,1,0:T(8,128)S(1)}, bf16[2,32,64,128]{3,2,1,0:T(8,128)(2,1)}) fusion(bf16[2,32,64,128]{3,2,1,0:T(8,128)(2,1)S(1)} %bitcast.150, bf16[2,32,256,128]{3,2,1,0:T(8,128)(2,1)} %bitcast.143, f32[2,32,64]{2,1,0:T(8,128)S(1)} %get-tuple-element.21, f32[2,32,256,64]{2,3,1,0:T(8,128)} %copy-done.3), kind=kOutput, calls=%fused_computation.23 | convolution fusion | flops 276300032 | bytes 10518528 | tf_op jit(solution)/shard_map/hcqk,hckd->hcqd/dot_general | solution.py:60
  385.3 3.9 copy.58
  389.2 4.8 all-to-all-start.3
  394.0 6.3 fusion.5
  401.6 9.4 %copy.62 = bf16[1,1,2,2048,128]{4,2,1,0,3:T(2,128)(2,1)} copy(bf16[1,1,2,2048,128]{4,3,2,1,0:T(8,128)(2,1)S(1)} %bitcast.139) | data formatting | bytes 2097152 | tf_op jit(solution)/shard_map/reshape | solution.py:107
  411.1 7.8 all-to-all-start.5
  418.9 14.1 %convolution_convert_fusion = bf16[2,32,256,128]{3,2,1,0:T(8,128)(2,1)} fusion(bf16[2,32,64,128]{3,2,1,0:T(8,128)(2,1)} %bitcast.149, f32[2,32,64]{2,1,0:T(8,128)S(1)} %get-tuple-element.21, f32[2,32,256,64]{2,3,1,0:T(8,128)} %copy-done.3), kind=kOutput, calls=%fused_computation.19 | convolution fusion | flops 275779840 | bytes 9453568 | tf_op jit(solution)/shard_map/hcqk,hcqd->hckd/dot_general | solution.py:77
  436.1 6.2 maximum_bitcast_fusion
  442.3 10.3 %copy.64 = bf16[32,2,2,2,128,128]{5,4,3,2,1,0:T(8,128)(2,1)} copy(bf16[32,2,2,2,128,128]{5,4,1,0,3,2:T(8,128)(2,1)} %maximum_bitcast_fusion) | data formatting | bytes 16777216 | tf_op jit(solution)/shard_map/transpose | solution.py:83
  452.6 7.7 broadcast_in_dim.5
  460.3 22.2 %scatter_fusion = bf16[96,2,2,128,128]{4,3,2,1,0:T(8,128)(2,1)} fusion(bf16[96,2,2,128,128]{4,3,2,1,0:T(8,128)(2,1)} %broadcast_in_dim.5, s32[64]{0:T(128)S(1)} %fusion.27, bf16[64,2,2,128,128]{4,3,2,1,0:T(8,128)(2,1)} %bitcast.130), kind=kCustom, calls=%fused_computation.2 | custom fusion | bytes 25166080 | tf_op jit(solution)/shard_map/scatter | solution.py:89
  482.5 5.1 all-to-all-start.6
  491.4 270.2 %all-to-all-done.6 = bf16[16,6,2,2,128,128]{5,4,3,2,1,0:T(8,128)(2,1)} async-done(((bf16[16,6,2,2,128,128]{5,4,3,2,1,0:T(8,128)(2,1)}), bf16[16,6,2,2,128,128]{5,4,3,2,1,0:T(8,128)(2,1)}, u32[]{:S(2)}, u32[]{:S(2)}) %all-to-all-start.6) | async-done | bytes 12582944 | tf_op jit(solution)/shard_map/all_to_all | solution.py:92
  761.6 10.8 %copy.65 = bf16[16,6,2,2,128,128]{5,4,3,2,0,1:T(8,128)(2,1)} copy(bf16[16,6,2,2,128,128]{5,4,3,2,1,0:T(8,128)(2,1)} %all-to-all-done.6) | data formatting | bytes 25165824 | tf_op jit(solution)/shard_map/all_to_all | solution.py:92
  772.4 29.1 %reshape.162 = bf16[8,2,6,65536]{3,1,0,2:T(2,128)(2,1)} reshape(bf16[16,6,2,2,128,128]{5,4,3,2,0,1:T(8,128)(2,1)} %copy.65) | data formatting | bytes 25165824 | tf_op jit(solution)/shard_map/reshape | solution.py:95
  801.5 25.1 %fusion.39 = (bf16[8,1,6,65536]{3,1,0,2:T(2,128)(2,1)}, bf16[8,1,6,65536]{3,1,0,2:T(2,128)(2,1)}) fusion(bf16[8,2,6,65536]{3,1,0,2:T(2,128)(2,1)} %reshape.162), kind=kLoop, calls=%fused_computation.52 | loop fusion | bytes 25165824 | tf_op jit(solution)/shard_map/slice | solution.py:102
  826.6 14.6 %copy.66 = bf16[8,1,6,65536]{3,2,0,1:T(8,128)(2,1)} copy(bf16[8,1,6,65536]{3,1,0,2:T(2,128)(2,1)} %get-tuple-element.17) | data formatting | bytes 12582912 | tf_op jit(solution)/shard_map/slice | solution.py:102
  841.2 6.4 reshape_squeeze.6
  847.6 7.1 copy.73
  854.7 14.6 %copy.68 = bf16[8,1,6,65536]{3,2,0,1:T(8,128)(2,1)} copy(bf16[8,1,6,65536]{3,1,0,2:T(2,128)(2,1)} %get-tuple-element.18) | data formatting | bytes 12582912 | tf_op jit(solution)/shard_map/slice | solution.py:102
  869.4 6.5 reshape_squeeze.7
  875.9 4.5 copy.74
  (46 shorter events, 29.0 us)
Async XLA Ops:
  42.1 20.1 %all-to-all-start.4 = ((bf16[1,1,32,128,128]{4,3,1,0,2:T(8,128)(2,1)}), bf16[1,1,32,128,128]{4,3,1,0,2:T(8,128)(2,1)S(1)}, u32[]{:S(2)}, u32[]{:S(2)}) async-start(bf16[1,1,32,128,128]{4,3,1,0,2:T(8,128)(2,1)} %bitcast.147), calls=%async_computation.4 | async-start | bytes 2097152 | tf_op jit(solution)/shard_map/all_to_all | solution.py:17
  62.2 5.2 copy-start.6
  62.2 279.3 %all-to-all-start.1 = ((bf16[16,6,2,2,128,128]{5,4,3,2,1,0:T(8,128)(2,1)}), bf16[16,6,2,2,128,128]{5,4,3,2,1,0:T(8,128)(2,1)}, u32[]{:S(2)}, u32[]{:S(2)}) async-start(bf16[16,6,2,2,128,128]{5,4,3,2,1,0:T(8,128)(2,1)} %bitcast.126), calls=%async_computation.1 | async-start | bytes 25165824 | tf_op jit(solution)/shard_map/all_to_all | solution.py:43
  367.1 2.0 copy-start
  369.1 3.2 copy-start.3
  369.1 3.2 copy-start.5
  389.2 21.9 %all-to-all-start.3 = ((bf16[1,1,2,2048,128]{4,2,1,0,3:T(2,128)(2,1)}), bf16[1,1,2,2048,128]{4,2,1,0,3:T(2,128)(2,1)S(1)}, u32[]{:S(2)}, u32[]{:S(2)}) async-start(bf16[1,1,2,2048,128]{4,2,1,0,3:T(2,128)(2,1)} %copy.58), calls=%async_computation.3 | async-start | bytes 2097152 | tf_op jit(solution)/shard_map/all_to_all | solution.py:108
  394.0 6.3 copy-start.1
  400.3 1.3 copy-start.4
  411.1 71.4 %all-to-all-start.5 = ((bf16[1,1,2,2048,128]{4,2,1,0,3:T(2,128)(2,1)}), bf16[1,1,2,2048,128]{4,2,1,0,3:T(2,128)(2,1)}, u32[]{:S(2)}, u32[]{:S(2)}) async-start(bf16[1,1,2,2048,128]{4,2,1,0,3:T(2,128)(2,1)} %copy.62), calls=%async_computation.5 | async-start | bytes 2097152 | tf_op jit(solution)/shard_map/all_to_all | solution.py:109
  482.5 279.1 %all-to-all-start.6 = ((bf16[16,6,2,2,128,128]{5,4,3,2,1,0:T(8,128)(2,1)}), bf16[16,6,2,2,128,128]{5,4,3,2,1,0:T(8,128)(2,1)}, u32[]{:S(2)}, u32[]{:S(2)}) async-start(bf16[16,6,2,2,128,128]{5,4,3,2,1,0:T(8,128)(2,1)} %bitcast.125), calls=%async_computation.6 | async-start | bytes 25165824 | tf_op jit(solution)/shard_map/all_to_all | solution.py:92
  875.9 4.6 copy-start.2
where the time goes:
time: 896 us; the launch traced here: 892 us
  waiting for transfers between devices  547 us (61%)
  local copies, waits for them, and re-layouts  220 us (25%)
  matrix products  46.3 us (5%)
  blocking collectives  39.3 us (4%)
  starting transfers between devices  27.9 us (3%)
  other arithmetic  9.73 us (1%)
    all_to_all x1, waiting for transfers between devices, on_device(): lax.all_to_all(served, ('grp', 'store'), split_axis=0, concat_axis=0, til...  271 us
    all_to_all x1, waiting for transfers between devices, on_device(): lax.all_to_all(grad_slots, ('grp', 'store'), split_axis=0, concat_axis=0,...  270 us
    slice x3, local copies, waits for them, and re-layouts, on_device(): half_grads = ret_grid[:, store_half].reshape(grp_count * capacity, -1)  54.4 us
    reshape x1, local copies, waits for them, and re-layouts, on_device(): ret_grid = returned.reshape(grp_count, nstore, capacity, -1)  29.1 us
    all_to_all x1, blocking collectives, on_device(): lax.all_to_all(query, 'seq', split_axis=2, concat_axis=3, tiled=True)  23.4 us
    scatter x1, local copies, waits for them, and re-layouts, on_device(): grad_slots = grad_slots.at[slot_index].set(block_grad).reshape(owners, ca...  22.2 us
  transfers between devices with their start and end apart: 5, of which 3 were waited for; matrix products, arithmetic and copies ran while one was open for 11% of the time, Pallas kernels for 0%

commit v1 on v0

v1 whole, which is shorter than its diff:
```python
import functools
import math

import jax
import jax.numpy as jnp
from jax import lax
from jax.experimental import pallas as pl
from jax.experimental.pallas import tpu as pltpu
from jax.sharding import PartitionSpec as P

RING = 8
CAP = 6
SLOTS = 2 * CAP
ROWS = RING * SLOTS
SPAN = 64
DH = 128
SEQ = 16
INST = 64
SPANS = INST // 2
BLK = 16
UNROLL = 4
SCALE = 1.0 / math.sqrt(DH)
F32 = jnp.float32
BF16 = jnp.bfloat16

SMEM = pl.BlockSpec(memory_space=pltpu.SMEM)
VMEM = pl.BlockSpec(memory_space=pltpu.VMEM)
ANY = pl.BlockSpec(memory_space=pl.ANY)

STAT_ROWS = RING * 16
SENT = 64
R_STAT, R_BLK, R_COUNT, R_SIZE = 128, 256, 384, 512


def cost(flops, nbytes):
    return pl.CostEstimate(flops=flops, bytes_accessed=nbytes, transcendentals=0)


def send_table_kernel(place, owner, table, count):
    for o in range(RING * 2):
        count[o] = 0

    def step(i, carry):
        own = owner[i]
        rank = count[own]
        count[own] = rank + 1
        chip = own >> 1
        slot = (own & 1) * CAP + rank
        table[i] = ((chip - place[0]) & (RING - 1)) * SLOTS + slot
        table[SENT + i] = chip * 16 + slot
        return carry

    lax.fori_loop(0, INST, step, 0)


def recv_table_kernel(place, names, table, count):
    def group(d, total):
        source = (place[0] - d) & (RING - 1)
        count[0] = 0
        count[1] = 0

        def step(i, total):
            own = names[source, i]
            core = own & 1
            rank = count[core]
            mine = ((own >> 1) == place[0]).astype(jnp.int32)
            count[core] = rank + mine
            slot = core * CAP + rank
            table[total] = d * SLOTS + slot
            table[R_STAT + total] = source * 16 + slot
            table[R_BLK + total] = core * BLK + names[source, INST + i]
            return total + mine

        return lax.fori_loop(0, INST, step, total)

    total = lax.fori_loop(0, RING, group, 0)
    for u in range(UNROLL):
        table[total + u] = ROWS
        table[R_STAT + total + u] = STAT_ROWS
        table[R_BLK + total + u] = 0
    table[R_COUNT] = total


def pack_kernel(table, rows, after, *refs):
    outs, stage, sems = refs[:RING], refs[RING], refs[RING + 1]

    def step(i, carry):
        row = table[i]
        span = i >> 1
        start = pl.multiple_of((span & 1) * SPAN, SPAN)
        for kind in range(2):
            stage[row, kind] = rows[span >> 1, kind, pl.ds(start, SPAN), :]
        return carry

    lax.fori_loop(0, INST, step, 0, unroll=4)
    copies = [
        pltpu.make_async_copy(stage.at[pl.ds(d * SLOTS, SLOTS)], outs[d], sems.at[d])
        for d in range(RING)
    ]
    for copy in copies:
        copy.start()
    for copy in copies:
        copy.wait()


def load_rows(parts, stage, sems):
    copies = [
        pltpu.make_async_copy(parts[d], stage.at[pl.ds(d * SLOTS, SLOTS)], sems.at[d])
        for d in range(RING)
    ]
    for copy in copies:
        copy.start()
    return copies


def load_store(pair, core, own, other, store, sems):
    mine = pltpu.make_async_copy(
        own.at[:, :, core, pair], store.at[pl.ds(core * BLK, BLK)], sems.at[RING]
    )
    theirs = pltpu.make_async_copy(
        other.at[:, :, pair], store.at[pl.ds((1 - core) * BLK, BLK)], sems.at[RING + 1]
    )
    mine.start()
    theirs.start()
    return [mine, theirs]


def dot(a, b, dims):
    return lax.dot_general(a, b, (dims, ((), ())), preferred_element_type=F32)


NT = ((1,), (1,))
NN = ((1,), (0,))
TN = ((0,), (0,))


def stat_kernel(pair, place, table, *refs):
    parts, own, other, out, stage, store, stats, sems = (
        refs[:RING],
        *refs[RING : RING + 7],
    )
    copies = load_rows(parts, stage, sems) + load_store(pair, place[1], own, other, store, sems)
    stage[ROWS] = jnp.zeros(stage.shape[1:], BF16)
    stats[...] = jnp.zeros(stats.shape, F32)
    for copy in copies:
        copy.wait()

    def step(it, carry):
        for u in range(UNROLL):
            n = it * UNROLL + u
            row, srow, block = table[n], table[R_STAT + n], table[R_BLK + n]
            score = dot(store[block, 0], stage[row, 0], NT) * SCALE
            gprob = dot(store[block, 1], stage[row, 1], NT)
            top = jnp.max(score, axis=0, keepdims=True)
            weight = jnp.exp(score - top)
            total = jnp.sum(weight, axis=0, keepdims=True)
            delta = jnp.sum(weight * gprob, axis=0, keepdims=True) / total
            stats[pl.ds(srow, 1), :] = jnp.concatenate([top + jnp.log(total), delta], axis=1)
        return carry

    lax.fori_loop(0, (table[R_COUNT] + UNROLL - 1) // UNROLL, step, 0)
    out[...] = stats[:STAT_ROWS]


def merge_kernel(table, given, out, first, second, merged):
    def take(c, carry):
        first[pl.ds(c, 1), :] = given[pl.ds(table[SENT + 2 * c], 1), :]
        second[pl.ds(c, 1), :] = given[pl.ds(table[SENT + 2 * c + 1], 1), :]
        return carry

    lax.fori_loop(0, SPANS, take, 0, unroll=8)
    log1, log2 = first[:, :SPAN], second[:, :SPAN]
    top = jnp.maximum(log1, log2)
    both = top + jnp.log(jnp.exp(log1 - top) + jnp.exp(log2 - top))
    delta = jnp.exp(log1 - both) * first[:, SPAN:] + jnp.exp(log2 - both) * second[:, SPAN:]
    merged[...] = jnp.concatenate([both, delta], axis=1)
    out[...] = jnp.zeros(out.shape, F32)

    def put(c, carry):
        row = merged[pl.ds(c, 1), :]
        out[pl.ds(table[SENT + 2 * c], 1), :] = row
        out[pl.ds(table[SENT + 2 * c + 1], 1), :] = row
        return carry

    lax.fori_loop(0, SPANS, put, 0, unroll=8)


def grad_kernel(pair, place, table, given, *refs):
    parts, own, other = refs[:RING], refs[RING], refs[RING + 1]
    outs = refs[RING + 2 : 2 * RING + 2]
    keep, send, stage, store, stats, result, total, sems = refs[2 * RING + 2 :]
    copies = load_rows(parts, stage, sems) + load_store(pair, place[1], own, other, store, sems)
    stage[ROWS] = jnp.zeros(stage.shape[1:], BF16)
    stats[:STAT_ROWS] = given[...]
    stats[STAT_ROWS:] = jnp.zeros((8, DH), F32)

    def clear(b, carry):
        total[b] = jnp.zeros(total.shape[1:], F32)
        return carry

    lax.fori_loop(0, 2 * BLK, clear, 0)
    for copy in copies:
        copy.wait()

    def step(it, carry):
        adds = []
        for u in range(UNROLL):
            n = it * UNROLL + u
            row, srow, block = table[n], table[R_STAT + n], table[R_BLK + n]
            query, grad = stage[row, 0], stage[row, 1]
            key, value = store[block, 0], store[block, 1]
            stat = stats[pl.ds(srow, 1), :]
            score = dot(key, query, NT) * SCALE
            prob = jnp.exp(score - stat[:, :SPAN])
            dscore = (prob * (dot(value, grad, NT) - stat[:, SPAN:])).astype(BF16)
            prob = prob.astype(BF16)
            result[row, 0] = dot(prob, value, TN).astype(BF16)
            result[row, 1] = (dot(dscore, key, TN) * SCALE).astype(BF16)
            total[block, 0] += dot(dscore, query, NN)
            total[block, 1] += dot(prob, grad, NN)
        return carry

    lax.fori_loop(0, (table[R_COUNT] + UNROLL - 1) // UNROLL, step, 0)
    copies = [
        pltpu.make_async_copy(result.at[pl.ds(d * SLOTS, SLOTS)], outs[d], sems.at[d])
        for d in range(RING)
    ]
    for copy in copies:
        copy.start()

    def finish(b, carry):
        for out, core in ((keep, place[1]), (send, 1 - place[1])):
            out[b, 0] = (total[core * BLK + b, 0] * SCALE).astype(BF16)
            out[b, 1] = total[core * BLK + b, 1].astype(BF16)
        return carry

    lax.fori_loop(0, BLK, finish, 0)
    for copy in copies:
        copy.wait()


def unpack_kernel(table, *refs):
    parts, out, stage, sems = refs[:RING], *refs[RING:]
    for copy in load_rows(parts, stage, sems):
        copy.wait()

    def step(c, carry):
        one, two = table[2 * c], table[2 * c + 1]
        start = pl.multiple_of((c & 1) * SPAN, SPAN)
        for kind in range(2):
            summed = stage[one, kind].astype(F32) + stage[two, kind].astype(F32)
            out[c >> 1, kind, pl.ds(start, SPAN), :] = summed.astype(BF16)
        return carry

    lax.fori_loop(0, SPANS, step, 0, unroll=2)


def join_kernel(place, keep0, keep1, got0, got1, out, sems):
    core = place[1]
    copies = []
    for n, (ref, half, pair) in enumerate(
        ((keep0, core, 0), (keep1, core, 1), (got0, 1 - core, 0), (got1, 1 - core, 1))
    ):
        copies.append(pltpu.make_async_copy(ref, out.at[:, :, half, pair], sems.at[n]))
    for copy in copies:
        copy.start()
    for copy in copies:
        copy.wait()


def shape(dims, dtype=BF16):
    return jax.ShapeDtypeStruct(dims, dtype)


PART = (SLOTS, 2, SPAN, DH)
PARAMS = pltpu.CompilerParams(vmem_limit_bytes=40 * 1024 * 1024)
STAGE = pltpu.VMEM((ROWS + 1, 2, SPAN, DH), BF16)
STORE = pltpu.VMEM((2 * BLK, 2, 128, DH), BF16)
STATS = pltpu.VMEM((STAT_ROWS + 8, DH), F32)
SEMS = pltpu.SemaphoreType.DMA((RING + 2,))


def ring_send(parts, sign):
    got = [None] * RING
    for d in (4, 3, 5, 2, 6, 1, 7):
        pairs = [(i, (i + sign * d) % RING) for i in range(RING)]
        got[d] = lax.ppermute(parts[d], "grp", pairs)
    got[0] = parts[0]
    return got


def on_device(query, kv_store, nbr_owner, nbr_block, d_out):
    core = lax.axis_index("store")
    place = jnp.stack([lax.axis_index("grp"), core]).astype(jnp.int32)
    owner = nbr_owner.reshape(INST)
    names = jnp.concatenate([owner, nbr_block.reshape(INST)]).reshape(1, 2 * INST)
    names = lax.all_gather(names, "grp", tiled=True)
    swap = [(0, 1), (1, 0)]
    kv_other = lax.ppermute(
        lax.dynamic_index_in_dim(kv_store, 1 - core, 2, keepdims=False), "store", swap
    )

    send_table = pl.pallas_call(
        send_table_kernel,
        out_shape=shape((2 * INST,), jnp.int32),
        in_specs=[SMEM, SMEM],
        out_specs=SMEM,
        scratch_shapes=[pltpu.SMEM((2 * RING,), jnp.int32)],
        name="send_table",
    )(place, owner)
    recv_table = pl.pallas_call(
        recv_table_kernel,
        out_shape=shape((R_SIZE,), jnp.int32),
        in_specs=[SMEM, SMEM],
        out_specs=SMEM,
        scratch_shapes=[pltpu.SMEM((2,), jnp.int32)],
        name="recv_table",
    )(place, names)

    query_rows = query.reshape(SEQ, 2, 128, DH)
    grad_rows = d_out.reshape(SEQ, 2, 128, DH)

    arrived = []
    after = owner
    for pair in range(2):
        rows = jnp.stack([query_rows[:, pair], grad_rows[:, pair]], axis=1)
        rows = lax.all_to_all(rows, "seq", split_axis=0, concat_axis=0, tiled=True)
        parts = pl.pallas_call(
            pack_kernel,
            out_shape=[shape(PART)] * RING,
            in_specs=[SMEM, VMEM, ANY],
            out_specs=[ANY] * RING,
            scratch_shapes=[
                pltpu.VMEM((ROWS, 2, SPAN, DH), BF16),
                pltpu.SemaphoreType.DMA((RING,)),
            ],
            compiler_params=PARAMS,
            cost_estimate=cost(0, 8 << 20),
            name="pack",
        )(send_table, rows, after)
        got = ring_send(parts, 1)
        after = got[1]
        arrived.append(got)

    results = []
    kv_grads = []
    for pair in range(2):
        parts = arrived[pair]
        stats = pl.pallas_call(
            functools.partial(stat_kernel, pair),
            out_shape=shape((STAT_ROWS, DH), F32),
            in_specs=[SMEM, SMEM] + [ANY] * (RING + 2),
            out_specs=VMEM,
            scratch_shapes=[STAGE, STORE, STATS, SEMS],
            compiler_params=PARAMS,
            cost_estimate=cost(8 << 30, 8 << 20),
            name="stats",
        )(place, recv_table, *parts, kv_store, kv_other)
        stats = lax.all_to_all(stats, "grp", split_axis=0, concat_axis=0, tiled=True)
        stats = pl.pallas_call(
            merge_kernel,
            out_shape=shape((STAT_ROWS, DH), F32),
            in_specs=[SMEM, VMEM],
            out_specs=VMEM,
            scratch_shapes=[pltpu.VMEM((SPANS, DH), F32)] * 3,
            name="merge",
        )(send_table, stats)
        stats = lax.all_to_all(stats, "grp", split_axis=0, concat_axis=0, tiled=True)
        outs = pl.pallas_call(
            functools.partial(grad_kernel, pair),
            out_shape=[shape(PART)] * RING + [shape((BLK, 2, 128, DH))] * 2,
            in_specs=[SMEM, SMEM, VMEM] + [ANY] * (RING + 2),
            out_specs=[ANY] * RING + [VMEM, VMEM],
            scratch_shapes=[
                STAGE,
                STORE,
                STATS,
                STAGE,
                pltpu.VMEM((2 * BLK, 2, 128, DH), F32),
                SEMS,
            ],
            compiler_params=PARAMS,
            cost_estimate=cost(16 << 30, 16 << 20),
            name="grads",
        )(place, recv_table, stats, *parts, kv_store, kv_other)
        got = ring_send(outs[:RING], -1)
        kv_grads.append((outs[RING], lax.ppermute(outs[RING + 1], "store", swap)))
        rows = pl.pallas_call(
            unpack_kernel,
            out_shape=shape((SEQ, 2, 128, DH)),
            in_specs=[SMEM] + [ANY] * RING,
            out_specs=VMEM,
            scratch_shapes=[
                pltpu.VMEM((ROWS, 2, SPAN, DH), BF16),
                pltpu.SemaphoreType.DMA((RING,)),
            ],
            compiler_params=PARAMS,
            cost_estimate=cost(0, 8 << 20),
            name="unpack",
        )(send_table, *got)
        results.append(lax.all_to_all(rows, "seq", split_axis=0, concat_axis=0, tiled=True))

    d_kv = pl.pallas_call(
        join_kernel,
        out_shape=shape(kv_store.shape),
        in_specs=[SMEM] + [ANY] * 4,
        out_specs=ANY,
        scratch_shapes=[pltpu.SemaphoreType.DMA((4,))],
        cost_estimate=cost(0, 8 << 20),
        name="join",
    )(place, kv_grads[0][0], kv_grads[1][0], kv_grads[0][1], kv_grads[1][1])
    attn_out = jnp.stack([results[0][:, 0], results[1][:, 0]], axis=1).reshape(query.shape)
    d_query = jnp.stack([results[0][:, 1], results[1][:, 1]], axis=1).reshape(query.shape)
    return (attn_out, d_query, d_kv)


def solution(mesh):
    in_specs = (
        P("grp", "store", None, "seq", None),
        P(("grp", "store"), None, None, "seq", None, None),
        P("grp", None, None),
        P("grp", None, None),
        P("grp", "store", None, "seq", None),
    )
    out_specs = (
        P("grp", "store", None, "seq", None),
        P("grp", "store", None, "seq", None),
        P(("grp", "store"), None, None, "seq", None, None),
    )
    return jax.shard_map(
        on_device, mesh=mesh, in_specs=in_specs, out_specs=out_specs, check_vma=False
    )
```

time: 896 us -> 590 us (0.66)
  waiting for transfers between devices: 547 us -> 153 us
  Pallas kernels: 0 us -> 239 us
  local copies, waits for them, and re-layouts: 220 us -> 33.7 us
  starting transfers between devices: 27.9 us -> 117 us
  matrix products: 46.3 us -> 0 us
    all_to_all x5 -> x6, waiting for transfers between devices: 547 us -> 22 us  [the longest x2 16 us: on_device(): rows = lax.all_to_all(rows, 'seq', split_axis=0, concat_axis=0, tiled=True)]
    pallas_call x0 -> x13, Pallas kernels: none -> 239 us  [the longest x1 129 us: on_device(): pl.pallas_call(join_kernel, out_shape=shape(kv_store.shape), in_specs=[SM...]
    ppermute x0 -> x31, waiting for transfers between devices: none -> 131 us  [the longest x28 131 us: ring_send(): got[d] = lax.ppermute(parts[d], 'grp', pairs)]
    ppermute x0 -> x31, starting transfers between devices: none -> 82.3 us  [the longest x28 81.8 us: ring_send(): got[d] = lax.ppermute(parts[d], 'grp', pairs)]
    slice x5 -> x3, local copies, waits for them, and re-layouts: 59.6 us -> 3.06 us  [the longest x1 1.69 us: on_device(): rows = jnp.stack([query_rows[:, pair], grad_rows[:, pair]], axis=1)]
    reshape x5 -> x2, local copies, waits for them, and re-layouts: 52.8 us -> 0.81 us  [the longest x1 0.7 us: on_device(): owner = nbr_owner.reshape(INST)]
    dot_general x8 -> x0, matrix products: 46.3 us -> none  [the longest x1 14.1 us: on_device(): jnp.einsum('hcqk,hcqd->hckd', prob_bf, grad_rows, preferred_element_type=...]
    scatter x1 -> x0, local copies, waits for them, and re-layouts: 22.2 us -> none  [on_device(): grad_slots = grad_slots.at[slot_index].set(block_grad).reshape(owners, ca...]
  transfers between devices with their start and end apart: 5 -> 37, of which waited for: 3 -> 16; matrix products, arithmetic and copies ran while one was open for 11% -> 1% of each run, Pallas kernels for 0% -> 38%
where the time goes in v1:
time: 590 us; the launch traced here: 593 us
  Pallas kernels  239 us (41%)
  waiting for transfers between devices  153 us (26%)
  starting transfers between devices  117 us (20%)
  blocking collectives  43 us (7%)
  local copies, waits for them, and re-layouts  33.7 us (6%)
    ppermute x28, waiting for transfers between devices, ring_send(): got[d] = lax.ppermute(parts[d], 'grp', pairs)  131 us
    pallas_call x1, Pallas kernels, on_device(): pl.pallas_call(join_kernel, out_shape=shape(kv_store.shape), in_specs=[SM...  129 us
    ppermute x28, starting transfers between devices, ring_send(): got[d] = lax.ppermute(parts[d], 'grp', pairs)  81.8 us
    pallas_call x2, Pallas kernels, on_device(): pl.pallas_call(functools.partial(grad_kernel, pair), out_shape=[shape(PAR...  61 us
    unnamed x88, local copies, waits for them, and re-layouts  26.7 us
    all_to_all x2, blocking collectives, on_device(): lax.all_to_all(stats, 'grp', split_axis=0, concat_axis=0, tiled=True)  24.2 us
    pallas_call x2, Pallas kernels, on_device(): pl.pallas_call(functools.partial(stat_kernel, pair), out_shape=shape((STA...  23.4 us
    all_gather x1, blocking collectives, on_device(): names = lax.all_gather(names, 'grp', tiled=True)  18.8 us
  transfers between devices with their start and end apart: 37, of which 16 were waited for; matrix products, arithmetic and copies ran while one was open for 1% of the time, Pallas kernels for 38%

profile of v1, /device:TPU:2, one launch (start us, length us, event | category | flops | bytes accessed | tf_op | source)
XLA Modules:
  0.0 592.8 jit_solution(16733691996131715650)
XLA Ops:
  3.4 7.5 %all-to-all-start = ((bf16[16,2,128,128]{3,2,1,0:T(8,128)(2,1)}), bf16[16,2,128,128]{3,2,1,0:T(8,128)(2,1)S(1)}, u32[]{:S(2)}, u32[]{:S(2)}) async-start(bf16[16,2,128,128]{3,2,1,0:T(8,128)(2,1)} %pad_maximum_fusion), calls=%async_computation | async-start | bytes 2097152 | tf_op jit(solution)/shard_map/all_to_all | solution.py:327
  15.1 11.5 %all-to-all-done.rows = bf16[16,2,128,128]{3,2,1,0:T(8,128)(2,1)S(1)} async-done(((bf16[16,2,128,128]{3,2,1,0:T(8,128)(2,1)}), bf16[16,2,128,128]{3,2,1,0:T(8,128)(2,1)S(1)}, u32[]{:S(2)}, u32[]{:S(2)}) %all-to-all-start) | async-done | bytes 1048608 | tf_op jit(solution)/shard_map/all_to_all | solution.py:327
  26.7 5.4 all-to-all-start.4
  42.8 4.4 all-to-all-done.4.rows
  47.2 7.3 %collective-permute-done.refs_1_.after = bf16[12,2,64,128]{3,2,1,0:T(8,128)(2,1)S(1)} collective-permute-done((bf16[12,2,64,128]{3,2,1,0:T(8,128)(2,1)}, bf16[12,2,64,128]{3,2,1,0:T(8,128)(2,1)S(1)}, u32[]{:S(2)}, u32[]{:S(2)}) %collective-permute-start) | collective-permute-done | bytes 393248 | tf_op jit(solution)/shard_map/ppermute | solution.py:287
  64.5 12.1 %collective-permute-done.15.refs_1_ = bf16[12,2,64,128]{3,2,1,0:T(8,128)(2,1)S(1)} collective-permute-done((bf16[12,2,64,128]{3,2,1,0:T(8,128)(2,1)S(1)}, bf16[12,2,64,128]{3,2,1,0:T(8,128)(2,1)S(1)}, u32[]{:S(2)}, u32[]{:S(2)}) %collective-permute-start.15) | collective-permute-done | bytes 393248 | tf_op jit(solution)/shard_map/ppermute | solution.py:287
  76.6 23.0 %collective-permute-done.16.refs_2_ = bf16[12,2,64,128]{3,2,1,0:T(8,128)(2,1)S(1)} collective-permute-done((bf16[12,2,64,128]{3,2,1,0:T(8,128)(2,1)S(1)}, bf16[12,2,64,128]{3,2,1,0:T(8,128)(2,1)S(1)}, u32[]{:S(2)}, u32[]{:S(2)}) %collective-permute-start.16) | collective-permute-done | bytes 393248 | tf_op jit(solution)/shard_map/ppermute | solution.py:287
  99.6 19.1 %collective-permute-done.17.refs_3_ = bf16[12,2,64,128]{3,2,1,0:T(8,128)(2,1)S(1)} collective-permute-done((bf16[12,2,64,128]{3,2,1,0:T(8,128)(2,1)S(1)}, bf16[12,2,64,128]{3,2,1,0:T(8,128)(2,1)S(1)}, u32[]{:S(2)}, u32[]{:S(2)}) %collective-permute-start.17) | collective-permute-done | bytes 393248 | tf_op jit(solution)/shard_map/ppermute | solution.py:287
  119.4 7.8 %collective-permute-start.21 = (bf16[12,2,64,128]{3,2,1,0:T(8,128)(2,1)}, bf16[12,2,64,128]{3,2,1,0:T(8,128)(2,1)S(1)}, u32[]{:S(2)}, u32[]{:S(2)}) collective-permute-start(bf16[12,2,64,128]{3,2,1,0:T(8,128)(2,1)} %get-tuple-element.62), channel_id=1, source_target_pairs={{0,14},{2,0},{4,2},{6,4},{8,6},{10,8},{12,10},{14,12},{1,15},{3,1}... | collective-permute-start | bytes 1179656 | tf_op jit(solution)/shard_map/ppermute | solution.py:287
  128.2 18.8 %all-gather.1 = s32[8,1,128]{2,1,0:T(1,128)} all-gather(s32[1,1,128]{2,1,0:T(1,128)S(1)} %add_bitcast_fusion), channel_id=2, replica_groups=mesh['seq'=16,'grp'=8,'store'=2] {'grp'}, dimensions={0}, use_global_device_ids=true | all-gather | bytes 4608 | tf_op jit(solution)/shard_map/all_gather | solution.py:297
  146.9 8.9 %recv_table.1.table = s32[512]{0:T(512)} custom-call(s32[2]{0:T(128)} %pad_add_fusion.place, s32[8,128]{1,0:T(8,128)} %bitcast.30), custom_call_target="tpu_custom_call" | custom-call | tf_op jit(solution)/shard_map/recv_table/pallas_call | solution.py:311
  163.8 11.8 %stats.3 = f32[128,128]{1,0:T(8,128)S(1)} custom-call(s32[2]{0:T(128)S(1)} %copy-done.8, s32[512]{0:T(512)S(1)} %copy-done.10, bf16[12,2,64,128]{3,2,1,0:T(8,128)(2,1)S(1)} %get-tuple-element.55.refs_0_, bf16[12,2,64,128]{3,2,1,0:T(8,128)(2,1)S(1)} %collective-permute-done.15.refs_1_, bf16[12,2,64,128]{3,2,1,0:T(8,128)(2,1)S(1)} %collective-permute-done.16.refs_2_, ...), custom_call_target="tpu_custom_call" | custom-call | flops 8589934592 | bytes 8388608 | tf_op jit(solution)/shard_map/stats/pallas_call | solution.py:349
  175.6 11.5 %all_to_all.64 = f32[8,16,128]{2,1,0:T(8,128)} all-to-all(f32[8,16,128]{2,1,0:T(8,128)S(1)} %bitcast.20), channel_id=1, replica_groups=mesh['seq'=16,'grp'=8,'store'=2] {'grp'}, dimensions={0} | all-to-all | bytes 131072 | tf_op jit(solution)/shard_map/all_to_all | solution.py:359
  214.3 30.4 %grads.3 = (bf16[12,2,64,128]{3,2,1,0:T(8,128)(2,1)S(1)}, bf16[12,2,64,128]{3,2,1,0:T(8,128)(2,1)S(1)}, bf16[12,2,64,128]{3,2,1,0:T(8,128)(2,1)S(1)}, bf16[12,2,...) custom-call(s32[2]{0:T(128)S(1)} %copy-done.9, ...), custom_call_target="tpu_custom_call" | custom-call | flops 17179869184 | bytes 16777216 | tf_op jit(solution)/shard_map/grads/pallas_call | solution.py:369
  250.3 6.6 %collective-permute-start.25 = (bf16[12,2,64,128]{3,2,1,0:T(8,128)(2,1)}, bf16[12,2,64,128]{3,2,1,0:T(8,128)(2,1)S(1)}, u32[]{:S(2)}, u32[]{:S(2)}) collective-permute-start(bf16[12,2,64,128]{3,2,1,0:T(8,128)(2,1)} %get-tuple-element.67), channel_id=1, source_target_pairs={{0,8},{2,10},{4,12},{6,14},{8,0},{10,2},{12,4},{14,6},{1,9},{3,11}... | collective-permute-start | bytes 1179656 | tf_op jit(solution)/shard_map/ppermute | solution.py:287
  261.0 5.6 collective-permute-start.26
  266.5 6.7 %collective-permute-done.22.refs_1_ = bf16[12,2,64,128]{3,2,1,0:T(8,128)(2,1)S(1)} collective-permute-done((bf16[12,2,64,128]{3,2,1,0:T(8,128)(2,1)S(1)}, bf16[12,2,64,128]{3,2,1,0:T(8,128)(2,1)S(1)}, u32[]{:S(2)}, u32[]{:S(2)}) %collective-permute-start.22) | collective-permute-done | bytes 393248 | tf_op jit(solution)/shard_map/ppermute | solution.py:287
  273.2 10.6 %collective-permute-start.27 = (bf16[12,2,64,128]{3,2,1,0:T(8,128)(2,1)}, bf16[12,2,64,128]{3,2,1,0:T(8,128)(2,1)S(1)}, u32[]{:S(2)}, u32[]{:S(2)}) collective-permute-start(bf16[12,2,64,128]{3,2,1,0:T(8,128)(2,1)} %get-tuple-element.69), channel_id=1, source_target_pairs={{0,4},{2,6},{4,8},{6,10},{8,12},{10,14},{12,0},{14,2},{1,5},{3,7},... | collective-permute-start | bytes 1179656 | tf_op jit(solution)/shard_map/ppermute | solution.py:287
  287.0 16.9 %collective-permute-start.28 = (bf16[12,2,64,128]{3,2,1,0:T(8,128)(2,1)}, bf16[12,2,64,128]{3,2,1,0:T(8,128)(2,1)S(1)}, u32[]{:S(2)}, u32[]{:S(2)}) collective-permute-start(bf16[12,2,64,128]{3,2,1,0:T(8,128)(2,1)} %get-tuple-element.70), channel_id=1, source_target_pairs={{0,2},{2,4},{4,6},{6,8},{8,10},{10,12},{12,14},{14,0},{1,3},{3,5},... | collective-permute-start | bytes 1179656 | tf_op jit(solution)/shard_map/ppermute | solution.py:287
  305.0 11.6 %stats.2 = f32[128,128]{1,0:T(8,128)S(1)} custom-call(s32[2]{0:T(128)S(1)} %copy-done.9, s32[512]{0:T(512)S(1)} %copy-done.11, bf16[12,2,64,128]{3,2,1,0:T(8,128)(2,1)S(1)} %copy-done.15, bf16[12,2,64,128]{3,2,1,0:T(8,128)(2,1)S(1)} %collective-permute-done.refs_1_.after, bf16[12,2,64,128]{3,2,1,0:T(8,128)(2,1)S(1)} %copy-done.22, ...), custom_call_target="tpu_custom_call" | custom-call | flops 8589934592 | bytes 8388608 | tf_op jit(solution)/shard_map/stats/pallas_call | solution.py:349
  316.6 12.7 %all_to_all.65 = f32[8,16,128]{2,1,0:T(8,128)} all-to-all(f32[8,16,128]{2,1,0:T(8,128)S(1)} %bitcast.21), channel_id=1, replica_groups=mesh['seq'=16,'grp'=8,'store'=2] {'grp'}, dimensions={0} | all-to-all | bytes 131072 | tf_op jit(solution)/shard_map/all_to_all | solution.py:359
  338.6 4.9 all-to-all-done.2
  343.6 7.2 %all-to-all-start.7 = ((bf16[16,2,128,128]{3,2,1,0:T(8,128)(2,1)}), bf16[16,2,128,128]{3,2,1,0:T(8,128)(2,1)S(1)}, u32[]{:S(2)}, u32[]{:S(2)}) async-start(bf16[16,2,128,128]{3,2,1,0:T(8,128)(2,1)} %unpack.3), calls=%async_computation.7 | async-start | bytes 2097152 | tf_op jit(solution)/shard_map/all_to_all | solution.py:401
  353.7 30.6 %grads.2 = (bf16[12,2,64,128]{3,2,1,0:T(8,128)(2,1)S(1)}, bf16[12,2,64,128]{3,2,1,0:T(8,128)(2,1)S(1)}, bf16[12,2,64,128]{3,2,1,0:T(8,128)(2,1)S(1)}, bf16[12,2,...) custom-call(s32[2]{0:T(128)S(1)} %copy-done.9, ...), custom_call_target="tpu_custom_call" | custom-call | flops 17179869184 | bytes 16777216 | tf_op jit(solution)/shard_map/grads/pallas_call | solution.py:369
  385.4 6.5 %collective-permute-start.11 = (bf16[12,2,64,128]{3,2,1,0:T(8,128)(2,1)S(1)}, bf16[12,2,64,128]{3,2,1,0:T(8,128)(2,1)S(1)}, u32[]{:S(2)}, u32[]{:S(2)}) collective-permute-start(bf16[12,2,64,128]{3,2,1,0:T(8,128)(2,1)S(1)} %get-tuple-element.51), channel_id=1, source_target_pairs={{0,8},{2,10},{4,12},{6,14},{8,0},{10,2},{12,4},{14,6},{1,9},{3,11}... | collective-permute-start | bytes 1179656 | tf_op jit(solution)/shard_map/ppermute | solution.py:287
  391.9 11.4 %collective-permute-done.8.refs_1_ = bf16[12,2,64,128]{3,2,1,0:T(8,128)(2,1)S(1)} collective-permute-done((bf16[12,2,64,128]{3,2,1,0:T(8,128)(2,1)S(1)}, bf16[12,2,64,128]{3,2,1,0:T(8,128)(2,1)S(1)}, u32[]{:S(2)}, u32[]{:S(2)}) %collective-permute-start.8) | collective-permute-done | bytes 393248 | tf_op jit(solution)/shard_map/ppermute | solution.py:287
  403.3 19.8 %collective-permute-done.9.refs_2_ = bf16[12,2,64,128]{3,2,1,0:T(8,128)(2,1)S(1)} collective-permute-done((bf16[12,2,64,128]{3,2,1,0:T(8,128)(2,1)S(1)}, bf16[12,2,64,128]{3,2,1,0:T(8,128)(2,1)S(1)}, u32[]{:S(2)}, u32[]{:S(2)}) %collective-permute-start.9) | collective-permute-done | bytes 393248 | tf_op jit(solution)/shard_map/ppermute | solution.py:287
  424.7 8.3 %collective-permute-done.10.refs_3_ = bf16[12,2,64,128]{3,2,1,0:T(8,128)(2,1)S(1)} collective-permute-done((bf16[12,2,64,128]{3,2,1,0:T(8,128)(2,1)S(1)}, bf16[12,2,64,128]{3,2,1,0:T(8,128)(2,1)S(1)}, u32[]{:S(2)}, u32[]{:S(2)}) %collective-permute-start.10) | collective-permute-done | bytes 393248 | tf_op jit(solution)/shard_map/ppermute | solution.py:287
  433.5 11.0 %collective-permute-done.13.refs_6_ = bf16[12,2,64,128]{3,2,1,0:T(8,128)(2,1)S(1)} collective-permute-done((bf16[12,2,64,128]{3,2,1,0:T(8,128)(2,1)S(1)}, bf16[12,2,64,128]{3,2,1,0:T(8,128)(2,1)S(1)}, u32[]{:S(2)}, u32[]{:S(2)}) %collective-permute-start.13) | collective-permute-done | bytes 393248 | tf_op jit(solution)/shard_map/ppermute | solution.py:287
  444.5 5.2 collective-permute-done.14.refs_7_
  453.2 7.2 %all-to-all-start.3 = ((bf16[16,2,128,128]{3,2,1,0:T(8,128)(2,1)}), bf16[16,2,128,128]{3,2,1,0:T(8,128)(2,1)}, u32[]{:S(2)}, u32[]{:S(2)}) async-start(bf16[16,2,128,128]{3,2,1,0:T(8,128)(2,1)} %unpack.2), calls=%async_computation.3 | async-start | bytes 2097152 | tf_op jit(solution)/shard_map/all_to_all | solution.py:401
  460.4 128.9 %join.1 = bf16[16,2,2,2,128,128]{5,4,3,2,1,0:T(8,128)(2,1)} custom-call(s32[2]{0:T(128)} %pad_add_fusion.place, bf16[16,2,128,128]{3,2,1,0:T(8,128)(2,1)} %copy-done.1, bf16[16,2,128,128]{3,2,1,0:T(8,128)(2,1)} %copy-done, bf16[16,2,128,128]{3,2,1,0:T(8,128)(2,1)} %collective-permute-done.29.got0, bf16[16,2,128,128]{3,2,1,0:T(8,128)(2,1)} %collective-permute-done.30.got1), custom_call_target="tpu_custom_call" | custom-call | bytes 8388608 | tf_op jit(solution)/shard_map/join/pallas_call | solution.py:403
  (158 shorter events, 100.6 us)
Async XLA Ops:
  3.4 23.3 %all-to-all-start = ((bf16[16,2,128,128]{3,2,1,0:T(8,128)(2,1)}), bf16[16,2,128,128]{3,2,1,0:T(8,128)(2,1)S(1)}, u32[]{:S(2)}, u32[]{:S(2)}) async-start(bf16[16,2,128,128]{3,2,1,0:T(8,128)(2,1)} %pad_maximum_fusion), calls=%async_computation | async-start | bytes 2097152 | tf_op jit(solution)/shard_map/all_to_all | solution.py:327
  14.0 143.3 %collective-permute-start.7 = (bf16[16,2,2,128,128]{4,3,2,1,0:T(8,128)(2,1)}, bf16[16,2,2,128,128]{4,3,2,1,0:T(8,128)(2,1)}, u32[]{:S(2)}, u32[]{:S(2)}) collective-permute-start(bf16[16,2,2,128,128]{4,3,2,1,0:T(8,128)(2,1)} %dynamic-slice_bitcast_fusion), channel_id=1, source_target_pairs={{0,1},{1,0},{2,3},{3,2},{4,5},{5,4},{6,7},{7,6},{8,9},{9,8},{10,11... | collective-permute-start | bytes 6291464 | tf_op jit(solution)/shard_map/ppermute | solution.py:299
  26.7 20.6 %all-to-all-start.4 = ((bf16[16,2,128,128]{3,2,1,0:T(8,128)(2,1)}), bf16[16,2,128,128]{3,2,1,0:T(8,128)(2,1)S(1)}, u32[]{:S(2)}, u32[]{:S(2)}) async-start(bf16[16,2,128,128]{3,2,1,0:T(8,128)(2,1)} %pad_maximum_fusion.1), calls=%async_computation.4 | async-start | bytes 2097152 | tf_op jit(solution)/shard_map/all_to_all | solution.py:327
  58.0 41.5 %collective-permute-start.16 = (bf16[12,2,64,128]{3,2,1,0:T(8,128)(2,1)S(1)}, bf16[12,2,64,128]{3,2,1,0:T(8,128)(2,1)S(1)}, u32[]{:S(2)}, u32[]{:S(2)}) collective-permute-start(bf16[12,2,64,128]{3,2,1,0:T(8,128)(2,1)S(1)} %get-tuple-element.57), channel_id=1, source_target_pairs={{0,4},{2,6},{4,8},{6,10},{8,12},{10,14},{12,0},{14,2},{1,5},{3,7},... | collective-permute-start | bytes 1179656 | tf_op jit(solution)/shard_map/ppermute | solution.py:287
  59.8 58.8 %collective-permute-start.17 = (bf16[12,2,64,128]{3,2,1,0:T(8,128)(2,1)S(1)}, bf16[12,2,64,128]{3,2,1,0:T(8,128)(2,1)S(1)}, u32[]{:S(2)}, u32[]{:S(2)}) collective-permute-start(bf16[12,2,64,128]{3,2,1,0:T(8,128)(2,1)S(1)} %get-tuple-element.58), channel_id=1, source_target_pairs={{0,6},{2,8},{4,10},{6,12},{8,14},{10,0},{12,2},{14,4},{1,7},{3,9},... | collective-permute-start | bytes 1179656 | tf_op jit(solution)/shard_map/ppermute | solution.py:287
  63.1 92.7 %collective-permute-start.18 = (bf16[12,2,64,128]{3,2,1,0:T(8,128)(2,1)}, bf16[12,2,64,128]{3,2,1,0:T(8,128)(2,1)S(1)}, u32[]{:S(2)}, u32[]{:S(2)}) collective-permute-start(bf16[12,2,64,128]{3,2,1,0:T(8,128)(2,1)} %get-tuple-element.59), channel_id=1, source_target_pairs={{0,8},{2,10},{4,12},{6,14},{8,0},{10,2},{12,4},{14,6},{1,9},{3,11}... | collective-permute-start | bytes 1179656 | tf_op jit(solution)/shard_map/ppermute | solution.py:287
  76.6 80.0 %collective-permute-start.19 = (bf16[12,2,64,128]{3,2,1,0:T(8,128)(2,1)}, bf16[12,2,64,128]{3,2,1,0:T(8,128)(2,1)}, u32[]{:S(2)}, u32[]{:S(2)}) collective-permute-start(bf16[12,2,64,128]{3,2,1,0:T(8,128)(2,1)} %get-tuple-element.60), channel_id=1, source_target_pairs={{0,10},{2,12},{4,14},{6,0},{8,2},{10,4},{12,6},{14,8},{1,11},{3,13... | collective-permute-start | bytes 1179656 | tf_op jit(solution)/shard_map/ppermute | solution.py:287
  99.6 57.1 %collective-permute-start.20 = (bf16[12,2,64,128]{3,2,1,0:T(8,128)(2,1)}, bf16[12,2,64,128]{3,2,1,0:T(8,128)(2,1)}, u32[]{:S(2)}, u32[]{:S(2)}) collective-permute-start(bf16[12,2,64,128]{3,2,1,0:T(8,128)(2,1)} %get-tuple-element.61), channel_id=1, source_target_pairs={{0,12},{2,14},{4,0},{6,2},{8,4},{10,6},{12,8},{14,10},{1,13},{3,15... | collective-permute-start | bytes 1179656 | tf_op jit(solution)/shard_map/ppermute | solution.py:287
  119.4 37.2 %collective-permute-start.21 = (bf16[12,2,64,128]{3,2,1,0:T(8,128)(2,1)}, bf16[12,2,64,128]{3,2,1,0:T(8,128)(2,1)S(1)}, u32[]{:S(2)}, u32[]{:S(2)}) collective-permute-start(bf16[12,2,64,128]{3,2,1,0:T(8,128)(2,1)} %get-tuple-element.62), channel_id=1, source_target_pairs={{0,14},{2,0},{4,2},{6,4},{8,6},{10,8},{12,10},{14,12},{1,15},{3,1}... | collective-permute-start | bytes 1179656 | tf_op jit(solution)/shard_map/ppermute | solution.py:287
  188.9 19.4 %all-to-all-start.6 = ((f32[8,16,128]{2,1,0:T(8,128)}), f32[8,16,128]{2,1,0:T(8,128)S(1)}, u32[]{:S(2)}, u32[]{:S(2)}) async-start(f32[8,16,128]{2,1,0:T(8,128)} %bitcast.27), calls=%async_computation.6 | async-start | bytes 131072 | tf_op jit(solution)/shard_map/all_to_all | solution.py:368
  192.3 54.4 %collective-permute-start.1 = (bf16[12,2,64,128]{3,2,1,0:T(8,128)(2,1)}, bf16[12,2,64,128]{3,2,1,0:T(8,128)(2,1)S(1)}, u32[]{:S(2)}, u32[]{:S(2)}) collective-permute-start(bf16[12,2,64,128]{3,2,1,0:T(8,128)(2,1)} %get-tuple-element.41), channel_id=1, source_target_pairs={{0,4},{2,6},{4,8},{6,10},{8,12},{10,14},{12,0},{14,2},{1,5},{3,7},... | collective-permute-start | bytes 1179656 | tf_op jit(solution)/shard_map/ppermute | solution.py:287
  195.1 52.4 %collective-permute-start.2 = (bf16[12,2,64,128]{3,2,1,0:T(8,128)(2,1)}, bf16[12,2,64,128]{3,2,1,0:T(8,128)(2,1)}, u32[]{:S(2)}, u32[]{:S(2)}) collective-permute-start(bf16[12,2,64,128]{3,2,1,0:T(8,128)(2,1)} %get-tuple-element.42), channel_id=1, source_target_pairs={{0,6},{2,8},{4,10},{6,12},{8,14},{10,0},{12,2},{14,4},{1,7},{3,9},... | collective-permute-start | bytes 1179656 | tf_op jit(solution)/shard_map/ppermute | solution.py:287
  198.7 48.8 %collective-permute-start.3 = (bf16[12,2,64,128]{3,2,1,0:T(8,128)(2,1)S(1)}, bf16[12,2,64,128]{3,2,1,0:T(8,128)(2,1)}, u32[]{:S(2)}, u32[]{:S(2)}) collective-permute-start(bf16[12,2,64,128]{3,2,1,0:T(8,128)(2,1)S(1)} %copy-done.20), channel_id=1, source_target_pairs={{0,8},{2,10},{4,12},{6,14},{8,0},{10,2},{12,4},{14,6},{1,9},{3,11}... | collective-permute-start | bytes 1179656 | tf_op jit(solution)/shard_map/ppermute | solution.py:287
  200.2 50.1 %collective-permute-start.4 = (bf16[12,2,64,128]{3,2,1,0:T(8,128)(2,1)S(1)}, bf16[12,2,64,128]{3,2,1,0:T(8,128)(2,1)}, u32[]{:S(2)}, u32[]{:S(2)}) collective-permute-start(bf16[12,2,64,128]{3,2,1,0:T(8,128)(2,1)S(1)} %copy-done.18), channel_id=1, source_target_pairs={{0,10},{2,12},{4,14},{6,0},{8,2},{10,4},{12,6},{14,8},{1,11},{3,13... | collective-permute-start | bytes 1179656 | tf_op jit(solution)/shard_map/ppermute | solution.py:287
  203.8 46.5 %collective-permute-start.5 = (bf16[12,2,64,128]{3,2,1,0:T(8,128)(2,1)S(1)}, bf16[12,2,64,128]{3,2,1,0:T(8,128)(2,1)}, u32[]{:S(2)}, u32[]{:S(2)}) collective-permute-start(bf16[12,2,64,128]{3,2,1,0:T(8,128)(2,1)S(1)} %get-tuple-element.45), channel_id=1, source_target_pairs={{0,12},{2,14},{4,0},{6,2},{8,4},{10,6},{12,8},{14,10},{1,13},{3,15... | collective-permute-start | bytes 1179656 | tf_op jit(solution)/shard_map/ppermute | solution.py:287
  247.5 25.7 %collective-permute-start.22 = (bf16[12,2,64,128]{3,2,1,0:T(8,128)(2,1)S(1)}, bf16[12,2,64,128]{3,2,1,0:T(8,128)(2,1)S(1)}, u32[]{:S(2)}, u32[]{:S(2)}) collective-permute-start(bf16[12,2,64,128]{3,2,1,0:T(8,128)(2,1)S(1)} %get-tuple-element.64), channel_id=1, source_target_pairs={{0,14},{2,0},{4,2},{6,4},{8,6},{10,8},{12,10},{14,12},{1,15},{3,1}... | collective-permute-start | bytes 1179656 | tf_op jit(solution)/shard_map/ppermute | solution.py:287
  247.5 39.6 %collective-permute-start.23 = (bf16[12,2,64,128]{3,2,1,0:T(8,128)(2,1)S(1)}, bf16[12,2,64,128]{3,2,1,0:T(8,128)(2,1)S(1)}, u32[]{:S(2)}, u32[]{:S(2)}) collective-permute-start(bf16[12,2,64,128]{3,2,1,0:T(8,128)(2,1)S(1)} %get-tuple-element.65), channel_id=1, source_target_pairs={{0,12},{2,14},{4,0},{6,2},{8,4},{10,6},{12,8},{14,10},{1,13},{3,15... | collective-permute-start | bytes 1179656 | tf_op jit(solution)/shard_map/ppermute | solution.py:287
  250.3 84.9 %collective-permute-start.24 = (bf16[12,2,64,128]{3,2,1,0:T(8,128)(2,1)}, bf16[12,2,64,128]{3,2,1,0:T(8,128)(2,1)S(1)}, u32[]{:S(2)}, u32[]{:S(2)}) collective-permute-start(bf16[12,2,64,128]{3,2,1,0:T(8,128)(2,1)} %get-tuple-element.66), channel_id=1, source_target_pairs={{0,10},{2,12},{4,14},{6,0},{8,2},{10,4},{12,6},{14,8},{1,11},{3,13... | collective-permute-start | bytes 1179656 | tf_op jit(solution)/shard_map/ppermute | solution.py:287
  250.3 84.9 %collective-permute-start.25 = (bf16[12,2,64,128]{3,2,1,0:T(8,128)(2,1)}, bf16[12,2,64,128]{3,2,1,0:T(8,128)(2,1)S(1)}, u32[]{:S(2)}, u32[]{:S(2)}) collective-permute-start(bf16[12,2,64,128]{3,2,1,0:T(8,128)(2,1)} %get-tuple-element.67), channel_id=1, source_target_pairs={{0,8},{2,10},{4,12},{6,14},{8,0},{10,2},{12,4},{14,6},{1,9},{3,11}... | collective-permute-start | bytes 1179656 | tf_op jit(solution)/shard_map/ppermute | solution.py:287
  261.0 74.2 %collective-permute-start.26 = (bf16[12,2,64,128]{3,2,1,0:T(8,128)(2,1)}, bf16[12,2,64,128]{3,2,1,0:T(8,128)(2,1)S(1)}, u32[]{:S(2)}, u32[]{:S(2)}) collective-permute-start(bf16[12,2,64,128]{3,2,1,0:T(8,128)(2,1)} %get-tuple-element.68), channel_id=1, source_target_pairs={{0,6},{2,8},{4,10},{6,12},{8,14},{10,0},{12,2},{14,4},{1,7},{3,9},... | collective-permute-start | bytes 1179656 | tf_op jit(solution)/shard_map/ppermute | solution.py:287
  273.2 61.9 %collective-permute-start.27 = (bf16[12,2,64,128]{3,2,1,0:T(8,128)(2,1)}, bf16[12,2,64,128]{3,2,1,0:T(8,128)(2,1)S(1)}, u32[]{:S(2)}, u32[]{:S(2)}) collective-permute-start(bf16[12,2,64,128]{3,2,1,0:T(8,128)(2,1)} %get-tuple-element.69), channel_id=1, source_target_pairs={{0,4},{2,6},{4,8},{6,10},{8,12},{10,14},{12,0},{14,2},{1,5},{3,7},... | collective-permute-start | bytes 1179656 | tf_op jit(solution)/shard_map/ppermute | solution.py:287
  287.0 48.1 %collective-permute-start.28 = (bf16[12,2,64,128]{3,2,1,0:T(8,128)(2,1)}, bf16[12,2,64,128]{3,2,1,0:T(8,128)(2,1)S(1)}, u32[]{:S(2)}, u32[]{:S(2)}) collective-permute-start(bf16[12,2,64,128]{3,2,1,0:T(8,128)(2,1)} %get-tuple-element.70), channel_id=1, source_target_pairs={{0,2},{2,4},{4,6},{6,8},{8,10},{10,12},{12,14},{14,0},{1,3},{3,5},... | collective-permute-start | bytes 1179656 | tf_op jit(solution)/shard_map/ppermute | solution.py:287
  343.6 109.6 %all-to-all-start.7 = ((bf16[16,2,128,128]{3,2,1,0:T(8,128)(2,1)}), bf16[16,2,128,128]{3,2,1,0:T(8,128)(2,1)S(1)}, u32[]{:S(2)}, u32[]{:S(2)}) async-start(bf16[16,2,128,128]{3,2,1,0:T(8,128)(2,1)} %unpack.3), calls=%async_computation.7 | async-start | bytes 2097152 | tf_op jit(solution)/shard_map/all_to_all | solution.py:401
  385.4 37.7 %collective-permute-start.9 = (bf16[12,2,64,128]{3,2,1,0:T(8,128)(2,1)S(1)}, bf16[12,2,64,128]{3,2,1,0:T(8,128)(2,1)S(1)}, u32[]{:S(2)}, u32[]{:S(2)}) collective-permute-start(bf16[12,2,64,128]{3,2,1,0:T(8,128)(2,1)S(1)} %get-tuple-element.49), channel_id=1, source_target_pairs={{0,12},{2,14},{4,0},{6,2},{8,4},{10,6},{12,8},{14,10},{1,13},{3,15... | collective-permute-start | bytes 1179656 | tf_op jit(solution)/shard_map/ppermute | solution.py:287
  385.4 47.6 %collective-permute-start.10 = (bf16[12,2,64,128]{3,2,1,0:T(8,128)(2,1)S(1)}, bf16[12,2,64,128]{3,2,1,0:T(8,128)(2,1)S(1)}, u32[]{:S(2)}, u32[]{:S(2)}) collective-permute-start(bf16[12,2,64,128]{3,2,1,0:T(8,128)(2,1)S(1)} %get-tuple-element.50), channel_id=1, source_target_pairs={{0,10},{2,12},{4,14},{6,0},{8,2},{10,4},{12,6},{14,8},{1,11},{3,13... | collective-permute-start | bytes 1179656 | tf_op jit(solution)/shard_map/ppermute | solution.py:287
  385.4 47.6 %collective-permute-start.11 = (bf16[12,2,64,128]{3,2,1,0:T(8,128)(2,1)S(1)}, bf16[12,2,64,128]{3,2,1,0:T(8,128)(2,1)S(1)}, u32[]{:S(2)}, u32[]{:S(2)}) collective-permute-start(bf16[12,2,64,128]{3,2,1,0:T(8,128)(2,1)S(1)} %get-tuple-element.51), channel_id=1, source_target_pairs={{0,8},{2,10},{4,12},{6,14},{8,0},{10,2},{12,4},{14,6},{1,9},{3,11}... | collective-permute-start | bytes 1179656 | tf_op jit(solution)/shard_map/ppermute | solution.py:287
  391.9 41.6 %collective-permute-start.12 = (bf16[12,2,64,128]{3,2,1,0:T(8,128)(2,1)S(1)}, bf16[12,2,64,128]{3,2,1,0:T(8,128)(2,1)S(1)}, u32[]{:S(2)}, u32[]{:S(2)}) collective-permute-start(bf16[12,2,64,128]{3,2,1,0:T(8,128)(2,1)S(1)} %get-tuple-element.52), channel_id=1, source_target_pairs={{0,6},{2,8},{4,10},{6,12},{8,14},{10,0},{12,2},{14,4},{1,7},{3,9},... | collective-permute-start | bytes 1179656 | tf_op jit(solution)/shard_map/ppermute | solution.py:287
  403.3 41.2 %collective-permute-start.13 = (bf16[12,2,64,128]{3,2,1,0:T(8,128)(2,1)S(1)}, bf16[12,2,64,128]{3,2,1,0:T(8,128)(2,1)S(1)}, u32[]{:S(2)}, u32[]{:S(2)}) collective-permute-start(bf16[12,2,64,128]{3,2,1,0:T(8,128)(2,1)S(1)} %get-tuple-element.53), channel_id=1, source_target_pairs={{0,4},{2,6},{4,8},{6,10},{8,12},{10,14},{12,0},{14,2},{1,5},{3,7},... | collective-permute-start | bytes 1179656 | tf_op jit(solution)/shard_map/ppermute | solution.py:287
  423.1 26.6 %collective-permute-start.14 = (bf16[12,2,64,128]{3,2,1,0:T(8,128)(2,1)S(1)}, bf16[12,2,64,128]{3,2,1,0:T(8,128)(2,1)S(1)}, u32[]{:S(2)}, u32[]{:S(2)}) collective-permute-start(bf16[12,2,64,128]{3,2,1,0:T(8,128)(2,1)S(1)} %get-tuple-element.54), channel_id=1, source_target_pairs={{0,2},{2,4},{4,6},{6,8},{8,10},{10,12},{12,14},{14,0},{1,3},{3,5},... | collective-permute-start | bytes 1179656 | tf_op jit(solution)/shard_map/ppermute | solution.py:287
  433.0 27.4 %collective-permute-start.29 = (bf16[16,2,128,128]{3,2,1,0:T(8,128)(2,1)S(1)}, bf16[16,2,128,128]{3,2,1,0:T(8,128)(2,1)}, u32[]{:S(2)}, u32[]{:S(2)}) collective-permute-start(bf16[16,2,128,128]{3,2,1,0:T(8,128)(2,1)S(1)} %get-tuple-element.73), channel_id=1, source_target_pairs={{0,1},{1,0},{2,3},{3,2},{4,5},{5,4},{6,7},{7,6},{8,9},{9,8},{10,11... | collective-permute-start | bytes 3145736 | tf_op jit(solution)/shard_map/ppermute | solution.py:387
  433.0 27.4 %collective-permute-start.30 = (bf16[16,2,128,128]{3,2,1,0:T(8,128)(2,1)S(1)}, bf16[16,2,128,128]{3,2,1,0:T(8,128)(2,1)}, u32[]{:S(2)}, u32[]{:S(2)}) collective-permute-start(bf16[16,2,128,128]{3,2,1,0:T(8,128)(2,1)S(1)} %copy-done.13), channel_id=1, source_target_pairs={{0,1},{1,0},{2,3},{3,2},{4,5},{5,4},{6,7},{7,6},{8,9},{9,8},{10,11... | collective-permute-start | bytes 3145736 | tf_op jit(solution)/shard_map/ppermute | solution.py:387
  453.2 136.2 %all-to-all-start.3 = ((bf16[16,2,128,128]{3,2,1,0:T(8,128)(2,1)}), bf16[16,2,128,128]{3,2,1,0:T(8,128)(2,1)}, u32[]{:S(2)}, u32[]{:S(2)}) async-start(bf16[16,2,128,128]{3,2,1,0:T(8,128)(2,1)} %unpack.2), calls=%async_computation.3 | async-start | bytes 2097152 | tf_op jit(solution)/shard_map/all_to_all | solution.py:401
  (48 other events, 1034.6 us)

commit v2 on v1

--- a/solution.py
+++ b/solution.py
@@ -19,13 +19,14 @@
 SPANS = INST // 2
 BLK = 16
 UNROLL = 4
+COST = 1 << 10
 SCALE = 1.0 / math.sqrt(DH)
 F32 = jnp.float32
 BF16 = jnp.bfloat16
 
 SMEM = pl.BlockSpec(memory_space=pltpu.SMEM)
 VMEM = pl.BlockSpec(memory_space=pltpu.VMEM)
-ANY = pl.BlockSpec(memory_space=pl.ANY)
+ANY = pl.BlockSpec(memory_space=pltpu.HBM)
 
 STAT_ROWS = RING * 16
 SENT = 64
@@ -255,17 +256,16 @@
     lax.fori_loop(0, SPANS, step, 0, unroll=2)
 
 
-def join_kernel(place, keep0, keep1, got0, got1, out, sems):
+def join_kernel(place, keep0, keep1, got0, got1, out):
     core = place[1]
-    copies = []
-    for n, (ref, half, pair) in enumerate(
-        ((keep0, core, 0), (keep1, core, 1), (got0, 1 - core, 0), (got1, 1 - core, 1))
+    for ref, half, pair in (
+        (keep0, core, 0),
+        (keep1, core, 1),
+        (got0, 1 - core, 0),
+        (got1, 1 - core, 1),
     ):
-        copies.append(pltpu.make_async_copy(ref, out.at[:, :, half, pair], sems.at[n]))
-    for copy in copies:
-        copy.start()
-    for copy in copies:
-        copy.wait()
+        for kind in range(2):
+            out[0, kind, half, pair] = ref[0, kind]
 
 
 def shape(dims, dtype=BF16):
@@ -273,7 +273,7 @@
 
 
 PART = (SLOTS, 2, SPAN, DH)
-PARAMS = pltpu.CompilerParams(vmem_limit_bytes=40 * 1024 * 1024)
+PARAMS = pltpu.CompilerParams(vmem_limit_bytes=60 * 1024 * 1024)
 STAGE = pltpu.VMEM((ROWS + 1, 2, SPAN, DH), BF16)
 STORE = pltpu.VMEM((2 * BLK, 2, 128, DH), BF16)
 STATS = pltpu.VMEM((STAT_ROWS + 8, DH), F32)
@@ -335,12 +335,12 @@
                 pltpu.SemaphoreType.DMA((RING,)),
             ],
             compiler_params=PARAMS,
-            cost_estimate=cost(0, 8 << 20),
+            cost_estimate=cost(0, COST),
             name="pack",
         )(send_table, rows, after)
         got = ring_send(parts, 1)
-        after = got[1]
         arrived.append(got)
+        after = recv_table
 
     results = []
     kv_grads = []
@@ -353,7 +353,7 @@
             out_specs=VMEM,
             scratch_shapes=[STAGE, STORE, STATS, SEMS],
             compiler_params=PARAMS,
-            cost_estimate=cost(8 << 30, 8 << 20),
+            cost_estimate=cost(COST, COST),
             name="stats",
         )(place, recv_table, *parts, kv_store, kv_other)
         stats = lax.all_to_all(stats, "grp", split_axis=0, concat_axis=0, tiled=True)
@@ -380,7 +380,7 @@
                 SEMS,
             ],
             compiler_params=PARAMS,
-            cost_estimate=cost(16 << 30, 16 << 20),
+            cost_estimate=cost(COST, COST),
             name="grads",
         )(place, recv_table, stats, *parts, kv_store, kv_other)
         got = ring_send(outs[:RING], -1)
@@ -395,7 +395,7 @@
                 pltpu.SemaphoreType.DMA((RING,)),
             ],
             compiler_params=PARAMS,
-            cost_estimate=cost(0, 8 << 20),
+            cost_estimate=cost(0, COST),
             name="unpack",
         )(send_table, *got)
         results.append(lax.all_to_all(rows, "seq", split_axis=0, concat_axis=0, tiled=True))
@@ -403,10 +403,10 @@
     d_kv = pl.pallas_call(
         join_kernel,
         out_shape=shape(kv_store.shape),
-        in_specs=[SMEM] + [ANY] * 4,
-        out_specs=ANY,
-        scratch_shapes=[pltpu.SemaphoreType.DMA((4,))],
-        cost_estimate=cost(0, 8 << 20),
+        grid=(BLK,),
+        in_specs=[SMEM] + [pl.BlockSpec((1, 2, 128, DH), lambda b: (b, 0, 0, 0))] * 4,
+        out_specs=pl.BlockSpec((1, 2, 2, 2, 128, DH), lambda b: (b, 0, 0, 0, 0, 0)),
+        cost_estimate=cost(0, COST),
         name="join",
     )(place, kv_grads[0][0], kv_grads[1][0], kv_grads[0][1], kv_grads[1][1])
     attn_out = jnp.stack([results[0][:, 0], results[1][:, 0]], axis=1).reshape(query.shape)

time: 590 us -> 469 us (0.79)
  Pallas kernels: 239 us -> 105 us
  blocking collectives: 43 us -> 78.1 us
  waiting for transfers between devices: 153 us -> 124 us
  starting transfers between devices: 117 us -> 141 us
  local copies, waits for them, and re-layouts: 33.7 us -> 12.6 us
    pallas_call x1, Pallas kernels: 129 us -> 10.1 us  [on_device(): pl.pallas_call(join_kernel, out_shape=shape(kv_store.shape), grid=(BLK,),...]
    all_to_all x2, blocking collectives: 24.2 us -> 58.6 us  [on_device(): lax.all_to_all(stats, 'grp', split_axis=0, concat_axis=0, tiled=True)]
    ppermute x28, waiting for transfers between devices: 131 us -> 106 us  [ring_send(): got[d] = lax.ppermute(parts[d], 'grp', pairs)]
    unnamed x88 -> x52, local copies, waits for them, and re-layouts: 26.7 us -> 5.83 us
    pallas_call x2, Pallas kernels: 61 us -> 46.6 us  [on_device(): pl.pallas_call(functools.partial(grad_kernel, pair), out_shape=[shape(PAR...]
    ppermute x28, starting transfers between devices: 81.8 us -> 95.5 us  [ring_send(): got[d] = lax.ppermute(parts[d], 'grp', pairs)]
    all_to_all x2, starting transfers between devices: 14.4 us -> 24.5 us  [on_device(): lax.all_to_all(rows, 'seq', split_axis=0, concat_axis=0, tiled=True)]
    all_to_all x2, waiting for transfers between devices: 16 us -> 9.43 us  [on_device(): rows = lax.all_to_all(rows, 'seq', split_axis=0, concat_axis=0, tiled=True)]
  transfers between devices with their start and end apart: 37 -> 37, of which waited for: 16 -> 17; matrix products, arithmetic and copies ran while one was open for 1% -> 2% of each run, Pallas kernels for 38% -> 22%
where the time goes in v2:
time: 469 us; the launch traced here: 467 us
  starting transfers between devices  141 us (30%)
  waiting for transfers between devices  124 us (26%)
  Pallas kernels  105 us (22%)
  blocking collectives  78.1 us (17%)
  local copies, waits for them, and re-layouts  12.6 us (3%)
  other arithmetic  6.16 us (1%)
    ppermute x28, waiting for transfers between devices, ring_send(): got[d] = lax.ppermute(parts[d], 'grp', pairs)  106 us
    ppermute x28, starting transfers between devices, ring_send(): got[d] = lax.ppermute(parts[d], 'grp', pairs)  95.5 us
    all_to_all x2, blocking collectives, on_device(): lax.all_to_all(stats, 'grp', split_axis=0, concat_axis=0, tiled=True)  58.6 us
    pallas_call x2, Pallas kernels, on_device(): pl.pallas_call(functools.partial(grad_kernel, pair), out_shape=[shape(PAR...  46.6 us
    all_to_all x2, starting transfers between devices, on_device(): lax.all_to_all(rows, 'seq', split_axis=0, concat_axis=0, tiled=True)  24.5 us
    all_gather x1, blocking collectives, on_device(): names = lax.all_gather(names, 'grp', tiled=True)  19.5 us
    pallas_call x2, Pallas kernels, on_device(): pl.pallas_call(functools.partial(stat_kernel, pair), out_shape=shape((STA...  19.3 us
    all_to_all x2, starting transfers between devices, on_device(): rows = lax.all_to_all(rows, 'seq', split_axis=0, concat_axis=0, tiled=True)  12.9 us
  transfers between devices with their start and end apart: 37, of which 17 were waited for; matrix products, arithmetic and copies ran while one was open for 2% of the time, Pallas kernels for 22%

profile of v2, /device:TPU:2, one launch (start us, length us, event | category | flops | bytes accessed | tf_op | source)
XLA Modules:
  0.0 467.4 jit_solution(4380662464614596988)
XLA Ops:
  4.4 7.5 %all-to-all-start.4 = ((bf16[16,2,128,128]{3,2,1,0:T(8,128)(2,1)}), bf16[16,2,128,128]{3,2,1,0:T(8,128)(2,1)S(1)}, u32[]{:S(2)}, u32[]{:S(2)}) async-start(bf16[16,2,128,128]{3,2,1,0:T(8,128)(2,1)} %pad_maximum_fusion.1), calls=%async_computation.4 | async-start | bytes 2097152 | tf_op jit(solution)/shard_map/all_to_all | solution.py:327
  18.3 9.4 %all-to-all-done.4.rows = bf16[16,2,128,128]{3,2,1,0:T(8,128)(2,1)S(1)} async-done(((bf16[16,2,128,128]{3,2,1,0:T(8,128)(2,1)}), bf16[16,2,128,128]{3,2,1,0:T(8,128)(2,1)S(1)}, u32[]{:S(2)}, u32[]{:S(2)}) %all-to-all-start.4) | async-done | bytes 1048608 | tf_op jit(solution)/shard_map/all_to_all | solution.py:327
  28.7 5.4 %all-to-all-start = ((bf16[16,2,128,128]{3,2,1,0:T(8,128)(2,1)}), bf16[16,2,128,128]{3,2,1,0:T(8,128)(2,1)S(1)}, u32[]{:S(2)}, u32[]{:S(2)}) async-start(bf16[16,2,128,128]{3,2,1,0:T(8,128)(2,1)} %pad_maximum_fusion), calls=%async_computation | async-start | bytes 2097152 | tf_op jit(solution)/shard_map/all_to_all | solution.py:327
  36.5 19.5 %all-gather.1 = s32[8,1,128]{2,1,0:T(1,128)} all-gather(s32[1,1,128]{2,1,0:T(1,128)S(1)} %add_bitcast_fusion), channel_id=2, replica_groups=mesh['seq'=16,'grp'=8,'store'=2] {'grp'}, dimensions={0}, use_global_device_ids=true | all-gather | bytes 4608 | tf_op jit(solution)/shard_map/all_gather | solution.py:297
  56.0 8.9 %recv_table.1.table.after = s32[512]{0:T(512)} custom-call(s32[2]{0:T(128)} %pad_add_fusion.place, s32[8,128]{1,0:T(8,128)} %bitcast.31), custom_call_target="tpu_custom_call" | custom-call | tf_op jit(solution)/shard_map/recv_table/pallas_call | solution.py:311
  75.7 12.0 %collective-permute-done.15.refs_1_ = bf16[12,2,64,128]{3,2,1,0:T(8,128)(2,1)S(1)} collective-permute-done((bf16[12,2,64,128]{3,2,1,0:T(8,128)(2,1)}, bf16[12,2,64,128]{3,2,1,0:T(8,128)(2,1)S(1)}, u32[]{:S(2)}, u32[]{:S(2)}) %collective-permute-start.15) | collective-permute-done | bytes 393248 | tf_op jit(solution)/shard_map/ppermute | solution.py:287
  87.7 20.6 %collective-permute-done.16.refs_2_ = bf16[12,2,64,128]{3,2,1,0:T(8,128)(2,1)S(1)} collective-permute-done((bf16[12,2,64,128]{3,2,1,0:T(8,128)(2,1)}, bf16[12,2,64,128]{3,2,1,0:T(8,128)(2,1)S(1)}, u32[]{:S(2)}, u32[]{:S(2)}) %collective-permute-start.16) | collective-permute-done | bytes 393248 | tf_op jit(solution)/shard_map/ppermute | solution.py:287
  108.3 16.0 %collective-permute-done.17.refs_3_ = bf16[12,2,64,128]{3,2,1,0:T(8,128)(2,1)S(1)} collective-permute-done((bf16[12,2,64,128]{3,2,1,0:T(8,128)(2,1)}, bf16[12,2,64,128]{3,2,1,0:T(8,128)(2,1)S(1)}, u32[]{:S(2)}, u32[]{:S(2)}) %collective-permute-start.17) | collective-permute-done | bytes 393248 | tf_op jit(solution)/shard_map/ppermute | solution.py:287
  125.1 10.3 %collective-permute-start.21 = (bf16[12,2,64,128]{3,2,1,0:T(8,128)(2,1)}, bf16[12,2,64,128]{3,2,1,0:T(8,128)(2,1)}, u32[]{:S(2)}, u32[]{:S(2)}) collective-permute-start(bf16[12,2,64,128]{3,2,1,0:T(8,128)(2,1)} %get-tuple-element.62), channel_id=1, source_target_pairs={{0,14},{2,0},{4,2},{6,4},{8,6},{10,8},{12,10},{14,12},{1,15},{3,1}... | collective-permute-start | bytes 1179656 | tf_op jit(solution)/shard_map/ppermute | solution.py:287
  139.9 5.0 %collective-permute-start.1 = (bf16[12,2,64,128]{3,2,1,0:T(8,128)(2,1)}, bf16[12,2,64,128]{3,2,1,0:T(8,128)(2,1)S(1)}, u32[]{:S(2)}, u32[]{:S(2)}) collective-permute-start(bf16[12,2,64,128]{3,2,1,0:T(8,128)(2,1)} %get-tuple-element.41), channel_id=1, source_target_pairs={{0,4},{2,6},{4,8},{6,10},{8,12},{10,14},{12,0},{14,2},{1,5},{3,7},... | collective-permute-start | bytes 1179656 | tf_op jit(solution)/shard_map/ppermute | solution.py:287
  150.7 9.6 %stats.3 = f32[128,128]{1,0:T(8,128)} custom-call(s32[2]{0:T(128)} %pad_add_fusion.place, s32[512]{0:T(512)} %recv_table.1.table.after, bf16[12,2,64,128]{3,2,1,0:T(8,128)(2,1)} %get-tuple-element.55.refs_0_, bf16[12,2,64,128]{3,2,1,0:T(8,128)(2,1)} %copy-done.9, bf16[12,2,64,128]{3,2,1,0:T(8,128)(2,1)} %copy-done.10, bf16[12,2,64,128]{3,2,1,0:T(8,128)(2,1)} %copy-done.11, ...), custom_call_target="tpu_custom_call" | custom-call | flops 1024 | bytes 1024 | tf_op jit(solution)/shard_map/stats/pallas_call | solution.py:349
  160.3 46.3 %all_to_all.64 = f32[8,16,128]{2,1,0:T(8,128)} all-to-all(f32[8,16,128]{2,1,0:T(8,128)} %bitcast.25), channel_id=1, replica_groups=mesh['seq'=16,'grp'=8,'store'=2] {'grp'}, dimensions={0} | all-to-all | bytes 131072 | tf_op jit(solution)/shard_map/all_to_all | solution.py:359
  212.3 5.0 %collective-permute-start.4 = (bf16[12,2,64,128]{3,2,1,0:T(8,128)(2,1)}, bf16[12,2,64,128]{3,2,1,0:T(8,128)(2,1)S(1)}, u32[]{:S(2)}, u32[]{:S(2)}) collective-permute-start(bf16[12,2,64,128]{3,2,1,0:T(8,128)(2,1)} %get-tuple-element.44), channel_id=1, source_target_pairs={{0,10},{2,12},{4,14},{6,0},{8,2},{10,4},{12,6},{14,8},{1,11},{3,13... | collective-permute-start | bytes 1179656 | tf_op jit(solution)/shard_map/ppermute | solution.py:287
  221.3 23.4 %grads.3 = (bf16[12,2,64,128]{3,2,1,0:T(8,128)(2,1)}, bf16[12,2,64,128]{3,2,1,0:T(8,128)(2,1)}, bf16[12,2,64,128]{3,2,1,0:T(8,128)(2,1)}, bf16[12,2,64,128]{3,2,...) custom-call(s32[2]{0:T(128)} %pad_add_fusion.place, ...), custom_call_target="tpu_custom_call" | custom-call | flops 1024 | bytes 1024 | tf_op jit(solution)/shard_map/grads/pallas_call | solution.py:369
  251.0 6.3 %collective-permute-start.24 = (bf16[12,2,64,128]{3,2,1,0:T(8,128)(2,1)}, bf16[12,2,64,128]{3,2,1,0:T(8,128)(2,1)}, u32[]{:S(2)}, u32[]{:S(2)}) collective-permute-start(bf16[12,2,64,128]{3,2,1,0:T(8,128)(2,1)} %get-tuple-element.66), channel_id=1, source_target_pairs={{0,10},{2,12},{4,14},{6,0},{8,2},{10,4},{12,6},{14,8},{1,11},{3,13... | collective-permute-start | bytes 1179656 | tf_op jit(solution)/shard_map/ppermute | solution.py:287
  259.7 7.8 %collective-permute-start.25 = (bf16[12,2,64,128]{3,2,1,0:T(8,128)(2,1)}, bf16[12,2,64,128]{3,2,1,0:T(8,128)(2,1)}, u32[]{:S(2)}, u32[]{:S(2)}) collective-permute-start(bf16[12,2,64,128]{3,2,1,0:T(8,128)(2,1)} %get-tuple-element.67), channel_id=1, source_target_pairs={{0,8},{2,10},{4,12},{6,14},{8,0},{10,2},{12,4},{14,6},{1,9},{3,11}... | collective-permute-start | bytes 1179656 | tf_op jit(solution)/shard_map/ppermute | solution.py:287
  267.4 16.0 %collective-permute-done.6.refs_7_ = bf16[12,2,64,128]{3,2,1,0:T(8,128)(2,1)S(1)} collective-permute-done((bf16[12,2,64,128]{3,2,1,0:T(8,128)(2,1)}, bf16[12,2,64,128]{3,2,1,0:T(8,128)(2,1)S(1)}, u32[]{:S(2)}, u32[]{:S(2)}) %collective-permute-start.6) | collective-permute-done | bytes 393248 | tf_op jit(solution)/shard_map/ppermute | solution.py:287
  283.4 7.4 %collective-permute-start.26 = (bf16[12,2,64,128]{3,2,1,0:T(8,128)(2,1)}, bf16[12,2,64,128]{3,2,1,0:T(8,128)(2,1)}, u32[]{:S(2)}, u32[]{:S(2)}) collective-permute-start(bf16[12,2,64,128]{3,2,1,0:T(8,128)(2,1)} %get-tuple-element.68), channel_id=1, source_target_pairs={{0,6},{2,8},{4,10},{6,12},{8,14},{10,0},{12,2},{14,4},{1,7},{3,9},... | collective-permute-start | bytes 1179656 | tf_op jit(solution)/shard_map/ppermute | solution.py:287
  290.8 5.9 %collective-permute-done.22.refs_1_ = bf16[12,2,64,128]{3,2,1,0:T(8,128)(2,1)S(1)} collective-permute-done((bf16[12,2,64,128]{3,2,1,0:T(8,128)(2,1)}, bf16[12,2,64,128]{3,2,1,0:T(8,128)(2,1)S(1)}, u32[]{:S(2)}, u32[]{:S(2)}) %collective-permute-start.22) | collective-permute-done | bytes 393248 | tf_op jit(solution)/shard_map/ppermute | solution.py:287
  296.7 5.2 %collective-permute-start.27 = (bf16[12,2,64,128]{3,2,1,0:T(8,128)(2,1)}, bf16[12,2,64,128]{3,2,1,0:T(8,128)(2,1)}, u32[]{:S(2)}, u32[]{:S(2)}) collective-permute-start(bf16[12,2,64,128]{3,2,1,0:T(8,128)(2,1)} %get-tuple-element.69), channel_id=1, source_target_pairs={{0,4},{2,6},{4,8},{6,10},{8,12},{10,14},{12,0},{14,2},{1,5},{3,7},... | collective-permute-start | bytes 1179656 | tf_op jit(solution)/shard_map/ppermute | solution.py:287
  301.9 12.0 %collective-permute-start.28 = (bf16[12,2,64,128]{3,2,1,0:T(8,128)(2,1)}, bf16[12,2,64,128]{3,2,1,0:T(8,128)(2,1)}, u32[]{:S(2)}, u32[]{:S(2)}) collective-permute-start(bf16[12,2,64,128]{3,2,1,0:T(8,128)(2,1)} %get-tuple-element.70), channel_id=1, source_target_pairs={{0,2},{2,4},{4,6},{6,8},{8,10},{10,12},{12,14},{14,0},{1,3},{3,5},... | collective-permute-start | bytes 1179656 | tf_op jit(solution)/shard_map/ppermute | solution.py:287
  314.0 9.6 %stats.2 = f32[128,128]{1,0:T(8,128)} custom-call(s32[2]{0:T(128)} %pad_add_fusion.place, s32[512]{0:T(512)} %recv_table.1.table.after, bf16[12,2,64,128]{3,2,1,0:T(8,128)(2,1)} %get-tuple-element.39.refs_0_, bf16[12,2,64,128]{3,2,1,0:T(8,128)(2,1)} %copy-done.3, bf16[12,2,64,128]{3,2,1,0:T(8,128)(2,1)} %copy-done.4, bf16[12,2,64,128]{3,2,1,0:T(8,128)(2,1)} %copy-done.5, ...), custom_call_target="tpu_custom_call" | custom-call | flops 1024 | bytes 1024 | tf_op jit(solution)/shard_map/stats/pallas_call | solution.py:349
  323.7 12.3 %all_to_all.65 = f32[8,16,128]{2,1,0:T(8,128)} all-to-all(f32[8,16,128]{2,1,0:T(8,128)} %bitcast.26), channel_id=1, replica_groups=mesh['seq'=16,'grp'=8,'store'=2] {'grp'}, dimensions={0} | all-to-all | bytes 131072 | tf_op jit(solution)/shard_map/all_to_all | solution.py:359
  349.4 17.2 %all-to-all-start.7 = ((bf16[16,2,128,128]{3,2,1,0:T(8,128)(2,1)}), bf16[16,2,128,128]{3,2,1,0:T(8,128)(2,1)S(1)}, u32[]{:S(2)}, u32[]{:S(2)}) async-start(bf16[16,2,128,128]{3,2,1,0:T(8,128)(2,1)} %unpack.3), calls=%async_computation.7 | async-start | bytes 2097152 | tf_op jit(solution)/shard_map/all_to_all | solution.py:401
  366.6 23.2 %grads.2 = (bf16[12,2,64,128]{3,2,1,0:T(8,128)(2,1)}, bf16[12,2,64,128]{3,2,1,0:T(8,128)(2,1)}, bf16[12,2,64,128]{3,2,1,0:T(8,128)(2,1)}, bf16[12,2,64,128]{3,2,...) custom-call(s32[2]{0:T(128)} %pad_add_fusion.place, ...), custom_call_target="tpu_custom_call" | custom-call | flops 1024 | bytes 1024 | tf_op jit(solution)/shard_map/grads/pallas_call | solution.py:369
  395.5 6.2 %collective-permute-start.11 = (bf16[12,2,64,128]{3,2,1,0:T(8,128)(2,1)}, bf16[12,2,64,128]{3,2,1,0:T(8,128)(2,1)S(1)}, u32[]{:S(2)}, u32[]{:S(2)}) collective-permute-start(bf16[12,2,64,128]{3,2,1,0:T(8,128)(2,1)} %get-tuple-element.51), channel_id=1, source_target_pairs={{0,8},{2,10},{4,12},{6,14},{8,0},{10,2},{12,4},{14,6},{1,9},{3,11}... | collective-permute-start | bytes 1179656 | tf_op jit(solution)/shard_map/ppermute | solution.py:287
  407.5 5.5 %collective-permute-start.13 = (bf16[12,2,64,128]{3,2,1,0:T(8,128)(2,1)}, bf16[12,2,64,128]{3,2,1,0:T(8,128)(2,1)}, u32[]{:S(2)}, u32[]{:S(2)}) collective-permute-start(bf16[12,2,64,128]{3,2,1,0:T(8,128)(2,1)} %get-tuple-element.53), channel_id=1, source_target_pairs={{0,4},{2,6},{4,8},{6,10},{8,12},{10,14},{12,0},{14,2},{1,5},{3,7},... | collective-permute-start | bytes 1179656 | tf_op jit(solution)/shard_map/ppermute | solution.py:287
  413.0 9.9 %collective-permute-done.9.refs_2_ = bf16[12,2,64,128]{3,2,1,0:T(8,128)(2,1)S(1)} collective-permute-done((bf16[12,2,64,128]{3,2,1,0:T(8,128)(2,1)}, bf16[12,2,64,128]{3,2,1,0:T(8,128)(2,1)S(1)}, u32[]{:S(2)}, u32[]{:S(2)}) %collective-permute-start.9) | collective-permute-done | bytes 393248 | tf_op jit(solution)/shard_map/ppermute | solution.py:287
  425.7 6.8 %collective-permute-done.12.refs_5_ = bf16[12,2,64,128]{3,2,1,0:T(8,128)(2,1)} collective-permute-done((bf16[12,2,64,128]{3,2,1,0:T(8,128)(2,1)}, bf16[12,2,64,128]{3,2,1,0:T(8,128)(2,1)}, u32[]{:S(2)}, u32[]{:S(2)}) %collective-permute-start.12) | collective-permute-done | bytes 393248 | tf_op jit(solution)/shard_map/ppermute | solution.py:287
  433.9 8.1 %collective-permute-done.14.refs_7_ = bf16[12,2,64,128]{3,2,1,0:T(8,128)(2,1)} collective-permute-done((bf16[12,2,64,128]{3,2,1,0:T(8,128)(2,1)}, bf16[12,2,64,128]{3,2,1,0:T(8,128)(2,1)}, u32[]{:S(2)}, u32[]{:S(2)}) %collective-permute-start.14) | collective-permute-done | bytes 393248 | tf_op jit(solution)/shard_map/ppermute | solution.py:287
  445.9 7.3 %all-to-all-start.3 = ((bf16[16,2,128,128]{3,2,1,0:T(8,128)(2,1)}), bf16[16,2,128,128]{3,2,1,0:T(8,128)(2,1)S(1)}, u32[]{:S(2)}, u32[]{:S(2)}) async-start(bf16[16,2,128,128]{3,2,1,0:T(8,128)(2,1)} %unpack.2), calls=%async_computation.3 | async-start | bytes 2097152 | tf_op jit(solution)/shard_map/all_to_all | solution.py:401
  454.2 10.1 %join.1 = bf16[16,2,2,2,128,128]{5,4,3,2,1,0:T(8,128)(2,1)} custom-call(s32[2]{0:T(128)} %pad_add_fusion.place, bf16[16,2,128,128]{3,2,1,0:T(8,128)(2,1)} %get-tuple-element.71.keep0, bf16[16,2,128,128]{3,2,1,0:T(8,128)(2,1)} %get-tuple-element.72.keep1, bf16[16,2,128,128]{3,2,1,0:T(8,128)(2,1)} %copy-done.13, ...), custom_call_target="tpu_custom_call" | custom-call | bytes 1024 | tf_op jit(solution)/shard_map/join/pallas_call | solution.py:403
  (122 shorter events, 90.5 us)
Async XLA Ops:
  4.4 23.3 %all-to-all-start.4 = ((bf16[16,2,128,128]{3,2,1,0:T(8,128)(2,1)}), bf16[16,2,128,128]{3,2,1,0:T(8,128)(2,1)S(1)}, u32[]{:S(2)}, u32[]{:S(2)}) async-start(bf16[16,2,128,128]{3,2,1,0:T(8,128)(2,1)} %pad_maximum_fusion.1), calls=%async_computation.4 | async-start | bytes 2097152 | tf_op jit(solution)/shard_map/all_to_all | solution.py:327
  15.1 134.3 %collective-permute-start.7 = (bf16[16,2,2,128,128]{4,3,2,1,0:T(8,128)(2,1)}, bf16[16,2,2,128,128]{4,3,2,1,0:T(8,128)(2,1)S(1)}, u32[]{:S(2)}, u32[]{:S(2)}) collective-permute-start(bf16[16,2,2,128,128]{4,3,2,1,0:T(8,128)(2,1)} %dynamic-slice_bitcast_fusion), channel_id=1, source_target_pairs={{0,1},{1,0},{2,3},{3,2},{4,5},{5,4},{6,7},{7,6},{8,9},{9,8},{10,11... | collective-permute-start | bytes 6291464 | tf_op jit(solution)/shard_map/ppermute | solution.py:299
  28.7 106.8 %all-to-all-start = ((bf16[16,2,128,128]{3,2,1,0:T(8,128)(2,1)}), bf16[16,2,128,128]{3,2,1,0:T(8,128)(2,1)S(1)}, u32[]{:S(2)}, u32[]{:S(2)}) async-start(bf16[16,2,128,128]{3,2,1,0:T(8,128)(2,1)} %pad_maximum_fusion), calls=%async_computation | async-start | bytes 2097152 | tf_op jit(solution)/shard_map/all_to_all | solution.py:327
  68.2 19.4 %collective-permute-start.15 = (bf16[12,2,64,128]{3,2,1,0:T(8,128)(2,1)}, bf16[12,2,64,128]{3,2,1,0:T(8,128)(2,1)S(1)}, u32[]{:S(2)}, u32[]{:S(2)}) collective-permute-start(bf16[12,2,64,128]{3,2,1,0:T(8,128)(2,1)} %get-tuple-element.56), channel_id=1, source_target_pairs={{0,2},{2,4},{4,6},{6,8},{8,10},{10,12},{12,14},{14,0},{1,3},{3,5},... | collective-permute-start | bytes 1179656 | tf_op jit(solution)/shard_map/ppermute | solution.py:287
  68.3 40.0 %collective-permute-start.16 = (bf16[12,2,64,128]{3,2,1,0:T(8,128)(2,1)}, bf16[12,2,64,128]{3,2,1,0:T(8,128)(2,1)S(1)}, u32[]{:S(2)}, u32[]{:S(2)}) collective-permute-start(bf16[12,2,64,128]{3,2,1,0:T(8,128)(2,1)} %get-tuple-element.57), channel_id=1, source_target_pairs={{0,4},{2,6},{4,8},{6,10},{8,12},{10,14},{12,0},{14,2},{1,5},{3,7},... | collective-permute-start | bytes 1179656 | tf_op jit(solution)/shard_map/ppermute | solution.py:287
  69.9 54.5 %collective-permute-start.17 = (bf16[12,2,64,128]{3,2,1,0:T(8,128)(2,1)}, bf16[12,2,64,128]{3,2,1,0:T(8,128)(2,1)S(1)}, u32[]{:S(2)}, u32[]{:S(2)}) collective-permute-start(bf16[12,2,64,128]{3,2,1,0:T(8,128)(2,1)} %get-tuple-element.58), channel_id=1, source_target_pairs={{0,6},{2,8},{4,10},{6,12},{8,14},{10,0},{12,2},{14,4},{1,7},{3,9},... | collective-permute-start | bytes 1179656 | tf_op jit(solution)/shard_map/ppermute | solution.py:287
  71.8 68.0 %collective-permute-start.18 = (bf16[12,2,64,128]{3,2,1,0:T(8,128)(2,1)}, bf16[12,2,64,128]{3,2,1,0:T(8,128)(2,1)S(1)}, u32[]{:S(2)}, u32[]{:S(2)}) collective-permute-start(bf16[12,2,64,128]{3,2,1,0:T(8,128)(2,1)} %get-tuple-element.59), channel_id=1, source_target_pairs={{0,8},{2,10},{4,12},{6,14},{8,0},{10,2},{12,4},{14,6},{1,9},{3,11}... | collective-permute-start | bytes 1179656 | tf_op jit(solution)/shard_map/ppermute | solution.py:287
  87.7 52.2 %collective-permute-start.19 = (bf16[12,2,64,128]{3,2,1,0:T(8,128)(2,1)}, bf16[12,2,64,128]{3,2,1,0:T(8,128)(2,1)}, u32[]{:S(2)}, u32[]{:S(2)}) collective-permute-start(bf16[12,2,64,128]{3,2,1,0:T(8,128)(2,1)} %get-tuple-element.60), channel_id=1, source_target_pairs={{0,10},{2,12},{4,14},{6,0},{8,2},{10,4},{12,6},{14,8},{1,11},{3,13... | collective-permute-start | bytes 1179656 | tf_op jit(solution)/shard_map/ppermute | solution.py:287
  108.3 36.6 %collective-permute-start.20 = (bf16[12,2,64,128]{3,2,1,0:T(8,128)(2,1)}, bf16[12,2,64,128]{3,2,1,0:T(8,128)(2,1)}, u32[]{:S(2)}, u32[]{:S(2)}) collective-permute-start(bf16[12,2,64,128]{3,2,1,0:T(8,128)(2,1)} %get-tuple-element.61), channel_id=1, source_target_pairs={{0,12},{2,14},{4,0},{6,2},{8,4},{10,6},{12,8},{14,10},{1,13},{3,15... | collective-permute-start | bytes 1179656 | tf_op jit(solution)/shard_map/ppermute | solution.py:287
  125.1 22.9 %collective-permute-start.21 = (bf16[12,2,64,128]{3,2,1,0:T(8,128)(2,1)}, bf16[12,2,64,128]{3,2,1,0:T(8,128)(2,1)}, u32[]{:S(2)}, u32[]{:S(2)}) collective-permute-start(bf16[12,2,64,128]{3,2,1,0:T(8,128)(2,1)} %get-tuple-element.62), channel_id=1, source_target_pairs={{0,14},{2,0},{4,2},{6,4},{8,6},{10,8},{12,10},{14,12},{1,15},{3,1}... | collective-permute-start | bytes 1179656 | tf_op jit(solution)/shard_map/ppermute | solution.py:287
  139.8 104.9 %collective-permute-start = (bf16[12,2,64,128]{3,2,1,0:T(8,128)(2,1)}, bf16[12,2,64,128]{3,2,1,0:T(8,128)(2,1)S(1)}, u32[]{:S(2)}, u32[]{:S(2)}) collective-permute-start(bf16[12,2,64,128]{3,2,1,0:T(8,128)(2,1)} %get-tuple-element.40), channel_id=1, source_target_pairs={{0,2},{2,4},{4,6},{6,8},{8,10},{10,12},{12,14},{14,0},{1,3},{3,5},... | collective-permute-start | bytes 1179656 | tf_op jit(solution)/shard_map/ppermute | solution.py:287
  139.9 107.4 %collective-permute-start.1 = (bf16[12,2,64,128]{3,2,1,0:T(8,128)(2,1)}, bf16[12,2,64,128]{3,2,1,0:T(8,128)(2,1)S(1)}, u32[]{:S(2)}, u32[]{:S(2)}) collective-permute-start(bf16[12,2,64,128]{3,2,1,0:T(8,128)(2,1)} %get-tuple-element.41), channel_id=1, source_target_pairs={{0,4},{2,6},{4,8},{6,10},{8,12},{10,14},{12,0},{14,2},{1,5},{3,7},... | collective-permute-start | bytes 1179656 | tf_op jit(solution)/shard_map/ppermute | solution.py:287
  144.9 102.4 %collective-permute-start.2 = (bf16[12,2,64,128]{3,2,1,0:T(8,128)(2,1)}, bf16[12,2,64,128]{3,2,1,0:T(8,128)(2,1)S(1)}, u32[]{:S(2)}, u32[]{:S(2)}) collective-permute-start(bf16[12,2,64,128]{3,2,1,0:T(8,128)(2,1)} %get-tuple-element.42), channel_id=1, source_target_pairs={{0,6},{2,8},{4,10},{6,12},{8,14},{10,0},{12,2},{14,4},{1,7},{3,9},... | collective-permute-start | bytes 1179656 | tf_op jit(solution)/shard_map/ppermute | solution.py:287
  148.0 100.0 %collective-permute-start.3 = (bf16[12,2,64,128]{3,2,1,0:T(8,128)(2,1)}, bf16[12,2,64,128]{3,2,1,0:T(8,128)(2,1)}, u32[]{:S(2)}, u32[]{:S(2)}) collective-permute-start(bf16[12,2,64,128]{3,2,1,0:T(8,128)(2,1)} %get-tuple-element.43), channel_id=1, source_target_pairs={{0,8},{2,10},{4,12},{6,14},{8,0},{10,2},{12,4},{14,6},{1,9},{3,11}... | collective-permute-start | bytes 1179656 | tf_op jit(solution)/shard_map/ppermute | solution.py:287
  212.3 38.7 %collective-permute-start.4 = (bf16[12,2,64,128]{3,2,1,0:T(8,128)(2,1)}, bf16[12,2,64,128]{3,2,1,0:T(8,128)(2,1)S(1)}, u32[]{:S(2)}, u32[]{:S(2)}) collective-permute-start(bf16[12,2,64,128]{3,2,1,0:T(8,128)(2,1)} %get-tuple-element.44), channel_id=1, source_target_pairs={{0,10},{2,12},{4,14},{6,0},{8,2},{10,4},{12,6},{14,8},{1,11},{3,13... | collective-permute-start | bytes 1179656 | tf_op jit(solution)/shard_map/ppermute | solution.py:287
  247.3 36.1 %collective-permute-start.6 = (bf16[12,2,64,128]{3,2,1,0:T(8,128)(2,1)}, bf16[12,2,64,128]{3,2,1,0:T(8,128)(2,1)S(1)}, u32[]{:S(2)}, u32[]{:S(2)}) collective-permute-start(bf16[12,2,64,128]{3,2,1,0:T(8,128)(2,1)} %get-tuple-element.46), channel_id=1, source_target_pairs={{0,14},{2,0},{4,2},{6,4},{8,6},{10,8},{12,10},{14,12},{1,15},{3,1}... | collective-permute-start | bytes 1179656 | tf_op jit(solution)/shard_map/ppermute | solution.py:287
  247.3 49.4 %collective-permute-start.22 = (bf16[12,2,64,128]{3,2,1,0:T(8,128)(2,1)}, bf16[12,2,64,128]{3,2,1,0:T(8,128)(2,1)S(1)}, u32[]{:S(2)}, u32[]{:S(2)}) collective-permute-start(bf16[12,2,64,128]{3,2,1,0:T(8,128)(2,1)} %get-tuple-element.64), channel_id=1, source_target_pairs={{0,14},{2,0},{4,2},{6,4},{8,6},{10,8},{12,10},{14,12},{1,15},{3,1}... | collective-permute-start | bytes 1179656 | tf_op jit(solution)/shard_map/ppermute | solution.py:287
  248.0 54.0 %collective-permute-start.23 = (bf16[12,2,64,128]{3,2,1,0:T(8,128)(2,1)}, bf16[12,2,64,128]{3,2,1,0:T(8,128)(2,1)S(1)}, u32[]{:S(2)}, u32[]{:S(2)}) collective-permute-start(bf16[12,2,64,128]{3,2,1,0:T(8,128)(2,1)} %get-tuple-element.65), channel_id=1, source_target_pairs={{0,12},{2,14},{4,0},{6,2},{8,4},{10,6},{12,8},{14,10},{1,13},{3,15... | collective-permute-start | bytes 1179656 | tf_op jit(solution)/shard_map/ppermute | solution.py:287
  251.0 90.1 %collective-permute-start.24 = (bf16[12,2,64,128]{3,2,1,0:T(8,128)(2,1)}, bf16[12,2,64,128]{3,2,1,0:T(8,128)(2,1)}, u32[]{:S(2)}, u32[]{:S(2)}) collective-permute-start(bf16[12,2,64,128]{3,2,1,0:T(8,128)(2,1)} %get-tuple-element.66), channel_id=1, source_target_pairs={{0,10},{2,12},{4,14},{6,0},{8,2},{10,4},{12,6},{14,8},{1,11},{3,13... | collective-permute-start | bytes 1179656 | tf_op jit(solution)/shard_map/ppermute | solution.py:287
  259.7 81.5 %collective-permute-start.25 = (bf16[12,2,64,128]{3,2,1,0:T(8,128)(2,1)}, bf16[12,2,64,128]{3,2,1,0:T(8,128)(2,1)}, u32[]{:S(2)}, u32[]{:S(2)}) collective-permute-start(bf16[12,2,64,128]{3,2,1,0:T(8,128)(2,1)} %get-tuple-element.67), channel_id=1, source_target_pairs={{0,8},{2,10},{4,12},{6,14},{8,0},{10,2},{12,4},{14,6},{1,9},{3,11}... | collective-permute-start | bytes 1179656 | tf_op jit(solution)/shard_map/ppermute | solution.py:287
  283.4 57.7 %collective-permute-start.26 = (bf16[12,2,64,128]{3,2,1,0:T(8,128)(2,1)}, bf16[12,2,64,128]{3,2,1,0:T(8,128)(2,1)}, u32[]{:S(2)}, u32[]{:S(2)}) collective-permute-start(bf16[12,2,64,128]{3,2,1,0:T(8,128)(2,1)} %get-tuple-element.68), channel_id=1, source_target_pairs={{0,6},{2,8},{4,10},{6,12},{8,14},{10,0},{12,2},{14,4},{1,7},{3,9},... | collective-permute-start | bytes 1179656 | tf_op jit(solution)/shard_map/ppermute | solution.py:287
  296.7 44.4 %collective-permute-start.27 = (bf16[12,2,64,128]{3,2,1,0:T(8,128)(2,1)}, bf16[12,2,64,128]{3,2,1,0:T(8,128)(2,1)}, u32[]{:S(2)}, u32[]{:S(2)}) collective-permute-start(bf16[12,2,64,128]{3,2,1,0:T(8,128)(2,1)} %get-tuple-element.69), channel_id=1, source_target_pairs={{0,4},{2,6},{4,8},{6,10},{8,12},{10,14},{12,0},{14,2},{1,5},{3,7},... | collective-permute-start | bytes 1179656 | tf_op jit(solution)/shard_map/ppermute | solution.py:287
  301.9 39.2 %collective-permute-start.28 = (bf16[12,2,64,128]{3,2,1,0:T(8,128)(2,1)}, bf16[12,2,64,128]{3,2,1,0:T(8,128)(2,1)}, u32[]{:S(2)}, u32[]{:S(2)}) collective-permute-start(bf16[12,2,64,128]{3,2,1,0:T(8,128)(2,1)} %get-tuple-element.70), channel_id=1, source_target_pairs={{0,2},{2,4},{4,6},{6,8},{8,10},{10,12},{12,14},{14,0},{1,3},{3,5},... | collective-permute-start | bytes 1179656 | tf_op jit(solution)/shard_map/ppermute | solution.py:287
  349.4 96.5 %all-to-all-start.7 = ((bf16[16,2,128,128]{3,2,1,0:T(8,128)(2,1)}), bf16[16,2,128,128]{3,2,1,0:T(8,128)(2,1)S(1)}, u32[]{:S(2)}, u32[]{:S(2)}) async-start(bf16[16,2,128,128]{3,2,1,0:T(8,128)(2,1)} %unpack.3), calls=%async_computation.7 | async-start | bytes 2097152 | tf_op jit(solution)/shard_map/all_to_all | solution.py:401
  389.9 33.0 %collective-permute-start.9 = (bf16[12,2,64,128]{3,2,1,0:T(8,128)(2,1)}, bf16[12,2,64,128]{3,2,1,0:T(8,128)(2,1)S(1)}, u32[]{:S(2)}, u32[]{:S(2)}) collective-permute-start(bf16[12,2,64,128]{3,2,1,0:T(8,128)(2,1)} %get-tuple-element.49), channel_id=1, source_target_pairs={{0,12},{2,14},{4,0},{6,2},{8,4},{10,6},{12,8},{14,10},{1,13},{3,15... | collective-permute-start | bytes 1179656 | tf_op jit(solution)/shard_map/ppermute | solution.py:287
  392.4 32.8 %collective-permute-start.10 = (bf16[12,2,64,128]{3,2,1,0:T(8,128)(2,1)}, bf16[12,2,64,128]{3,2,1,0:T(8,128)(2,1)S(1)}, u32[]{:S(2)}, u32[]{:S(2)}) collective-permute-start(bf16[12,2,64,128]{3,2,1,0:T(8,128)(2,1)} %get-tuple-element.50), channel_id=1, source_target_pairs={{0,10},{2,12},{4,14},{6,0},{8,2},{10,4},{12,6},{14,8},{1,11},{3,13... | collective-permute-start | bytes 1179656 | tf_op jit(solution)/shard_map/ppermute | solution.py:287
  395.5 29.7 %collective-permute-start.11 = (bf16[12,2,64,128]{3,2,1,0:T(8,128)(2,1)}, bf16[12,2,64,128]{3,2,1,0:T(8,128)(2,1)S(1)}, u32[]{:S(2)}, u32[]{:S(2)}) collective-permute-start(bf16[12,2,64,128]{3,2,1,0:T(8,128)(2,1)} %get-tuple-element.51), channel_id=1, source_target_pairs={{0,8},{2,10},{4,12},{6,14},{8,0},{10,2},{12,4},{14,6},{1,9},{3,11}... | collective-permute-start | bytes 1179656 | tf_op jit(solution)/shard_map/ppermute | solution.py:287
  401.7 30.9 %collective-permute-start.12 = (bf16[12,2,64,128]{3,2,1,0:T(8,128)(2,1)}, bf16[12,2,64,128]{3,2,1,0:T(8,128)(2,1)}, u32[]{:S(2)}, u32[]{:S(2)}) collective-permute-start(bf16[12,2,64,128]{3,2,1,0:T(8,128)(2,1)} %get-tuple-element.52), channel_id=1, source_target_pairs={{0,6},{2,8},{4,10},{6,12},{8,14},{10,0},{12,2},{14,4},{1,7},{3,9},... | collective-permute-start | bytes 1179656 | tf_op jit(solution)/shard_map/ppermute | solution.py:287
  407.5 26.4 %collective-permute-start.13 = (bf16[12,2,64,128]{3,2,1,0:T(8,128)(2,1)}, bf16[12,2,64,128]{3,2,1,0:T(8,128)(2,1)}, u32[]{:S(2)}, u32[]{:S(2)}) collective-permute-start(bf16[12,2,64,128]{3,2,1,0:T(8,128)(2,1)} %get-tuple-element.53), channel_id=1, source_target_pairs={{0,4},{2,6},{4,8},{6,10},{8,12},{10,14},{12,0},{14,2},{1,5},{3,7},... | collective-permute-start | bytes 1179656 | tf_op jit(solution)/shard_map/ppermute | solution.py:287
  425.2 28.0 %collective-permute-start.29 = (bf16[16,2,128,128]{3,2,1,0:T(8,128)(2,1)}, bf16[16,2,128,128]{3,2,1,0:T(8,128)(2,1)S(1)}, u32[]{:S(2)}, u32[]{:S(2)}) collective-permute-start(bf16[16,2,128,128]{3,2,1,0:T(8,128)(2,1)} %get-tuple-element.73), channel_id=1, source_target_pairs={{0,1},{1,0},{2,3},{3,2},{4,5},{5,4},{6,7},{7,6},{8,9},{9,8},{10,11... | collective-permute-start | bytes 3145736 | tf_op jit(solution)/shard_map/ppermute | solution.py:387
  425.2 28.0 %collective-permute-start.30 = (bf16[16,2,128,128]{3,2,1,0:T(8,128)(2,1)}, bf16[16,2,128,128]{3,2,1,0:T(8,128)(2,1)}, u32[]{:S(2)}, u32[]{:S(2)}) collective-permute-start(bf16[16,2,128,128]{3,2,1,0:T(8,128)(2,1)} %get-tuple-element.74), channel_id=1, source_target_pairs={{0,1},{1,0},{2,3},{3,2},{4,5},{5,4},{6,7},{7,6},{8,9},{9,8},{10,11... | collective-permute-start | bytes 3145736 | tf_op jit(solution)/shard_map/ppermute | solution.py:387
  445.9 19.2 %all-to-all-start.3 = ((bf16[16,2,128,128]{3,2,1,0:T(8,128)(2,1)}), bf16[16,2,128,128]{3,2,1,0:T(8,128)(2,1)S(1)}, u32[]{:S(2)}, u32[]{:S(2)}) async-start(bf16[16,2,128,128]{3,2,1,0:T(8,128)(2,1)} %unpack.2), calls=%async_computation.3 | async-start | bytes 2097152 | tf_op jit(solution)/shard_map/all_to_all | solution.py:401
  (30 other events, 687.0 us)

commit v3 on v2

v3 whole, which is shorter than its diff:
```python
import functools
import math

import jax
import jax.numpy as jnp
from jax import lax
from jax.experimental import pallas as pl
from jax.experimental.pallas import tpu as pltpu
from jax.sharding import PartitionSpec as P

RING = 8
CAP = 6
SLOTS = 2 * CAP
ROWS = RING * SLOTS
SPAN = 64
DH = 128
SEQ = 16
INST = 64
SPANS = INST // 2
BLK = 16
UNROLL = 4
COST = 1 << 10
LIST = 104
SCALE = 1.0 / math.sqrt(DH)
F32 = jnp.float32
BF16 = jnp.bfloat16

SMEM = pl.BlockSpec(memory_space=pltpu.SMEM)
VMEM = pl.BlockSpec(memory_space=pltpu.VMEM)
ANY = pl.BlockSpec(memory_space=pltpu.HBM)

STAT_ROWS = RING * 16
R_STAT, R_BLK, R_PAIR, R_COUNT, R_SIZE = 128, 256, 384, 512, 640


def cost(flops, nbytes):
    return pl.CostEstimate(flops=flops, bytes_accessed=nbytes, transcendentals=0)


def recv_table_kernel(place, names, table, count, where):
    def rank(source, carry):
        for o in range(RING * 2):
            count[o] = 0

        def step(i, carry):
            own = names[source, i]
            slot = (own & 1) * CAP + count[own]
            count[own] = count[own] + 1
            where[source * INST + i] = (own >> 1) * STAT_ROWS + source * 16 + slot
            return carry

        return lax.fori_loop(0, INST, step, carry, unroll=8)

    lax.fori_loop(0, RING, rank, 0)

    def group(source, total):
        def step(i, total):
            own = names[source, i]
            at = where[source * INST + i]
            table[total] = ((place[0] - source) & (RING - 1)) * SLOTS + (at & 15)
            table[R_STAT + total] = at & (STAT_ROWS - 1)
            table[R_BLK + total] = (own & 1) * BLK + names[source, INST + i]
            table[R_PAIR + total] = where[source * INST + (i ^ 1)]
            return total + ((own >> 1) == place[0]).astype(jnp.int32)

        return lax.fori_loop(0, INST, step, total, unroll=8)

    total = lax.fori_loop(0, RING, group, 0)

    def pad(n, carry):
        table[n] = ROWS
        table[R_STAT + n] = STAT_ROWS
        table[R_BLK + n] = 0
        table[R_PAIR + n] = 0
        return carry

    lax.fori_loop(total, LIST, pad, 0)
    table[R_COUNT] = total


def part_copies(stage, parts, sems, load):
    copies = []
    for d in range(RING):
        rows = stage.at[pl.ds(d * SLOTS, SLOTS)]
        ends = (parts[d], rows) if load else (rows, parts[d])
        copies.append(pltpu.make_async_copy(*ends, sems.at[d]))
        copies[-1].start()
    return copies


def pack_kernel(place, names, rows, *refs):
    outs, (table, sent, stage, count, sems) = refs[-RING - 5 : -5], refs[-5:]
    for o in range(RING * 2):
        count[o] = 0

    def step(i, carry):
        own = names[i]
        chip = ((own >> 1) - place[0]) & (RING - 1)
        row = chip * SLOTS + (own & 1) * CAP + count[own]
        count[own] = count[own] + 1
        table[i] = row
        span = i >> 1
        start = pl.multiple_of((span & 1) * SPAN, SPAN)
        for kind in range(2):
            stage[row, kind] = rows[span >> 1, kind, pl.ds(start, SPAN), :]
        sent[0, i] = own
        sent[0, INST + i] = names[INST + i]
        return carry

    lax.fori_loop(0, INST, step, 0, unroll=4)
    for copy in part_copies(stage, outs, sems, False):
        copy.wait()


def gate_kernel(after, *refs):
    pass


def load_store(pair, core, own, other, store, sems):
    mine = pltpu.make_async_copy(
        own.at[:, :, core, pair], store.at[pl.ds(core * BLK, BLK)], sems.at[RING]
    )
    theirs = pltpu.make_async_copy(
        other.at[:, :, pair], store.at[pl.ds((1 - core) * BLK, BLK)], sems.at[RING + 1]
    )
    mine.start()
    theirs.start()
    return [mine, theirs]


def dot(a, b, dims):
    return lax.dot_general(a, b, (dims, ((), ())), preferred_element_type=F32)


NT = ((1,), (1,))
NN = ((1,), (0,))
TN = ((0,), (0,))


def load_all(pair, place, parts, own, other, stage, store, sems):
    copies = load_store(pair, place[1], own, other, store, sems)
    copies += part_copies(stage, parts, sems, True)
    stage[ROWS] = jnp.zeros(stage.shape[1:], BF16)
    return copies


def stat_kernel(pair, place, table, *refs):
    parts, own, other = refs[:RING], refs[RING], refs[RING + 1]
    out, stage, store, stats, sems = refs[-5:]
    copies = load_all(pair, place, parts, own, other, stage, store, sems)
    stats[...] = jnp.zeros(stats.shape, F32)
    for copy in copies:
        copy.wait()

    def step(it, carry):
        for u in range(UNROLL):
            n = it * UNROLL + u
            row, srow, block = table[n], table[R_STAT + n], table[R_BLK + n]
            score = dot(store[block, 0], stage[row, 0], NT) * SCALE
            gprob = dot(store[block, 1], stage[row, 1], NT)
            top = jnp.max(score, axis=0, keepdims=True)
            weight = jnp.exp(score - top)
            total = jnp.sum(weight, axis=0, keepdims=True)
            delta = jnp.sum(weight * gprob, axis=0, keepdims=True) / total
            stats[pl.ds(srow, 1), :] = jnp.concatenate([top + jnp.log(total), delta], axis=1)
        return carry

    lax.fori_loop(0, (table[R_COUNT] + UNROLL - 1) // UNROLL, step, 0)
    out[...] = stats[:STAT_ROWS]


def grad_kernel(pair, place, table, given, *refs):
    parts, own, other = refs[:RING], refs[RING], refs[RING + 1]
    outs = refs[RING + 2 : 2 * RING + 2]
    keep, send, stage, store, result, mine, theirs, stats, total, sems = refs[2 * RING + 2 :]
    copies = load_all(pair, place, parts, own, other, stage, store, sems)
    base = place[0] * STAT_ROWS

    def take(n, carry):
        srow = jnp.minimum(table[R_STAT + n], STAT_ROWS - 1)
        mine[pl.ds(n, 1), :] = given[pl.ds(base + srow, 1), :]
        theirs[pl.ds(n, 1), :] = given[pl.ds(table[R_PAIR + n], 1), :]
        return carry

    lax.fori_loop(0, LIST, take, 0, unroll=8)
    log1, log2 = mine[:, :SPAN], theirs[:, :SPAN]
    top = jnp.maximum(log1, log2)
    both = top + jnp.log(jnp.exp(log1 - top) + jnp.exp(log2 - top))
    delta = jnp.exp(log1 - both) * mine[:, SPAN:] + jnp.exp(log2 - both) * theirs[:, SPAN:]
    merged = jnp.concatenate([both, delta], axis=1)
    used = lax.broadcasted_iota(jnp.int32, (LIST, DH), 0) < table[R_COUNT]
    stats[...] = jnp.where(used, merged, 0.0)

    def clear(b, carry):
        total[b] = jnp.zeros(total.shape[1:], F32)
        return carry

    lax.fori_loop(0, 2 * BLK, clear, 0)
    for copy in copies:
        copy.wait()

    def step(it, carry):
        adds = []
        for u in range(UNROLL):
            n = it * UNROLL + u
            row, block = table[n], table[R_BLK + n]
            query, grad = stage[row, 0], stage[row, 1]
            key, value = store[block, 0], store[block, 1]
            stat = stats[pl.ds(n, 1), :]
            score = dot(key, query, NT) * SCALE
            prob = jnp.exp(score - stat[:, :SPAN])
            dscore = (prob * (dot(value, grad, NT) - stat[:, SPAN:])).astype(BF16)
            prob = prob.astype(BF16)
            result[row, 0] = dot(prob, value, TN).astype(BF16)
            result[row, 1] = (dot(dscore, key, TN) * SCALE).astype(BF16)
            total[block, 0] += dot(dscore, query, NN)
            total[block, 1] += dot(prob, grad, NN)
        return carry

    lax.fori_loop(0, (table[R_COUNT] + UNROLL - 1) // UNROLL, step, 0)
    copies = part_copies(result, outs, sems, False)

    def finish(b, carry):
        for half, core in ((keep, place[1]), (send, 1 - place[1])):
            half[b, 0] = (total[core * BLK + b, 0] * SCALE).astype(BF16)
            half[b, 1] = total[core * BLK + b, 1].astype(BF16)
        return carry

    lax.fori_loop(0, BLK, finish, 0)
    for copy in copies:
        copy.wait()


def unpack_kernel(table, *refs):
    parts, (out, stage, sems) = refs[:RING], refs[-3:]
    for copy in part_copies(stage, parts, sems, True):
        copy.wait()
    def step(c, carry):
        one, two = table[2 * c], table[2 * c + 1]
        start = pl.multiple_of((c & 1) * SPAN, SPAN)
        for kind in range(2):
            summed = stage[one, kind].astype(F32) + stage[two, kind].astype(F32)
            out[c >> 1, kind, pl.ds(start, SPAN), :] = summed.astype(BF16)
        return carry

    lax.fori_loop(0, SPANS, step, 0, unroll=2)


def join_kernel(place, keep0, keep1, got0, got1, out):
    core = place[1]
    for ref, half, pair in (
        (keep0, core, 0),
        (keep1, core, 1),
        (got0, 1 - core, 0),
        (got1, 1 - core, 1),
    ):
        for kind in range(2):
            out[0, kind, half, pair] = ref[0, kind]


def shape(dims, dtype=BF16):
    return jax.ShapeDtypeStruct(dims, dtype)


PARAMS = pltpu.CompilerParams(vmem_limit_bytes=60 * 1024 * 1024)
PART = (SLOTS, 2, SPAN, DH)
STAGE = pltpu.VMEM((ROWS + 1, 2, SPAN, DH), BF16)
STORE = pltpu.VMEM((2 * BLK, 2, 128, DH), BF16)
SEMS = pltpu.SemaphoreType.DMA((RING + 2,))


EARLY, LATE = (3, 5, 4, 1, 7), (2, 6)


def exchange(rows):
    return lax.all_to_all(rows, "seq", split_axis=0, concat_axis=0, tiled=True)


def ring_send(parts, sign, gated=(), after=None):
    parts = list(parts)
    if gated:
        for d, part in zip(gated, gate([parts[d] for d in gated], after)):
            parts[d] = part
    got = [parts[0]]
    for d in range(1, RING):
        pairs = [(i, (i + sign * d) % RING) for i in range(RING)]
        got.append(lax.ppermute(parts[d], "grp", pairs))
    return got


def gate(parts, after):
    return pl.pallas_call(
        gate_kernel,
        out_shape=[shape(part.shape, part.dtype) for part in parts],
        in_specs=[ANY] * (len(parts) + 1),
        out_specs=[ANY] * len(parts),
        input_output_aliases={n + 1: n for n in range(len(parts))},
        cost_estimate=cost(0, COST),
        name="gate",
    )(after, *parts)


def on_device(query, kv_store, nbr_owner, nbr_block, d_out):
    core = lax.axis_index("store")
    place = jnp.stack([lax.axis_index("grp"), core]).astype(jnp.int32)
    names = jnp.concatenate([nbr_owner.reshape(INST), nbr_block.reshape(INST)])
    swap = [(0, 1), (1, 0)]
    kv_other = lax.ppermute(
        lax.dynamic_index_in_dim(kv_store, 1 - core, 2, keepdims=False), "store", swap
    )
    query_rows = query.reshape(SEQ, 2, 128, DH)
    grad_rows = d_out.reshape(SEQ, 2, 128, DH)

    arrived = []
    after = []
    for pair in range(2):
        rows = jnp.stack([query_rows[:, pair], grad_rows[:, pair]], axis=1)
        rows = exchange(rows)
        outs = pl.pallas_call(
            pack_kernel,
            out_shape=[shape(PART)] * RING
            + [shape((INST,), jnp.int32), shape((1, 2 * INST), jnp.int32)],
            in_specs=[SMEM, SMEM, VMEM] + [ANY] * len(after),
            out_specs=[ANY] * RING + [SMEM, SMEM],
            scratch_shapes=[
                pltpu.VMEM((ROWS, 2, SPAN, DH), BF16),
                pltpu.SMEM((2 * RING,), jnp.int32),
                pltpu.SemaphoreType.DMA((RING,)),
            ],
            compiler_params=PARAMS,
            cost_estimate=cost(0, COST),
            name="pack",
        )(place, names, rows, *after)
        send_table, sent = outs[RING:]
        if pair == 0:
            recv_table = pl.pallas_call(
                recv_table_kernel,
                out_shape=shape((R_SIZE,), jnp.int32),
                in_specs=[SMEM, SMEM],
                out_specs=SMEM,
                scratch_shapes=[
                    pltpu.SMEM((2 * RING,), jnp.int32),
                    pltpu.SMEM((RING * INST,), jnp.int32),
                ],
                cost_estimate=cost(0, COST),
                name="recv_table",
            )(place, lax.all_gather(sent, "grp", tiled=True))
            arrived.append(ring_send(outs[:RING], 1, LATE, recv_table))
            after = [arrived[0][d] for d in EARLY]
        else:
            arrived.append(ring_send(outs[:RING], 1))

    partial = []
    kv_grads = []
    after = []
    for pair in range(2):
        stats = pl.pallas_call(
            functools.partial(stat_kernel, pair),
            out_shape=shape((STAT_ROWS, DH), F32),
            in_specs=[SMEM, SMEM] + [ANY] * (RING + 2 + len(after)),
            out_specs=VMEM,
            scratch_shapes=[STAGE, STORE, pltpu.VMEM((STAT_ROWS + 8, DH), F32), SEMS],
            compiler_params=PARAMS,
            cost_estimate=cost(COST, COST),
            name="stats",
        )(place, recv_table, *arrived[pair], kv_store, kv_other, *after)
        given = lax.all_gather(stats, "grp").reshape(RING * STAT_ROWS, DH)
        outs = pl.pallas_call(
            functools.partial(grad_kernel, pair),
            out_shape=[shape(PART)] * RING + [shape((BLK, 2, 128, DH))] * 2,
            in_specs=[SMEM, SMEM, VMEM] + [ANY] * (RING + 2),
            out_specs=[ANY] * RING + [VMEM] * 2,
            scratch_shapes=[STAGE, STORE, STAGE]
            + [pltpu.VMEM((LIST, DH), F32)] * 3
            + [pltpu.VMEM((2 * BLK, 2, 128, DH), F32), SEMS],
            compiler_params=PARAMS,
            cost_estimate=cost(COST, COST),
            name="grads",
        )(place, recv_table, given, *arrived[pair], kv_store, kv_other)
        partial.append(outs[:RING])
        after = [outs[RING]]
        kv_grads.append((outs[RING], lax.ppermute(outs[RING + 1], "store", swap)))

    returned = [ring_send(partial[pair], -1) for pair in range(2)]
    results = []
    for pair in range(2):
        after = [returned[1][d] for d in (3, 5, 4)] if pair == 0 else []
        rows = pl.pallas_call(
            unpack_kernel,
            out_shape=shape((SEQ, 2, 128, DH)),
            in_specs=[SMEM] + [ANY] * (RING + len(after)),
            out_specs=VMEM,
            scratch_shapes=[
                pltpu.VMEM((ROWS, 2, SPAN, DH), BF16),
                pltpu.SemaphoreType.DMA((RING,)),
            ],
            compiler_params=PARAMS,
            cost_estimate=cost(0, COST),
            name="unpack",
        )(send_table, *returned[pair], *after)
        results.append(exchange(rows))

    d_kv = pl.pallas_call(
        join_kernel,
        out_shape=shape(kv_store.shape),
        grid=(BLK,),
        in_specs=[SMEM] + [pl.BlockSpec((1, 2, 128, DH), lambda b: (b, 0, 0, 0))] * 4,
        out_specs=pl.BlockSpec((1, 2, 2, 2, 128, DH), lambda b: (b, 0, 0, 0, 0, 0)),
        cost_estimate=cost(0, COST),
        name="join",
    )(place, kv_grads[0][0], kv_grads[1][0], kv_grads[0][1], kv_grads[1][1])
    attn_out = jnp.stack([results[0][:, 0], results[1][:, 0]], axis=1).reshape(query.shape)
    d_query = jnp.stack([results[0][:, 1], results[1][:, 1]], axis=1).reshape(query.shape)
    return (attn_out, d_query, d_kv)


def solution(mesh):
    in_specs = (
        P("grp", "store", None, "seq", None),
        P(("grp", "store"), None, None, "seq", None, None),
        P("grp", None, None),
        P("grp", None, None),
        P("grp", "store", None, "seq", None),
    )
    out_specs = (
        P("grp", "store", None, "seq", None),
        P("grp", "store", None, "seq", None),
        P(("grp", "store"), None, None, "seq", None, None),
    )
    return jax.shard_map(
        on_device, mesh=mesh, in_specs=in_specs, out_specs=out_specs, check_vma=False
    )
```

time: 469 us -> 492 us (1.049)
  blocking collectives: 78.1 us -> 143 us
  starting transfers between devices: 141 us -> 79.6 us
  waiting for transfers between devices: 124 us -> 138 us
    all_gather x1 -> x3, blocking collectives: 19.5 us -> 143 us  [the longest x2 117 us: on_device(): given = lax.all_gather(stats, 'grp').reshape(RING * STAT_ROWS, DH)]
    all_to_all x2 -> x0, blocking collectives: 58.6 us -> none  [on_device(): lax.all_to_all(stats, 'grp', split_axis=0, concat_axis=0, tiled=True)]
    ppermute x28, starting transfers between devices: 95.5 us -> 53.4 us  [ring_send(): got.append(lax.ppermute(parts[d], 'grp', pairs))]
    ppermute x28, waiting for transfers between devices: 106 us -> 128 us  [ring_send(): got.append(lax.ppermute(parts[d], 'grp', pairs))]
    all_to_all x6 -> x4, starting transfers between devices: 44.6 us -> 26.2 us  [exchange(): return lax.all_to_all(rows, 'seq', split_axis=0, concat_axis=0, tiled=True)]
    all_to_all x6 -> x4, waiting for transfers between devices: 17.8 us -> 10.6 us  [exchange(): return lax.all_to_all(rows, 'seq', split_axis=0, concat_axis=0, tiled=True)]
    pallas_call x5 -> x3, Pallas kernels: 12 us -> 8.3 us  [the longest x2 8.29 us: on_device(): pl.pallas_call(pack_kernel, out_shape=[shape(PART)] * RING + [shape((INST...]
  transfers between devices with their start and end apart: 37 -> 35, of which waited for: 17 -> 13; matrix products, arithmetic and copies ran while one was open for 2% -> 1% of each run, Pallas kernels for 22% -> 21%
where the time goes in v3:
time: 492 us; the launch traced here: 487 us
  blocking collectives  143 us (29%)
  waiting for transfers between devices  138 us (28%)
  Pallas kernels  105 us (21%)
  starting transfers between devices  79.6 us (16%)
  local copies, waits for them, and re-layouts  13.1 us (3%)
  other arithmetic  6.67 us (1%)
    ppermute x28, waiting for transfers between devices, ring_send(): got.append(lax.ppermute(parts[d], 'grp', pairs))  128 us
    all_gather x2, blocking collectives, on_device(): given = lax.all_gather(stats, 'grp').reshape(RING * STAT_ROWS, DH)  117 us
    ppermute x28, starting transfers between devices, ring_send(): got.append(lax.ppermute(parts[d], 'grp', pairs))  53.4 us
    pallas_call x2, Pallas kernels, on_device(): pl.pallas_call(functools.partial(grad_kernel, pair), out_shape=[shape(PAR...  48.7 us
    all_gather x1, blocking collectives, on_device(): lax.all_gather(sent, 'grp', tiled=True)  26.4 us
    all_to_all x4, starting transfers between devices, exchange(): return lax.all_to_all(rows, 'seq', split_axis=0, concat_axis=0, tiled=True)  26.2 us
    pallas_call x2, Pallas kernels, on_device(): pl.pallas_call(functools.partial(stat_kernel, pair), out_shape=shape((STA...  19.9 us
    all_to_all x4, waiting for transfers between devices, exchange(): return lax.all_to_all(rows, 'seq', split_axis=0, concat_axis=0, tiled=True)  10.6 us
  transfers between devices with their start and end apart: 35, of which 13 were waited for; matrix products, arithmetic and copies ran while one was open for 1% of the time, Pallas kernels for 21%

profile of v3, /device:TPU:2, one launch (start us, length us, event | category | flops | bytes accessed | tf_op | source)
XLA Modules:
  0.0 486.6 jit_solution(7321231827870798720)
XLA Ops:
  4.4 7.5 %all-to-all-start.1 = ((bf16[16,2,128,128]{3,2,1,0:T(8,128)(2,1)}), bf16[16,2,128,128]{3,2,1,0:T(8,128)(2,1)S(1)}, u32[]{:S(2)}, u32[]{:S(2)}) async-start(bf16[16,2,128,128]{3,2,1,0:T(8,128)(2,1)} %pad_maximum_fusion.1), calls=%async_computation.1 | async-start | bytes 2097152 | tf_op jit(solution)/shard_map/all_to_all | solution.py:276
  17.8 9.9 %all-to-all-done.1.rows = bf16[16,2,128,128]{3,2,1,0:T(8,128)(2,1)S(1)} async-done(((bf16[16,2,128,128]{3,2,1,0:T(8,128)(2,1)}), bf16[16,2,128,128]{3,2,1,0:T(8,128)(2,1)S(1)}, u32[]{:S(2)}, u32[]{:S(2)}) %all-to-all-start.1) | async-done | bytes 1048608 | tf_op jit(solution)/shard_map/all_to_all | solution.py:276
  28.7 5.4 %all-to-all-start = ((bf16[16,2,128,128]{3,2,1,0:T(8,128)(2,1)}), bf16[16,2,128,128]{3,2,1,0:T(8,128)(2,1)S(1)}, u32[]{:S(2)}, u32[]{:S(2)}) async-start(bf16[16,2,128,128]{3,2,1,0:T(8,128)(2,1)} %pad_maximum_fusion), calls=%async_computation | async-start | bytes 2097152 | tf_op jit(solution)/shard_map/all_to_all | solution.py:276
  35.3 4.2 pack.2
  39.4 4.7 collective-permute-start
  46.4 5.4 %collective-permute-start.2 = (bf16[12,2,64,128]{3,2,1,0:T(8,128)(2,1)}, bf16[12,2,64,128]{3,2,1,0:T(8,128)(2,1)}, u32[]{:S(2)}, u32[]{:S(2)}) collective-permute-start(bf16[12,2,64,128]{3,2,1,0:T(8,128)(2,1)} %get-tuple-element.45), channel_id=1, source_target_pairs={{0,8},{2,10},{4,12},{6,14},{8,0},{10,2},{12,4},{14,6},{1,9},{3,11}... | collective-permute-start | bytes 1179656 | tf_op jit(solution)/shard_map/ppermute | solution.py:287
  52.8 28.9 %collective-permute-done.refs_0_.refs_3_ = bf16[12,2,64,128]{3,2,1,0:T(8,128)(2,1)S(1)} collective-permute-done((bf16[12,2,64,128]{3,2,1,0:T(8,128)(2,1)}, bf16[12,2,64,128]{3,2,1,0:T(8,128)(2,1)S(1)}, u32[]{:S(2)}, u32[]{:S(2)}) %collective-permute-start) | collective-permute-done | bytes 393248 | tf_op jit(solution)/shard_map/ppermute | solution.py:287
  81.7 26.4 %all-gather.2 = s32[8,1,128]{2,1,0:T(1,128)} all-gather(s32[1,1,128]{2,1,0:T(1,128)} %bitcast.15), channel_id=1, replica_groups=mesh['seq'=16,'grp'=8,'store'=2] {'grp'}, dimensions={0}, use_global_device_ids=true | all-gather | bytes 4608 | tf_op jit(solution)/shard_map/all_gather | solution.py:347
  108.1 10.2 %recv_table.1.after.table = s32[640]{0:T(1024)} custom-call(s32[2]{0:T(128)} %pad_add_fusion.place, s32[8,128]{1,0:T(8,128)} %bitcast.14), custom_call_target="tpu_custom_call" | custom-call | bytes 1024 | tf_op jit(solution)/shard_map/recv_table/pallas_call | solution.py:336
  123.5 4.1 pack.3
  128.8 9.1 %collective-permute-done.5.refs_2_ = bf16[12,2,64,128]{3,2,1,0:T(8,128)(2,1)} collective-permute-done((bf16[12,2,64,128]{3,2,1,0:T(8,128)(2,1)}, bf16[12,2,64,128]{3,2,1,0:T(8,128)(2,1)}, u32[]{:S(2)}, u32[]{:S(2)}) %collective-permute-start.5) | collective-permute-done | bytes 393248 | tf_op jit(solution)/shard_map/ppermute | solution.py:287
  141.9 7.2 %collective-permute-done.15.refs_1_ = bf16[12,2,64,128]{3,2,1,0:T(8,128)(2,1)S(1)} collective-permute-done((bf16[12,2,64,128]{3,2,1,0:T(8,128)(2,1)}, bf16[12,2,64,128]{3,2,1,0:T(8,128)(2,1)S(1)}, u32[]{:S(2)}, u32[]{:S(2)}) %collective-permute-start.15) | collective-permute-done | bytes 393248 | tf_op jit(solution)/shard_map/ppermute | solution.py:287
  150.3 18.8 %collective-permute-done.16.refs_2_ = bf16[12,2,64,128]{3,2,1,0:T(8,128)(2,1)S(1)} collective-permute-done((bf16[12,2,64,128]{3,2,1,0:T(8,128)(2,1)}, bf16[12,2,64,128]{3,2,1,0:T(8,128)(2,1)S(1)}, u32[]{:S(2)}, u32[]{:S(2)}) %collective-permute-start.16) | collective-permute-done | bytes 393248 | tf_op jit(solution)/shard_map/ppermute | solution.py:287
  171.3 10.0 %stats.2 = f32[128,128]{1,0:T(8,128)} custom-call(s32[2]{0:T(128)} %pad_add_fusion.place, s32[640]{0:T(1024)} %recv_table.1.after.table, bf16[12,2,64,128]{3,2,1,0:T(8,128)(2,1)} %get-tuple-element.50.refs_0_, bf16[12,2,64,128]{3,2,1,0:T(8,128)(2,1)} %collective-permute-done.3.refs_3_.refs_1_, bf16[12,2,64,128]{3,2,1,0:T(8,128)(2,1)} %collective-permute-done.5.refs_2_, ...), custom_call_target="tpu_custom_call" | custom-call | flops 1024 | bytes 1024 | tf_op jit(solution)/shard_map/stats/pallas_call | solution.py:357
  181.3 47.6 %all-gather.given = f32[1024,128]{1,0:T(8,128)} all-gather(f32[128,128]{1,0:T(8,128)} %stats.2), channel_id=2, replica_groups=mesh['seq'=16,'grp'=8,'store'=2] {'grp'}, dimensions={0}, use_global_device_ids=true | all-gather | bytes 589824 | tf_op jit(solution)/shard_map/all_gather | solution.py:367
  228.9 24.3 %grads.2 = (bf16[12,2,64,128]{3,2,1,0:T(8,128)(2,1)}, bf16[12,2,64,128]{3,2,1,0:T(8,128)(2,1)}, bf16[12,2,64,128]{3,2,1,0:T(8,128)(2,1)}, bf16[12,2,64,128]{3,2,...) custom-call(s32[2]{0:T(128)} %pad_add_fusion.place, ...), custom_call_target="tpu_custom_call" | custom-call | flops 1024 | bytes 1024 | tf_op jit(solution)/shard_map/grads/pallas_call | solution.py:368
  263.2 10.0 %stats.3 = f32[128,128]{1,0:T(8,128)} custom-call(s32[2]{0:T(128)} %pad_add_fusion.place, s32[640]{0:T(1024)} %recv_table.1.after.table, bf16[12,2,64,128]{3,2,1,0:T(8,128)(2,1)} %get-tuple-element.63.refs_0_, bf16[12,2,64,128]{3,2,1,0:T(8,128)(2,1)} %copy-done.4, bf16[12,2,64,128]{3,2,1,0:T(8,128)(2,1)} %copy-done.5, bf16[12,2,64,128]{3,2,1,0:T(8,128)(2,1)} %copy-done.6, ...), custom_call_target="tpu_custom_call" | custom-call | flops 1024 | bytes 1024 | tf_op jit(solution)/shard_map/stats/pallas_call | solution.py:357
  273.1 68.9 %all-gather.1.given = f32[1024,128]{1,0:T(8,128)} all-gather(f32[128,128]{1,0:T(8,128)} %stats.3), channel_id=3, replica_groups=mesh['seq'=16,'grp'=8,'store'=2] {'grp'}, dimensions={0}, use_global_device_ids=true | all-gather | bytes 589824 | tf_op jit(solution)/shard_map/all_gather | solution.py:367
  342.1 24.4 %grads.3 = (bf16[12,2,64,128]{3,2,1,0:T(8,128)(2,1)}, bf16[12,2,64,128]{3,2,1,0:T(8,128)(2,1)}, bf16[12,2,64,128]{3,2,1,0:T(8,128)(2,1)}, bf16[12,2,64,128]{3,2,...) custom-call(s32[2]{0:T(128)} %pad_add_fusion.place, ...), custom_call_target="tpu_custom_call" | custom-call | flops 1024 | bytes 1024 | tf_op jit(solution)/shard_map/grads/pallas_call | solution.py:368
  374.7 5.1 %collective-permute-start.24 = (bf16[12,2,64,128]{3,2,1,0:T(8,128)(2,1)}, bf16[12,2,64,128]{3,2,1,0:T(8,128)(2,1)S(1)}, u32[]{:S(2)}, u32[]{:S(2)}) collective-permute-start(bf16[12,2,64,128]{3,2,1,0:T(8,128)(2,1)} %get-tuple-element.74), channel_id=1, source_target_pairs={{0,8},{2,10},{4,12},{6,14},{8,0},{10,2},{12,4},{14,6},{1,9},{3,11}... | collective-permute-start | bytes 1179656 | tf_op jit(solution)/shard_map/ppermute | solution.py:287
  379.7 9.4 %collective-permute-done.13.refs_6_ = bf16[12,2,64,128]{3,2,1,0:T(8,128)(2,1)S(1)} collective-permute-done((bf16[12,2,64,128]{3,2,1,0:T(8,128)(2,1)S(1)}, bf16[12,2,64,128]{3,2,1,0:T(8,128)(2,1)S(1)}, u32[]{:S(2)}, u32[]{:S(2)}) %collective-permute-start.13) | collective-permute-done | bytes 393248 | tf_op jit(solution)/shard_map/ppermute | solution.py:287
  389.2 14.9 %collective-permute-done.14.refs_7_ = bf16[12,2,64,128]{3,2,1,0:T(8,128)(2,1)S(1)} collective-permute-done((bf16[12,2,64,128]{3,2,1,0:T(8,128)(2,1)S(1)}, bf16[12,2,64,128]{3,2,1,0:T(8,128)(2,1)S(1)}, u32[]{:S(2)}, u32[]{:S(2)}) %collective-permute-start.14) | collective-permute-done | bytes 393248 | tf_op jit(solution)/shard_map/ppermute | solution.py:287
  404.0 22.6 %collective-permute-done.23.refs_9_.refs_5_ = bf16[12,2,64,128]{3,2,1,0:T(8,128)(2,1)S(1)} collective-permute-done((bf16[12,2,64,128]{3,2,1,0:T(8,128)(2,1)}, bf16[12,2,64,128]{3,2,1,0:T(8,128)(2,1)S(1)}, u32[]{:S(2)}, u32[]{:S(2)}) %collective-permute-start.23) | collective-permute-done | bytes 393248 | tf_op jit(solution)/shard_map/ppermute | solution.py:287
  427.5 3.9 unpack.2
  431.5 6.1 %all-to-all-start.2 = ((bf16[16,2,128,128]{3,2,1,0:T(8,128)(2,1)}), bf16[16,2,128,128]{3,2,1,0:T(8,128)(2,1)S(1)}, u32[]{:S(2)}, u32[]{:S(2)}) async-start(bf16[16,2,128,128]{3,2,1,0:T(8,128)(2,1)} %unpack.2), calls=%async_computation.2 | async-start | bytes 2097152 | tf_op jit(solution)/shard_map/all_to_all | solution.py:276
  437.5 4.4 collective-permute-start.26
  445.5 6.3 %collective-permute-done.26.refs_2_ = bf16[12,2,64,128]{3,2,1,0:T(8,128)(2,1)S(1)} collective-permute-done((bf16[12,2,64,128]{3,2,1,0:T(8,128)(2,1)}, bf16[12,2,64,128]{3,2,1,0:T(8,128)(2,1)S(1)}, u32[]{:S(2)}, u32[]{:S(2)}) %collective-permute-start.26) | collective-permute-done | bytes 393248 | tf_op jit(solution)/shard_map/ppermute | solution.py:287
  451.8 4.5 collective-permute-done.27.refs_6_
  456.3 4.2 collective-permute-done.28.refs_7_
  461.3 3.9 unpack.3
  465.2 7.2 %all-to-all-start.3 = ((bf16[16,2,128,128]{3,2,1,0:T(8,128)(2,1)}), bf16[16,2,128,128]{3,2,1,0:T(8,128)(2,1)S(1)}, u32[]{:S(2)}, u32[]{:S(2)}) async-start(bf16[16,2,128,128]{3,2,1,0:T(8,128)(2,1)} %unpack.3), calls=%async_computation.3 | async-start | bytes 2097152 | tf_op jit(solution)/shard_map/all_to_all | solution.py:276
  473.4 10.1 %join.1 = bf16[16,2,2,2,128,128]{5,4,3,2,1,0:T(8,128)(2,1)} custom-call(s32[2]{0:T(128)} %pad_add_fusion.place, bf16[16,2,128,128]{3,2,1,0:T(8,128)(2,1)} %get-tuple-element.71.refs_10_.keep0, bf16[16,2,128,128]{3,2,1,0:T(8,128)(2,1)} %get-tuple-element.80.keep1, bf16[16,2,128,128]{3,2,1,0:T(8,128)(2,1)} %collective-permute-done.29.got0, ...), custom_call_target="tpu_custom_call" | custom-call | bytes 1024 | tf_op jit(solution)/shard_map/join/pallas_call | solution.py:403
  (118 shorter events, 56.1 us)
Async XLA Ops:
  4.4 23.3 %all-to-all-start.1 = ((bf16[16,2,128,128]{3,2,1,0:T(8,128)(2,1)}), bf16[16,2,128,128]{3,2,1,0:T(8,128)(2,1)S(1)}, u32[]{:S(2)}, u32[]{:S(2)}) async-start(bf16[16,2,128,128]{3,2,1,0:T(8,128)(2,1)} %pad_maximum_fusion.1), calls=%async_computation.1 | async-start | bytes 2097152 | tf_op jit(solution)/shard_map/all_to_all | solution.py:276
  15.1 154.9 %collective-permute-start.7 = (bf16[16,2,2,128,128]{4,3,2,1,0:T(8,128)(2,1)}, bf16[16,2,2,128,128]{4,3,2,1,0:T(8,128)(2,1)S(1)}, u32[]{:S(2)}, u32[]{:S(2)}) collective-permute-start(bf16[16,2,2,128,128]{4,3,2,1,0:T(8,128)(2,1)} %dynamic-slice_bitcast_fusion), channel_id=1, source_target_pairs={{0,1},{1,0},{2,3},{3,2},{4,5},{5,4},{6,7},{7,6},{8,9},{9,8},{10,11... | collective-permute-start | bytes 6291464 | tf_op jit(solution)/shard_map/ppermute | solution.py:308
  28.7 93.8 %all-to-all-start = ((bf16[16,2,128,128]{3,2,1,0:T(8,128)(2,1)}), bf16[16,2,128,128]{3,2,1,0:T(8,128)(2,1)S(1)}, u32[]{:S(2)}, u32[]{:S(2)}) async-start(bf16[16,2,128,128]{3,2,1,0:T(8,128)(2,1)} %pad_maximum_fusion), calls=%async_computation | async-start | bytes 2097152 | tf_op jit(solution)/shard_map/all_to_all | solution.py:276
  39.4 42.2 %collective-permute-start = (bf16[12,2,64,128]{3,2,1,0:T(8,128)(2,1)}, bf16[12,2,64,128]{3,2,1,0:T(8,128)(2,1)S(1)}, u32[]{:S(2)}, u32[]{:S(2)}) collective-permute-start(bf16[12,2,64,128]{3,2,1,0:T(8,128)(2,1)} %get-tuple-element.43), channel_id=1, source_target_pairs={{0,6},{2,8},{4,10},{6,12},{8,14},{10,0},{12,2},{14,4},{1,7},{3,9},... | collective-permute-start | bytes 1179656 | tf_op jit(solution)/shard_map/ppermute | solution.py:287
  44.1 74.2 %collective-permute-start.1 = (bf16[12,2,64,128]{3,2,1,0:T(8,128)(2,1)}, bf16[12,2,64,128]{3,2,1,0:T(8,128)(2,1)}, u32[]{:S(2)}, u32[]{:S(2)}) collective-permute-start(bf16[12,2,64,128]{3,2,1,0:T(8,128)(2,1)} %get-tuple-element.44), channel_id=1, source_target_pairs={{0,10},{2,12},{4,14},{6,0},{8,2},{10,4},{12,6},{14,8},{1,11},{3,13... | collective-permute-start | bytes 1179656 | tf_op jit(solution)/shard_map/ppermute | solution.py:287
  46.4 73.5 %collective-permute-start.2 = (bf16[12,2,64,128]{3,2,1,0:T(8,128)(2,1)}, bf16[12,2,64,128]{3,2,1,0:T(8,128)(2,1)}, u32[]{:S(2)}, u32[]{:S(2)}) collective-permute-start(bf16[12,2,64,128]{3,2,1,0:T(8,128)(2,1)} %get-tuple-element.45), channel_id=1, source_target_pairs={{0,8},{2,10},{4,12},{6,14},{8,0},{10,2},{12,4},{14,6},{1,9},{3,11}... | collective-permute-start | bytes 1179656 | tf_op jit(solution)/shard_map/ppermute | solution.py:287
  51.7 70.8 %collective-permute-start.3 = (bf16[12,2,64,128]{3,2,1,0:T(8,128)(2,1)}, bf16[12,2,64,128]{3,2,1,0:T(8,128)(2,1)}, u32[]{:S(2)}, u32[]{:S(2)}) collective-permute-start(bf16[12,2,64,128]{3,2,1,0:T(8,128)(2,1)} %get-tuple-element.46), channel_id=1, source_target_pairs={{0,2},{2,4},{4,6},{6,8},{8,10},{10,12},{12,14},{14,0},{1,3},{3,5},... | collective-permute-start | bytes 1179656 | tf_op jit(solution)/shard_map/ppermute | solution.py:287
  81.7 40.9 %collective-permute-start.4 = (bf16[12,2,64,128]{3,2,1,0:T(8,128)(2,1)}, bf16[12,2,64,128]{3,2,1,0:T(8,128)(2,1)}, u32[]{:S(2)}, u32[]{:S(2)}) collective-permute-start(bf16[12,2,64,128]{3,2,1,0:T(8,128)(2,1)} %get-tuple-element.47), channel_id=1, source_target_pairs={{0,14},{2,0},{4,2},{6,4},{8,6},{10,8},{12,10},{14,12},{1,15},{3,1}... | collective-permute-start | bytes 1179656 | tf_op jit(solution)/shard_map/ppermute | solution.py:287
  118.3 19.5 %collective-permute-start.5 = (bf16[12,2,64,128]{3,2,1,0:T(8,128)(2,1)}, bf16[12,2,64,128]{3,2,1,0:T(8,128)(2,1)}, u32[]{:S(2)}, u32[]{:S(2)}) collective-permute-start(bf16[12,2,64,128]{3,2,1,0:T(8,128)(2,1)} %get-tuple-element.53), channel_id=1, source_target_pairs={{0,4},{2,6},{4,8},{6,10},{8,12},{10,14},{12,0},{14,2},{1,5},{3,7},... | collective-permute-start | bytes 1179656 | tf_op jit(solution)/shard_map/ppermute | solution.py:287
  119.9 18.9 %collective-permute-start.6 = (bf16[12,2,64,128]{3,2,1,0:T(8,128)(2,1)}, bf16[12,2,64,128]{3,2,1,0:T(8,128)(2,1)}, u32[]{:S(2)}, u32[]{:S(2)}) collective-permute-start(bf16[12,2,64,128]{3,2,1,0:T(8,128)(2,1)} %get-tuple-element.54), channel_id=1, source_target_pairs={{0,12},{2,14},{4,0},{6,2},{8,4},{10,6},{12,8},{14,10},{1,13},{3,15... | collective-permute-start | bytes 1179656 | tf_op jit(solution)/shard_map/ppermute | solution.py:287
  127.6 21.5 %collective-permute-start.15 = (bf16[12,2,64,128]{3,2,1,0:T(8,128)(2,1)}, bf16[12,2,64,128]{3,2,1,0:T(8,128)(2,1)S(1)}, u32[]{:S(2)}, u32[]{:S(2)}) collective-permute-start(bf16[12,2,64,128]{3,2,1,0:T(8,128)(2,1)} %get-tuple-element.64), channel_id=1, source_target_pairs={{0,2},{2,4},{4,6},{6,8},{8,10},{10,12},{12,14},{14,0},{1,3},{3,5},... | collective-permute-start | bytes 1179656 | tf_op jit(solution)/shard_map/ppermute | solution.py:287
  128.7 40.5 %collective-permute-start.16 = (bf16[12,2,64,128]{3,2,1,0:T(8,128)(2,1)}, bf16[12,2,64,128]{3,2,1,0:T(8,128)(2,1)S(1)}, u32[]{:S(2)}, u32[]{:S(2)}) collective-permute-start(bf16[12,2,64,128]{3,2,1,0:T(8,128)(2,1)} %get-tuple-element.65), channel_id=1, source_target_pairs={{0,4},{2,6},{4,8},{6,10},{8,12},{10,14},{12,0},{14,2},{1,5},{3,7},... | collective-permute-start | bytes 1179656 | tf_op jit(solution)/shard_map/ppermute | solution.py:287
  137.9 115.3 %collective-permute-start.17 = (bf16[12,2,64,128]{3,2,1,0:T(8,128)(2,1)}, bf16[12,2,64,128]{3,2,1,0:T(8,128)(2,1)S(1)}, u32[]{:S(2)}, u32[]{:S(2)}) collective-permute-start(bf16[12,2,64,128]{3,2,1,0:T(8,128)(2,1)} %get-tuple-element.66), channel_id=1, source_target_pairs={{0,6},{2,8},{4,10},{6,12},{8,14},{10,0},{12,2},{14,4},{1,7},{3,9},... | collective-permute-start | bytes 1179656 | tf_op jit(solution)/shard_map/ppermute | solution.py:287
  138.7 118.1 %collective-permute-start.18 = (bf16[12,2,64,128]{3,2,1,0:T(8,128)(2,1)}, bf16[12,2,64,128]{3,2,1,0:T(8,128)(2,1)S(1)}, u32[]{:S(2)}, u32[]{:S(2)}) collective-permute-start(bf16[12,2,64,128]{3,2,1,0:T(8,128)(2,1)} %get-tuple-element.67), channel_id=1, source_target_pairs={{0,8},{2,10},{4,12},{6,14},{8,0},{10,2},{12,4},{14,6},{1,9},{3,11}... | collective-permute-start | bytes 1179656 | tf_op jit(solution)/shard_map/ppermute | solution.py:287
  149.1 107.7 %collective-permute-start.19 = (bf16[12,2,64,128]{3,2,1,0:T(8,128)(2,1)}, bf16[12,2,64,128]{3,2,1,0:T(8,128)(2,1)}, u32[]{:S(2)}, u32[]{:S(2)}) collective-permute-start(bf16[12,2,64,128]{3,2,1,0:T(8,128)(2,1)} %get-tuple-element.68), channel_id=1, source_target_pairs={{0,10},{2,12},{4,14},{6,0},{8,2},{10,4},{12,6},{14,8},{1,11},{3,13... | collective-permute-start | bytes 1179656 | tf_op jit(solution)/shard_map/ppermute | solution.py:287
  169.2 90.6 %collective-permute-start.20 = (bf16[12,2,64,128]{3,2,1,0:T(8,128)(2,1)}, bf16[12,2,64,128]{3,2,1,0:T(8,128)(2,1)}, u32[]{:S(2)}, u32[]{:S(2)}) collective-permute-start(bf16[12,2,64,128]{3,2,1,0:T(8,128)(2,1)} %get-tuple-element.69), channel_id=1, source_target_pairs={{0,12},{2,14},{4,0},{6,2},{8,4},{10,6},{12,8},{14,10},{1,13},{3,15... | collective-permute-start | bytes 1179656 | tf_op jit(solution)/shard_map/ppermute | solution.py:287
  170.0 92.9 %collective-permute-start.21 = (bf16[12,2,64,128]{3,2,1,0:T(8,128)(2,1)}, bf16[12,2,64,128]{3,2,1,0:T(8,128)(2,1)}, u32[]{:S(2)}, u32[]{:S(2)}) collective-permute-start(bf16[12,2,64,128]{3,2,1,0:T(8,128)(2,1)} %get-tuple-element.70), channel_id=1, source_target_pairs={{0,14},{2,0},{4,2},{6,4},{8,6},{10,8},{12,10},{14,12},{1,15},{3,1}... | collective-permute-start | bytes 1179656 | tf_op jit(solution)/shard_map/ppermute | solution.py:287
  253.2 113.3 %collective-permute-start.8 = (bf16[12,2,64,128]{3,2,1,0:T(8,128)(2,1)}, bf16[12,2,64,128]{3,2,1,0:T(8,128)(2,1)S(1)}, u32[]{:S(2)}, u32[]{:S(2)}) collective-permute-start(bf16[12,2,64,128]{3,2,1,0:T(8,128)(2,1)} %get-tuple-element.56), channel_id=1, source_target_pairs={{0,14},{2,0},{4,2},{6,4},{8,6},{10,8},{12,10},{14,12},{1,15},{3,1}... | collective-permute-start | bytes 1179656 | tf_op jit(solution)/shard_map/ppermute | solution.py:287
  256.8 111.1 %collective-permute-start.9 = (bf16[12,2,64,128]{3,2,1,0:T(8,128)(2,1)}, bf16[12,2,64,128]{3,2,1,0:T(8,128)(2,1)S(1)}, u32[]{:S(2)}, u32[]{:S(2)}) collective-permute-start(bf16[12,2,64,128]{3,2,1,0:T(8,128)(2,1)} %get-tuple-element.57), channel_id=1, source_target_pairs={{0,12},{2,14},{4,0},{6,2},{8,4},{10,6},{12,8},{14,10},{1,13},{3,15... | collective-permute-start | bytes 1179656 | tf_op jit(solution)/shard_map/ppermute | solution.py:287
  256.9 113.2 %collective-permute-start.10 = (bf16[12,2,64,128]{3,2,1,0:T(8,128)(2,1)}, bf16[12,2,64,128]{3,2,1,0:T(8,128)(2,1)S(1)}, u32[]{:S(2)}, u32[]{:S(2)}) collective-permute-start(bf16[12,2,64,128]{3,2,1,0:T(8,128)(2,1)} %get-tuple-element.58), channel_id=1, source_target_pairs={{0,10},{2,12},{4,14},{6,0},{8,2},{10,4},{12,6},{14,8},{1,11},{3,13... | collective-permute-start | bytes 1179656 | tf_op jit(solution)/shard_map/ppermute | solution.py:287
  259.8 114.0 %collective-permute-start.11 = (bf16[12,2,64,128]{3,2,1,0:T(8,128)(2,1)}, bf16[12,2,64,128]{3,2,1,0:T(8,128)(2,1)S(1)}, u32[]{:S(2)}, u32[]{:S(2)}) collective-permute-start(bf16[12,2,64,128]{3,2,1,0:T(8,128)(2,1)} %get-tuple-element.59), channel_id=1, source_target_pairs={{0,8},{2,10},{4,12},{6,14},{8,0},{10,2},{12,4},{14,6},{1,9},{3,11}... | collective-permute-start | bytes 1179656 | tf_op jit(solution)/shard_map/ppermute | solution.py:287
  262.9 111.8 %collective-permute-start.12 = (bf16[12,2,64,128]{3,2,1,0:T(8,128)(2,1)}, bf16[12,2,64,128]{3,2,1,0:T(8,128)(2,1)}, u32[]{:S(2)}, u32[]{:S(2)}) collective-permute-start(bf16[12,2,64,128]{3,2,1,0:T(8,128)(2,1)} %get-tuple-element.60), channel_id=1, source_target_pairs={{0,6},{2,8},{4,10},{6,12},{8,14},{10,0},{12,2},{14,4},{1,7},{3,9},... | collective-permute-start | bytes 1179656 | tf_op jit(solution)/shard_map/ppermute | solution.py:287
  366.5 22.6 %collective-permute-start.13 = (bf16[12,2,64,128]{3,2,1,0:T(8,128)(2,1)S(1)}, bf16[12,2,64,128]{3,2,1,0:T(8,128)(2,1)S(1)}, u32[]{:S(2)}, u32[]{:S(2)}) collective-permute-start(bf16[12,2,64,128]{3,2,1,0:T(8,128)(2,1)S(1)} %copy-done.25), channel_id=1, source_target_pairs={{0,4},{2,6},{4,8},{6,10},{8,12},{10,14},{12,0},{14,2},{1,5},{3,7},... | collective-permute-start | bytes 1179656 | tf_op jit(solution)/shard_map/ppermute | solution.py:287
  367.9 36.1 %collective-permute-start.14 = (bf16[12,2,64,128]{3,2,1,0:T(8,128)(2,1)S(1)}, bf16[12,2,64,128]{3,2,1,0:T(8,128)(2,1)S(1)}, u32[]{:S(2)}, u32[]{:S(2)}) collective-permute-start(bf16[12,2,64,128]{3,2,1,0:T(8,128)(2,1)S(1)} %copy-done.24), channel_id=1, source_target_pairs={{0,2},{2,4},{4,6},{6,8},{8,10},{10,12},{12,14},{14,0},{1,3},{3,5},... | collective-permute-start | bytes 1179656 | tf_op jit(solution)/shard_map/ppermute | solution.py:287
  370.1 33.9 %collective-permute-start.22 = (bf16[12,2,64,128]{3,2,1,0:T(8,128)(2,1)}, bf16[12,2,64,128]{3,2,1,0:T(8,128)(2,1)S(1)}, u32[]{:S(2)}, u32[]{:S(2)}) collective-permute-start(bf16[12,2,64,128]{3,2,1,0:T(8,128)(2,1)} %get-tuple-element.72), channel_id=1, source_target_pairs={{0,10},{2,12},{4,14},{6,0},{8,2},{10,4},{12,6},{14,8},{1,11},{3,13... | collective-permute-start | bytes 1179656 | tf_op jit(solution)/shard_map/ppermute | solution.py:287
  374.6 52.1 %collective-permute-start.23 = (bf16[12,2,64,128]{3,2,1,0:T(8,128)(2,1)}, bf16[12,2,64,128]{3,2,1,0:T(8,128)(2,1)S(1)}, u32[]{:S(2)}, u32[]{:S(2)}) collective-permute-start(bf16[12,2,64,128]{3,2,1,0:T(8,128)(2,1)} %get-tuple-element.73), channel_id=1, source_target_pairs={{0,6},{2,8},{4,10},{6,12},{8,14},{10,0},{12,2},{14,4},{1,7},{3,9},... | collective-permute-start | bytes 1179656 | tf_op jit(solution)/shard_map/ppermute | solution.py:287
  374.7 52.0 %collective-permute-start.24 = (bf16[12,2,64,128]{3,2,1,0:T(8,128)(2,1)}, bf16[12,2,64,128]{3,2,1,0:T(8,128)(2,1)S(1)}, u32[]{:S(2)}, u32[]{:S(2)}) collective-permute-start(bf16[12,2,64,128]{3,2,1,0:T(8,128)(2,1)} %get-tuple-element.74), channel_id=1, source_target_pairs={{0,8},{2,10},{4,12},{6,14},{8,0},{10,2},{12,4},{14,6},{1,9},{3,11}... | collective-permute-start | bytes 1179656 | tf_op jit(solution)/shard_map/ppermute | solution.py:287
  431.5 33.7 %all-to-all-start.2 = ((bf16[16,2,128,128]{3,2,1,0:T(8,128)(2,1)}), bf16[16,2,128,128]{3,2,1,0:T(8,128)(2,1)S(1)}, u32[]{:S(2)}, u32[]{:S(2)}) async-start(bf16[16,2,128,128]{3,2,1,0:T(8,128)(2,1)} %unpack.2), calls=%async_computation.2 | async-start | bytes 2097152 | tf_op jit(solution)/shard_map/all_to_all | solution.py:276
  441.9 18.6 %collective-permute-start.28 = (bf16[12,2,64,128]{3,2,1,0:T(8,128)(2,1)}, bf16[12,2,64,128]{3,2,1,0:T(8,128)(2,1)S(1)}, u32[]{:S(2)}, u32[]{:S(2)}) collective-permute-start(bf16[12,2,64,128]{3,2,1,0:T(8,128)(2,1)} %get-tuple-element.79), channel_id=1, source_target_pairs={{0,2},{2,4},{4,6},{6,8},{8,10},{10,12},{12,14},{14,0},{1,3},{3,5},... | collective-permute-start | bytes 1179656 | tf_op jit(solution)/shard_map/ppermute | solution.py:287
  443.9 28.5 %collective-permute-start.30 = (bf16[16,2,128,128]{3,2,1,0:T(8,128)(2,1)}, bf16[16,2,128,128]{3,2,1,0:T(8,128)(2,1)S(1)}, u32[]{:S(2)}, u32[]{:S(2)}) collective-permute-start(bf16[16,2,128,128]{3,2,1,0:T(8,128)(2,1)} %get-tuple-element.82), channel_id=1, source_target_pairs={{0,1},{1,0},{2,3},{3,2},{4,5},{5,4},{6,7},{7,6},{8,9},{9,8},{10,11... | collective-permute-start | bytes 3145736 | tf_op jit(solution)/shard_map/ppermute | solution.py:382
  445.5 26.9 %collective-permute-start.29 = (bf16[16,2,128,128]{3,2,1,0:T(8,128)(2,1)}, bf16[16,2,128,128]{3,2,1,0:T(8,128)(2,1)}, u32[]{:S(2)}, u32[]{:S(2)}) collective-permute-start(bf16[16,2,128,128]{3,2,1,0:T(8,128)(2,1)} %get-tuple-element.81), channel_id=1, source_target_pairs={{0,1},{1,0},{2,3},{3,2},{4,5},{5,4},{6,7},{7,6},{8,9},{9,8},{10,11... | collective-permute-start | bytes 3145736 | tf_op jit(solution)/shard_map/ppermute | solution.py:382
  465.2 19.2 %all-to-all-start.3 = ((bf16[16,2,128,128]{3,2,1,0:T(8,128)(2,1)}), bf16[16,2,128,128]{3,2,1,0:T(8,128)(2,1)S(1)}, u32[]{:S(2)}, u32[]{:S(2)}) async-start(bf16[16,2,128,128]{3,2,1,0:T(8,128)(2,1)} %unpack.3), calls=%async_computation.3 | async-start | bytes 2097152 | tf_op jit(solution)/shard_map/all_to_all | solution.py:276
  (29 other events, 669.3 us)

commit v4 on v3

--- a/solution.py
+++ b/solution.py
@@ -29,7 +29,7 @@
 VMEM = pl.BlockSpec(memory_space=pltpu.VMEM)
 ANY = pl.BlockSpec(memory_space=pltpu.HBM)
 
-STAT_ROWS = RING * 16
+STAT_ROWS = ROWS
 R_STAT, R_BLK, R_PAIR, R_COUNT, R_SIZE = 128, 256, 384, 512, 640
 
 
@@ -46,7 +46,7 @@
             own = names[source, i]
             slot = (own & 1) * CAP + count[own]
             count[own] = count[own] + 1
-            where[source * INST + i] = (own >> 1) * STAT_ROWS + source * 16 + slot
+            where[source * INST + i] = (own >> 1) * STAT_ROWS + source * SLOTS + slot
             return carry
 
         return lax.fori_loop(0, INST, step, carry, unroll=8)
@@ -57,8 +57,9 @@
         def step(i, total):
             own = names[source, i]
             at = where[source * INST + i]
-            table[total] = ((place[0] - source) & (RING - 1)) * SLOTS + (at & 15)
-            table[R_STAT + total] = at & (STAT_ROWS - 1)
+            local = at - (own >> 1) * STAT_ROWS
+            table[total] = local + (((place[0] - source) & (RING - 1)) - source) * SLOTS
+            table[R_STAT + total] = local
             table[R_BLK + total] = (own & 1) * BLK + names[source, INST + i]
             table[R_PAIR + total] = where[source * INST + (i ^ 1)]
             return total + ((own >> 1) == place[0]).astype(jnp.int32)
@@ -80,16 +81,17 @@
 
 def part_copies(stage, parts, sems, load):
     copies = []
-    for d in range(RING):
+    for n in range(RING):
+        d = ORDER[n] if load else n
         rows = stage.at[pl.ds(d * SLOTS, SLOTS)]
-        ends = (parts[d], rows) if load else (rows, parts[d])
-        copies.append(pltpu.make_async_copy(*ends, sems.at[d]))
+        ends = (parts[n], rows) if load else (rows, parts[n])
+        copies.append(pltpu.make_async_copy(*ends, sems.at[n]))
         copies[-1].start()
     return copies
 
 
 def pack_kernel(place, names, rows, *refs):
-    outs, (table, sent, stage, count, sems) = refs[-RING - 5 : -5], refs[-5:]
+    outs, (table, stage, count, sems) = refs[-RING - 4 : -4], refs[-4:]
     for o in range(RING * 2):
         count[o] = 0
 
@@ -103,8 +105,6 @@
         start = pl.multiple_of((span & 1) * SPAN, SPAN)
         for kind in range(2):
             stage[row, kind] = rows[span >> 1, kind, pl.ds(start, SPAN), :]
-        sent[0, i] = own
-        sent[0, INST + i] = names[INST + i]
         return carry
 
     lax.fori_loop(0, INST, step, 0, unroll=4)
@@ -112,7 +112,7 @@
         copy.wait()
 
 
-def gate_kernel(after, *refs):
+def gate_kernel(*refs):
     pass
 
 
@@ -166,13 +166,14 @@
         return carry
 
     lax.fori_loop(0, (table[R_COUNT] + UNROLL - 1) // UNROLL, step, 0)
-    out[...] = stats[:STAT_ROWS]
+    for chip in range(RING):
+        out[pl.ds(chip * STAT_ROWS, STAT_ROWS), :] = stats[:STAT_ROWS]
 
 
 def grad_kernel(pair, place, table, given, *refs):
     parts, own, other = refs[:RING], refs[RING], refs[RING + 1]
-    outs = refs[RING + 2 : 2 * RING + 2]
-    keep, send, stage, store, result, mine, theirs, stats, total, sems = refs[2 * RING + 2 :]
+    outs = refs[-RING - 10 : -10]
+    keep, send, stage, store, result, mine, theirs, stats, total, sems = refs[-10:]
     copies = load_all(pair, place, parts, own, other, stage, store, sems)
     base = place[0] * STAT_ROWS
 
@@ -270,34 +271,39 @@
 
 
 EARLY, LATE = (3, 5, 4, 1, 7), (2, 6)
-
-
-def exchange(rows):
-    return lax.all_to_all(rows, "seq", split_axis=0, concat_axis=0, tiled=True)
-
-
-def ring_send(parts, sign, gated=(), after=None):
+ORDER = (0, 4, 3, 5, 2, 6, 1, 7)
+
+
+def exchange(rows, axis):
+    return lax.all_to_all(rows, axis, split_axis=0, concat_axis=0, tiled=True)
+
+
+def ring_send(parts, sign, gated=(), after=()):
     parts = list(parts)
     if gated:
         for d, part in zip(gated, gate([parts[d] for d in gated], after)):
             parts[d] = part
-    got = [parts[0]]
-    for d in range(1, RING):
+    got = list(parts)
+    for d in sorted(range(1, RING), key=ORDER.index):
         pairs = [(i, (i + sign * d) % RING) for i in range(RING)]
-        got.append(lax.ppermute(parts[d], "grp", pairs))
+        got[d] = lax.ppermute(parts[d], "grp", pairs)
     return got
+
+
+def ordered(parts):
+    return [parts[d] for d in ORDER]
 
 
 def gate(parts, after):
     return pl.pallas_call(
         gate_kernel,
         out_shape=[shape(part.shape, part.dtype) for part in parts],
-        in_specs=[ANY] * (len(parts) + 1),
+        in_specs=[ANY] * (len(parts) + len(after)),
         out_specs=[ANY] * len(parts),
-        input_output_aliases={n + 1: n for n in range(len(parts))},
+        input_output_aliases={n + len(after): n for n in range(len(parts))},
         cost_estimate=cost(0, COST),
         name="gate",
-    )(after, *parts)
+    )(*after, *parts)
 
 
 def on_device(query, kv_store, nbr_owner, nbr_block, d_out):
@@ -312,16 +318,19 @@
     grad_rows = d_out.reshape(SEQ, 2, 128, DH)
 
     arrived = []
-    after = []
+    all_names = lax.all_gather(names.reshape(1, 2 * INST), "grp", tiled=True)
+    after = [kv_other, all_names]
     for pair in range(2):
         rows = jnp.stack([query_rows[:, pair], grad_rows[:, pair]], axis=1)
-        rows = exchange(rows)
+        if pair == 1:
+            (rows,) = gate([rows], [recv_table] + after)
+        rows = exchange(rows, "seq")
         outs = pl.pallas_call(
             pack_kernel,
             out_shape=[shape(PART)] * RING
-            + [shape((INST,), jnp.int32), shape((1, 2 * INST), jnp.int32)],
+            + [shape((INST,), jnp.int32)],
             in_specs=[SMEM, SMEM, VMEM] + [ANY] * len(after),
-            out_specs=[ANY] * RING + [SMEM, SMEM],
+            out_specs=[ANY] * RING + [SMEM],
             scratch_shapes=[
                 pltpu.VMEM((ROWS, 2, SPAN, DH), BF16),
                 pltpu.SMEM((2 * RING,), jnp.int32),
@@ -331,7 +340,7 @@
             cost_estimate=cost(0, COST),
             name="pack",
         )(place, names, rows, *after)
-        send_table, sent = outs[RING:]
+        send_table = outs[RING]
         if pair == 0:
             recv_table = pl.pallas_call(
                 recv_table_kernel,
@@ -344,27 +353,31 @@
                 ],
                 cost_estimate=cost(0, COST),
                 name="recv_table",
-            )(place, lax.all_gather(sent, "grp", tiled=True))
-            arrived.append(ring_send(outs[:RING], 1, LATE, recv_table))
+            )(place, all_names)
+            arrived.append(ring_send(outs[:RING], 1, LATE, [recv_table]))
             after = [arrived[0][d] for d in EARLY]
-        else:
-            arrived.append(ring_send(outs[:RING], 1))
-
-    partial = []
+    bulk = outs[:RING]
+
+    after = [send_table]
     kv_grads = []
-    after = []
+    returned = []
     for pair in range(2):
         stats = pl.pallas_call(
             functools.partial(stat_kernel, pair),
-            out_shape=shape((STAT_ROWS, DH), F32),
+            out_shape=shape((RING * STAT_ROWS, DH), F32),
             in_specs=[SMEM, SMEM] + [ANY] * (RING + 2 + len(after)),
             out_specs=VMEM,
             scratch_shapes=[STAGE, STORE, pltpu.VMEM((STAT_ROWS + 8, DH), F32), SEMS],
             compiler_params=PARAMS,
             cost_estimate=cost(COST, COST),
             name="stats",
-        )(place, recv_table, *arrived[pair], kv_store, kv_other, *after)
-        given = lax.all_gather(stats, "grp").reshape(RING * STAT_ROWS, DH)
+        )(place, recv_table, *ordered(arrived[pair]), kv_store, kv_other, *after)
+        given = exchange(stats, "grp")
+        moved = ring_send(bulk, 1 - 2 * pair, range(1, RING), [stats])
+        if pair == 0:
+            arrived.append(moved)
+        else:
+            returned.append(moved)
         outs = pl.pallas_call(
             functools.partial(grad_kernel, pair),
             out_shape=[shape(PART)] * RING + [shape((BLK, 2, 128, DH))] * 2,
@@ -376,19 +389,18 @@
             compiler_params=PARAMS,
             cost_estimate=cost(COST, COST),
             name="grads",
-        )(place, recv_table, given, *arrived[pair], kv_store, kv_other)
-        partial.append(outs[:RING])
+        )(place, recv_table, given, *ordered(arrived[pair]), kv_store, kv_other)
+        bulk = outs[:RING]
         after = [outs[RING]]
         kv_grads.append((outs[RING], lax.ppermute(outs[RING + 1], "store", swap)))
-
-    returned = [ring_send(partial[pair], -1) for pair in range(2)]
+    returned.append(ring_send(bulk, -1))
+
     results = []
     for pair in range(2):
-        after = [returned[1][d] for d in (3, 5, 4)] if pair == 0 else []
         rows = pl.pallas_call(
             unpack_kernel,
             out_shape=shape((SEQ, 2, 128, DH)),
-            in_specs=[SMEM] + [ANY] * (RING + len(after)),
+            in_specs=[SMEM] + [ANY] * (RING + 1),
             out_specs=VMEM,
             scratch_shapes=[
                 pltpu.VMEM((ROWS, 2, SPAN, DH), BF16),
@@ -397,8 +409,8 @@
             compiler_params=PARAMS,
             cost_estimate=cost(0, COST),
             name="unpack",
-        )(send_table, *returned[pair], *after)
-        results.append(exchange(rows))
+        )(send_table, *ordered(returned[pair]), kv_grads[1][0])
+        results.append(exchange(rows, "seq"))
 
     d_kv = pl.pallas_call(
         join_kernel,

time: 492 us -> 425 us (0.86)
  blocking collectives: 143 us -> 19.6 us
  starting transfers between devices: 79.6 us -> 110 us
  waiting for transfers between devices: 138 us -> 159 us
  Pallas kernels: 105 us -> 110 us
    all_gather x3 -> x1, blocking collectives: 143 us -> 19.6 us  [on_device(): all_names = lax.all_gather(names.reshape(1, 2 * INST), 'grp', tiled=True)]
    all_to_all x4 -> x6, starting transfers between devices: 26.2 us -> 43 us  [exchange(): return lax.all_to_all(rows, axis, split_axis=0, concat_axis=0, tiled=True)]
    all_to_all x4 -> x6, waiting for transfers between devices: 10.6 us -> 25.8 us  [exchange(): return lax.all_to_all(rows, axis, split_axis=0, concat_axis=0, tiled=True)]
    ppermute x28, starting transfers between devices: 53.4 us -> 66.9 us  [ring_send(): got[d] = lax.ppermute(parts[d], 'grp', pairs)]
    ppermute x28, waiting for transfers between devices: 128 us -> 133 us  [ring_send(): got[d] = lax.ppermute(parts[d], 'grp', pairs)]
  transfers between devices with their start and end apart: 35 -> 37, of which waited for: 13 -> 20; matrix products, arithmetic and copies ran while one was open for 1% -> 1% of each run, Pallas kernels for 21% -> 19%
where the time goes in v4:
time: 425 us; the launch traced here: 420 us
  waiting for transfers between devices  159 us (37%)
  starting transfers between devices  110 us (26%)
  Pallas kernels  110 us (26%)
  blocking collectives  19.6 us (5%)
  local copies, waits for them, and re-layouts  13.6 us (3%)
  other arithmetic  6.79 us (2%)
    ppermute x28, waiting for transfers between devices, ring_send(): got[d] = lax.ppermute(parts[d], 'grp', pairs)  133 us
    ppermute x28, starting transfers between devices, ring_send(): got[d] = lax.ppermute(parts[d], 'grp', pairs)  66.9 us
    pallas_call x2, Pallas kernels, on_device(): pl.pallas_call(functools.partial(grad_kernel, pair), out_shape=[shape(PAR...  52.7 us
    all_to_all x6, starting transfers between devices, exchange(): return lax.all_to_all(rows, axis, split_axis=0, concat_axis=0, tiled=True)  43 us
    all_to_all x6, waiting for transfers between devices, exchange(): return lax.all_to_all(rows, axis, split_axis=0, concat_axis=0, tiled=True)  25.8 us
    pallas_call x2, Pallas kernels, on_device(): pl.pallas_call(functools.partial(stat_kernel, pair), out_shape=shape((RIN...  21.6 us
    all_gather x1, blocking collectives, on_device(): all_names = lax.all_gather(names.reshape(1, 2 * INST), 'grp', tiled=True)  19.6 us
    pallas_call x1, Pallas kernels, on_device(): pl.pallas_call(join_kernel, out_shape=shape(kv_store.shape), grid=(BLK,),...  10.1 us
  transfers between devices with their start and end apart: 37, of which 20 were waited for; matrix products, arithmetic and copies ran while one was open for 1% of the time, Pallas kernels for 19%

profile of v4, /device:TPU:2, one launch (start us, length us, event | category | flops | bytes accessed | tf_op | source)
XLA Modules:
  0.0 420.0 jit_solution(10818037877509773359)
XLA Ops:
  6.2 7.5 %all-to-all-start = ((bf16[16,2,128,128]{3,2,1,0:T(8,128)(2,1)}), bf16[16,2,128,128]{3,2,1,0:T(8,128)(2,1)S(1)}, u32[]{:S(2)}, u32[]{:S(2)}) async-start(bf16[16,2,128,128]{3,2,1,0:T(8,128)(2,1)} %pad_maximum_fusion), calls=%async_computation | async-start | bytes 2097152 | tf_op jit(solution)/shard_map/all_to_all | solution.py:278
  14.2 19.6 %all-gather.1 = s32[8,1,128]{2,1,0:T(1,128)} all-gather(s32[1,1,128]{2,1,0:T(1,128)S(1)} %fusion.4), channel_id=2, replica_groups=mesh['seq'=16,'grp'=8,'store'=2] {'grp'}, dimensions={0}, use_global_device_ids=true | all-gather | bytes 4608 | tf_op jit(solution)/shard_map/all_gather | solution.py:321
  36.7 4.1 pack.2
  41.2 4.7 %collective-permute-start.2 = (bf16[12,2,64,128]{3,2,1,0:T(8,128)(2,1)}, bf16[12,2,64,128]{3,2,1,0:T(8,128)(2,1)S(1)}, u32[]{:S(2)}, u32[]{:S(2)}) collective-permute-start(bf16[12,2,64,128]{3,2,1,0:T(8,128)(2,1)} %get-tuple-element.57), channel_id=1, source_target_pairs={{0,10},{2,12},{4,14},{6,0},{8,2},{10,4},{12,6},{14,8},{1,11},{3,13... | collective-permute-start | bytes 1179656 | tf_op jit(solution)/shard_map/ppermute | solution.py:289
  51.4 10.0 %recv_table.1.refs_0_.table = s32[640]{0:T(1024)} custom-call(s32[2]{0:T(128)} %pad_add_fusion.place, s32[8,128]{1,0:T(8,128)} %bitcast.24), custom_call_target="tpu_custom_call" | custom-call | bytes 1024 | tf_op jit(solution)/shard_map/recv_table/pallas_call | solution.py:345
  63.7 21.7 %collective-permute-done.1.refs_1_.refs_0_.refs_2_ = bf16[12,2,64,128]{3,2,1,0:T(8,128)(2,1)S(1)} collective-permute-done((bf16[12,2,64,128]{3,2,1,0:T(8,128)(2,1)}, bf16[12,2,64,128]{3,2,1,0:T(8,128)(2,1)S(1)}, u32[]{:S(2)}, u32[]{:S(2)}) %collective-permute-start.1) | collective-permute-done | bytes 393248 | tf_op jit(solution)/shard_map/ppermute | solution.py:289
  95.0 6.5 %all-to-all-start.1 = ((bf16[16,2,128,128]{3,2,1,0:T(8,128)(2,1)}), bf16[16,2,128,128]{3,2,1,0:T(8,128)(2,1)S(1)}, u32[]{:S(2)}, u32[]{:S(2)}) async-start(bf16[16,2,128,128]{3,2,1,0:T(8,128)(2,1)} %gate.4), calls=%async_computation.1 | async-start | bytes 2097152 | tf_op jit(solution)/shard_map/all_to_all | solution.py:278
  105.8 10.9 %all-to-all-done.1.rows = bf16[16,2,128,128]{3,2,1,0:T(8,128)(2,1)S(1)} async-done(((bf16[16,2,128,128]{3,2,1,0:T(8,128)(2,1)}), bf16[16,2,128,128]{3,2,1,0:T(8,128)(2,1)S(1)}, u32[]{:S(2)}, u32[]{:S(2)}) %all-to-all-start.1) | async-done | bytes 1048608 | tf_op jit(solution)/shard_map/all_to_all | solution.py:278
  117.6 4.0 pack.3
  122.6 10.8 %stats.2.refs_0_ = f32[768,128]{1,0:T(8,128)} custom-call(s32[2]{0:T(128)} %pad_add_fusion.place, s32[640]{0:T(1024)} %recv_table.1.refs_0_.table, bf16[12,2,64,128]{3,2,1,0:T(8,128)(2,1)} %get-tuple-element.62.refs_0_, bf16[12,2,64,128]{3,2,1,0:T(8,128)(2,1)} %copy-done.3, bf16[12,2,64,128]{3,2,1,0:T(8,128)(2,1)} %copy-done.1, ...), custom_call_target="tpu_custom_call" | custom-call | flops 1024 | bytes 1024 | tf_op jit(solution)/shard_map/stats/pallas_call | solution.py:365
  133.4 4.2 %collective-permute-start.8 = (bf16[12,2,64,128]{3,2,1,0:T(8,128)(2,1)}, bf16[12,2,64,128]{3,2,1,0:T(8,128)(2,1)S(1)}, u32[]{:S(2)}, u32[]{:S(2)}) collective-permute-start(bf16[12,2,64,128]{3,2,1,0:T(8,128)(2,1)} %get-tuple-element.76), channel_id=1, source_target_pairs={{0,8},{2,10},{4,12},{6,14},{8,0},{10,2},{12,4},{14,6},{1,9},{3,11}... | collective-permute-start | bytes 1179656 | tf_op jit(solution)/shard_map/ppermute | solution.py:289
  139.5 6.1 %all-to-all-start.2 = ((f32[8,96,128]{2,1,0:T(8,128)}), f32[8,96,128]{2,1,0:T(8,128)S(1)}, u32[]{:S(2)}, u32[]{:S(2)}) async-start(f32[8,96,128]{2,1,0:T(8,128)} %bitcast.15), calls=%async_computation.2 | async-start | bytes 786432 | tf_op jit(solution)/shard_map/all_to_all | solution.py:278
  145.6 5.0 %collective-permute-start.10 = (bf16[12,2,64,128]{3,2,1,0:T(8,128)(2,1)}, bf16[12,2,64,128]{3,2,1,0:T(8,128)(2,1)S(1)}, u32[]{:S(2)}, u32[]{:S(2)}) collective-permute-start(bf16[12,2,64,128]{3,2,1,0:T(8,128)(2,1)} %get-tuple-element.78), channel_id=1, source_target_pairs={{0,10},{2,12},{4,14},{6,0},{8,2},{10,4},{12,6},{14,8},{1,11},{3,13... | collective-permute-start | bytes 1179656 | tf_op jit(solution)/shard_map/ppermute | solution.py:289
  158.5 24.0 %collective-permute-done.9.refs_2_ = bf16[12,2,64,128]{3,2,1,0:T(8,128)(2,1)S(1)} collective-permute-done((bf16[12,2,64,128]{3,2,1,0:T(8,128)(2,1)}, bf16[12,2,64,128]{3,2,1,0:T(8,128)(2,1)S(1)}, u32[]{:S(2)}, u32[]{:S(2)}) %collective-permute-start.9) | collective-permute-done | bytes 393248 | tf_op jit(solution)/shard_map/ppermute | solution.py:289
  183.4 7.3 %all-to-all-done.2 = f32[8,96,128]{2,1,0:T(8,128)S(1)} async-done(((f32[8,96,128]{2,1,0:T(8,128)}), f32[8,96,128]{2,1,0:T(8,128)S(1)}, u32[]{:S(2)}, u32[]{:S(2)}) %all-to-all-start.2) | async-done | bytes 393248 | tf_op jit(solution)/shard_map/all_to_all | solution.py:278
  191.5 26.3 %grads.2 = (bf16[12,2,64,128]{3,2,1,0:T(8,128)(2,1)}, bf16[12,2,64,128]{3,2,1,0:T(8,128)(2,1)}, bf16[12,2,64,128]{3,2,1,0:T(8,128)(2,1)}, bf16[12,2,64,128]{3,2,...) custom-call(s32[2]{0:T(128)} %pad_add_fusion.place, ...), custom_call_target="tpu_custom_call" | custom-call | flops 1024 | bytes 1024 | tf_op jit(solution)/shard_map/grads/pallas_call | solution.py:381
  219.2 10.8 %stats.3.refs_0_ = f32[768,128]{1,0:T(8,128)} custom-call(s32[2]{0:T(128)} %pad_add_fusion.place, s32[640]{0:T(1024)} %recv_table.1.refs_0_.table, bf16[12,2,64,128]{3,2,1,0:T(8,128)(2,1)} %get-tuple-element.68.refs_0_, bf16[12,2,64,128]{3,2,1,0:T(8,128)(2,1)} %copy-done.8, bf16[12,2,64,128]{3,2,1,0:T(8,128)(2,1)} %copy-done.9, ...), custom_call_target="tpu_custom_call" | custom-call | flops 1024 | bytes 1024 | tf_op jit(solution)/shard_map/stats/pallas_call | solution.py:365
  231.7 7.9 %all-to-all-start.3 = ((f32[8,96,128]{2,1,0:T(8,128)}), f32[8,96,128]{2,1,0:T(8,128)S(1)}, u32[]{:S(2)}, u32[]{:S(2)}) async-start(f32[8,96,128]{2,1,0:T(8,128)} %bitcast.16), calls=%async_computation.3 | async-start | bytes 786432 | tf_op jit(solution)/shard_map/all_to_all | solution.py:278
  246.4 7.7 %collective-permute-done.15.refs_1_ = bf16[12,2,64,128]{3,2,1,0:T(8,128)(2,1)S(1)} collective-permute-done((bf16[12,2,64,128]{3,2,1,0:T(8,128)(2,1)}, bf16[12,2,64,128]{3,2,1,0:T(8,128)(2,1)S(1)}, u32[]{:S(2)}, u32[]{:S(2)}) %collective-permute-start.15) | collective-permute-done | bytes 393248 | tf_op jit(solution)/shard_map/ppermute | solution.py:289
  254.0 15.4 %collective-permute-done.16.refs_2_ = bf16[12,2,64,128]{3,2,1,0:T(8,128)(2,1)S(1)} collective-permute-done((bf16[12,2,64,128]{3,2,1,0:T(8,128)(2,1)}, bf16[12,2,64,128]{3,2,1,0:T(8,128)(2,1)S(1)}, u32[]{:S(2)}, u32[]{:S(2)}) %collective-permute-start.16) | collective-permute-done | bytes 393248 | tf_op jit(solution)/shard_map/ppermute | solution.py:289
  269.4 6.3 %collective-permute-start.21 = (bf16[12,2,64,128]{3,2,1,0:T(8,128)(2,1)}, bf16[12,2,64,128]{3,2,1,0:T(8,128)(2,1)S(1)}, u32[]{:S(2)}, u32[]{:S(2)}) collective-permute-start(bf16[12,2,64,128]{3,2,1,0:T(8,128)(2,1)} %get-tuple-element.97), channel_id=1, source_target_pairs={{0,2},{2,4},{4,6},{6,8},{8,10},{10,12},{12,14},{14,0},{1,3},{3,5},... | collective-permute-start | bytes 1179656 | tf_op jit(solution)/shard_map/ppermute | solution.py:289
  279.2 26.4 %grads.3 = (bf16[12,2,64,128]{3,2,1,0:T(8,128)(2,1)}, bf16[12,2,64,128]{3,2,1,0:T(8,128)(2,1)}, bf16[12,2,64,128]{3,2,1,0:T(8,128)(2,1)}, bf16[12,2,64,128]{3,2,...) custom-call(s32[2]{0:T(128)} %pad_add_fusion.place, ...), custom_call_target="tpu_custom_call" | custom-call | flops 1024 | bytes 1024 | tf_op jit(solution)/shard_map/grads/pallas_call | solution.py:381
  310.9 7.7 %all-to-all-start.4 = ((bf16[16,2,128,128]{3,2,1,0:T(8,128)(2,1)}), bf16[16,2,128,128]{3,2,1,0:T(8,128)(2,1)S(1)}, u32[]{:S(2)}, u32[]{:S(2)}) async-start(bf16[16,2,128,128]{3,2,1,0:T(8,128)(2,1)} %unpack.2), calls=%async_computation.4 | async-start | bytes 2097152 | tf_op jit(solution)/shard_map/all_to_all | solution.py:278
  318.6 4.5 %collective-permute-start.22 = (bf16[12,2,64,128]{3,2,1,0:T(8,128)(2,1)}, bf16[12,2,64,128]{3,2,1,0:T(8,128)(2,1)S(1)}, u32[]{:S(2)}, u32[]{:S(2)}) collective-permute-start(bf16[12,2,64,128]{3,2,1,0:T(8,128)(2,1)} %get-tuple-element.100), channel_id=1, source_target_pairs={{0,8},{2,10},{4,12},{6,14},{8,0},{10,2},{12,4},{14,6},{1,9},{3,11}... | collective-permute-start | bytes 1179656 | tf_op jit(solution)/shard_map/ppermute | solution.py:289
  323.0 4.7 %collective-permute-start.23 = (bf16[12,2,64,128]{3,2,1,0:T(8,128)(2,1)S(1)}, bf16[12,2,64,128]{3,2,1,0:T(8,128)(2,1)S(1)}, u32[]{:S(2)}, u32[]{:S(2)}) collective-permute-start(bf16[12,2,64,128]{3,2,1,0:T(8,128)(2,1)S(1)} %copy-done.37), channel_id=1, source_target_pairs={{0,10},{2,12},{4,14},{6,0},{8,2},{10,4},{12,6},{14,8},{1,11},{3,13... | collective-permute-start | bytes 1179656 | tf_op jit(solution)/shard_map/ppermute | solution.py:289
  331.9 13.0 %collective-permute-done.22.refs_1_ = bf16[12,2,64,128]{3,2,1,0:T(8,128)(2,1)S(1)} collective-permute-done((bf16[12,2,64,128]{3,2,1,0:T(8,128)(2,1)}, bf16[12,2,64,128]{3,2,1,0:T(8,128)(2,1)S(1)}, u32[]{:S(2)}, u32[]{:S(2)}) %collective-permute-start.22) | collective-permute-done | bytes 393248 | tf_op jit(solution)/shard_map/ppermute | solution.py:289
  345.2 16.5 %collective-permute-done.23.refs_2_ = bf16[12,2,64,128]{3,2,1,0:T(8,128)(2,1)S(1)} collective-permute-done((bf16[12,2,64,128]{3,2,1,0:T(8,128)(2,1)S(1)}, bf16[12,2,64,128]{3,2,1,0:T(8,128)(2,1)S(1)}, u32[]{:S(2)}, u32[]{:S(2)}) %collective-permute-start.23) | collective-permute-done | bytes 393248 | tf_op jit(solution)/shard_map/ppermute | solution.py:289
  361.7 7.4 %collective-permute-start.28 = (bf16[12,2,64,128]{3,2,1,0:T(8,128)(2,1)}, bf16[12,2,64,128]{3,2,1,0:T(8,128)(2,1)S(1)}, u32[]{:S(2)}, u32[]{:S(2)}) collective-permute-start(bf16[12,2,64,128]{3,2,1,0:T(8,128)(2,1)} %get-tuple-element.106), channel_id=1, source_target_pairs={{0,2},{2,4},{4,6},{6,8},{8,10},{10,12},{12,14},{14,0},{1,3},{3,5},... | collective-permute-start | bytes 1179656 | tf_op jit(solution)/shard_map/ppermute | solution.py:289
  370.2 15.8 %collective-permute-done.25.refs_4_ = bf16[12,2,64,128]{3,2,1,0:T(8,128)(2,1)S(1)} collective-permute-done((bf16[12,2,64,128]{3,2,1,0:T(8,128)(2,1)}, bf16[12,2,64,128]{3,2,1,0:T(8,128)(2,1)S(1)}, u32[]{:S(2)}, u32[]{:S(2)}) %collective-permute-start.25) | collective-permute-done | bytes 393248 | tf_op jit(solution)/shard_map/ppermute | solution.py:289
  395.3 7.2 %all-to-all-start.5 = ((bf16[16,2,128,128]{3,2,1,0:T(8,128)(2,1)}), bf16[16,2,128,128]{3,2,1,0:T(8,128)(2,1)S(1)}, u32[]{:S(2)}, u32[]{:S(2)}) async-start(bf16[16,2,128,128]{3,2,1,0:T(8,128)(2,1)} %unpack.3), calls=%async_computation.5 | async-start | bytes 2097152 | tf_op jit(solution)/shard_map/all_to_all | solution.py:278
  402.7 10.1 %join.1 = bf16[16,2,2,2,128,128]{5,4,3,2,1,0:T(8,128)(2,1)} custom-call(s32[2]{0:T(128)} %pad_add_fusion.place, bf16[16,2,128,128]{3,2,1,0:T(8,128)(2,1)} %get-tuple-element.83.refs_10_.keep0, bf16[16,2,128,128]{3,2,1,0:T(8,128)(2,1)} %get-tuple-element.98.refs_8_.keep1, bf16[16,2,128,128]{3,2,1,0:T(8,128)(2,1)} %collective-permute-done.29.got0, ...), custom_call_target="tpu_custom_call" | custom-call | bytes 1024 | tf_op jit(solution)/shard_map/join/pallas_call | solution.py:415
  412.8 5.0 %all-to-all-done.5 = bf16[16,2,128,128]{3,2,1,0:T(8,128)(2,1)S(1)} async-done(((bf16[16,2,128,128]{3,2,1,0:T(8,128)(2,1)}), bf16[16,2,128,128]{3,2,1,0:T(8,128)(2,1)S(1)}, u32[]{:S(2)}, u32[]{:S(2)}) %all-to-all-start.5) | async-done | bytes 1048608 | tf_op jit(solution)/shard_map/all_to_all | solution.py:278
  (148 shorter events, 79.6 us)
Async XLA Ops:
  4.0 31.1 %collective-permute-start = (bf16[16,2,2,128,128]{4,3,2,1,0:T(8,128)(2,1)}, bf16[16,2,2,128,128]{4,3,2,1,0:T(8,128)(2,1)S(1)}, u32[]{:S(2)}, u32[]{:S(2)}) collective-permute-start(bf16[16,2,2,128,128]{4,3,2,1,0:T(8,128)(2,1)} %dynamic-slice_bitcast_fusion), channel_id=1, source_target_pairs={{0,1},{1,0},{2,3},{3,2},{4,5},{5,4},{6,7},{7,6},{8,9},{9,8},{10,11... | collective-permute-start | bytes 6291464 | tf_op jit(solution)/shard_map/ppermute | solution.py:314
  6.2 28.8 %all-to-all-start = ((bf16[16,2,128,128]{3,2,1,0:T(8,128)(2,1)}), bf16[16,2,128,128]{3,2,1,0:T(8,128)(2,1)S(1)}, u32[]{:S(2)}, u32[]{:S(2)}) async-start(bf16[16,2,128,128]{3,2,1,0:T(8,128)(2,1)} %pad_maximum_fusion), calls=%async_computation | async-start | bytes 2097152 | tf_op jit(solution)/shard_map/all_to_all | solution.py:278
  40.8 44.6 %collective-permute-start.1 = (bf16[12,2,64,128]{3,2,1,0:T(8,128)(2,1)}, bf16[12,2,64,128]{3,2,1,0:T(8,128)(2,1)S(1)}, u32[]{:S(2)}, u32[]{:S(2)}) collective-permute-start(bf16[12,2,64,128]{3,2,1,0:T(8,128)(2,1)} %get-tuple-element.56), channel_id=1, source_target_pairs={{0,6},{2,8},{4,10},{6,12},{8,14},{10,0},{12,2},{14,4},{1,7},{3,9},... | collective-permute-start | bytes 1179656 | tf_op jit(solution)/shard_map/ppermute | solution.py:289
  41.2 47.1 %collective-permute-start.2 = (bf16[12,2,64,128]{3,2,1,0:T(8,128)(2,1)}, bf16[12,2,64,128]{3,2,1,0:T(8,128)(2,1)S(1)}, u32[]{:S(2)}, u32[]{:S(2)}) collective-permute-start(bf16[12,2,64,128]{3,2,1,0:T(8,128)(2,1)} %get-tuple-element.57), channel_id=1, source_target_pairs={{0,10},{2,12},{4,14},{6,0},{8,2},{10,4},{12,6},{14,8},{1,11},{3,13... | collective-permute-start | bytes 1179656 | tf_op jit(solution)/shard_map/ppermute | solution.py:289
  45.9 42.9 %collective-permute-start.3 = (bf16[12,2,64,128]{3,2,1,0:T(8,128)(2,1)}, bf16[12,2,64,128]{3,2,1,0:T(8,128)(2,1)S(1)}, u32[]{:S(2)}, u32[]{:S(2)}) collective-permute-start(bf16[12,2,64,128]{3,2,1,0:T(8,128)(2,1)} %get-tuple-element.58), channel_id=1, source_target_pairs={{0,8},{2,10},{4,12},{6,14},{8,0},{10,2},{12,4},{14,6},{1,9},{3,11}... | collective-permute-start | bytes 1179656 | tf_op jit(solution)/shard_map/ppermute | solution.py:289
  48.2 44.5 %collective-permute-start.4 = (bf16[12,2,64,128]{3,2,1,0:T(8,128)(2,1)}, bf16[12,2,64,128]{3,2,1,0:T(8,128)(2,1)S(1)}, u32[]{:S(2)}, u32[]{:S(2)}) collective-permute-start(bf16[12,2,64,128]{3,2,1,0:T(8,128)(2,1)} %get-tuple-element.59), channel_id=1, source_target_pairs={{0,2},{2,4},{4,6},{6,8},{8,10},{10,12},{12,14},{14,0},{1,3},{3,5},... | collective-permute-start | bytes 1179656 | tf_op jit(solution)/shard_map/ppermute | solution.py:289
  49.2 45.0 %collective-permute-start.5 = (bf16[12,2,64,128]{3,2,1,0:T(8,128)(2,1)}, bf16[12,2,64,128]{3,2,1,0:T(8,128)(2,1)S(1)}, u32[]{:S(2)}, u32[]{:S(2)}) collective-permute-start(bf16[12,2,64,128]{3,2,1,0:T(8,128)(2,1)} %get-tuple-element.60), channel_id=1, source_target_pairs={{0,14},{2,0},{4,2},{6,4},{8,6},{10,8},{12,10},{14,12},{1,15},{3,1}... | collective-permute-start | bytes 1179656 | tf_op jit(solution)/shard_map/ppermute | solution.py:289
  133.4 25.0 %collective-permute-start.8 = (bf16[12,2,64,128]{3,2,1,0:T(8,128)(2,1)}, bf16[12,2,64,128]{3,2,1,0:T(8,128)(2,1)S(1)}, u32[]{:S(2)}, u32[]{:S(2)}) collective-permute-start(bf16[12,2,64,128]{3,2,1,0:T(8,128)(2,1)} %get-tuple-element.76), channel_id=1, source_target_pairs={{0,8},{2,10},{4,12},{6,14},{8,0},{10,2},{12,4},{14,6},{1,9},{3,11}... | collective-permute-start | bytes 1179656 | tf_op jit(solution)/shard_map/ppermute | solution.py:289
  137.7 44.8 %collective-permute-start.9 = (bf16[12,2,64,128]{3,2,1,0:T(8,128)(2,1)}, bf16[12,2,64,128]{3,2,1,0:T(8,128)(2,1)S(1)}, u32[]{:S(2)}, u32[]{:S(2)}) collective-permute-start(bf16[12,2,64,128]{3,2,1,0:T(8,128)(2,1)} %get-tuple-element.77), channel_id=1, source_target_pairs={{0,6},{2,8},{4,10},{6,12},{8,14},{10,0},{12,2},{14,4},{1,7},{3,9},... | collective-permute-start | bytes 1179656 | tf_op jit(solution)/shard_map/ppermute | solution.py:289
  139.5 51.3 %all-to-all-start.2 = ((f32[8,96,128]{2,1,0:T(8,128)}), f32[8,96,128]{2,1,0:T(8,128)S(1)}, u32[]{:S(2)}, u32[]{:S(2)}) async-start(f32[8,96,128]{2,1,0:T(8,128)} %bitcast.15), calls=%async_computation.2 | async-start | bytes 786432 | tf_op jit(solution)/shard_map/all_to_all | solution.py:278
  145.6 72.3 %collective-permute-start.10 = (bf16[12,2,64,128]{3,2,1,0:T(8,128)(2,1)}, bf16[12,2,64,128]{3,2,1,0:T(8,128)(2,1)S(1)}, u32[]{:S(2)}, u32[]{:S(2)}) collective-permute-start(bf16[12,2,64,128]{3,2,1,0:T(8,128)(2,1)} %get-tuple-element.78), channel_id=1, source_target_pairs={{0,10},{2,12},{4,14},{6,0},{8,2},{10,4},{12,6},{14,8},{1,11},{3,13... | collective-permute-start | bytes 1179656 | tf_op jit(solution)/shard_map/ppermute | solution.py:289
  150.6 67.2 %collective-permute-start.11 = (bf16[12,2,64,128]{3,2,1,0:T(8,128)(2,1)}, bf16[12,2,64,128]{3,2,1,0:T(8,128)(2,1)S(1)}, u32[]{:S(2)}, u32[]{:S(2)}) collective-permute-start(bf16[12,2,64,128]{3,2,1,0:T(8,128)(2,1)} %get-tuple-element.79), channel_id=1, source_target_pairs={{0,4},{2,6},{4,8},{6,10},{8,12},{10,14},{12,0},{14,2},{1,5},{3,7},... | collective-permute-start | bytes 1179656 | tf_op jit(solution)/shard_map/ppermute | solution.py:289
  151.2 66.7 %collective-permute-start.12 = (bf16[12,2,64,128]{3,2,1,0:T(8,128)(2,1)}, bf16[12,2,64,128]{3,2,1,0:T(8,128)(2,1)S(1)}, u32[]{:S(2)}, u32[]{:S(2)}) collective-permute-start(bf16[12,2,64,128]{3,2,1,0:T(8,128)(2,1)} %get-tuple-element.80), channel_id=1, source_target_pairs={{0,12},{2,14},{4,0},{6,2},{8,4},{10,6},{12,8},{14,10},{1,13},{3,15... | collective-permute-start | bytes 1179656 | tf_op jit(solution)/shard_map/ppermute | solution.py:289
  158.5 59.5 %collective-permute-start.13 = (bf16[12,2,64,128]{3,2,1,0:T(8,128)(2,1)}, bf16[12,2,64,128]{3,2,1,0:T(8,128)(2,1)S(1)}, u32[]{:S(2)}, u32[]{:S(2)}) collective-permute-start(bf16[12,2,64,128]{3,2,1,0:T(8,128)(2,1)} %get-tuple-element.81), channel_id=1, source_target_pairs={{0,2},{2,4},{4,6},{6,8},{8,10},{10,12},{12,14},{14,0},{1,3},{3,5},... | collective-permute-start | bytes 1179656 | tf_op jit(solution)/shard_map/ppermute | solution.py:289
  182.4 35.5 %collective-permute-start.14 = (bf16[12,2,64,128]{3,2,1,0:T(8,128)(2,1)}, bf16[12,2,64,128]{3,2,1,0:T(8,128)(2,1)S(1)}, u32[]{:S(2)}, u32[]{:S(2)}) collective-permute-start(bf16[12,2,64,128]{3,2,1,0:T(8,128)(2,1)} %get-tuple-element.82), channel_id=1, source_target_pairs={{0,14},{2,0},{4,2},{6,4},{8,6},{10,8},{12,10},{14,12},{1,15},{3,1}... | collective-permute-start | bytes 1179656 | tf_op jit(solution)/shard_map/ppermute | solution.py:289
  230.0 24.0 %collective-permute-start.15 = (bf16[12,2,64,128]{3,2,1,0:T(8,128)(2,1)}, bf16[12,2,64,128]{3,2,1,0:T(8,128)(2,1)S(1)}, u32[]{:S(2)}, u32[]{:S(2)}) collective-permute-start(bf16[12,2,64,128]{3,2,1,0:T(8,128)(2,1)} %get-tuple-element.91), channel_id=1, source_target_pairs={{0,8},{2,10},{4,12},{6,14},{8,0},{10,2},{12,4},{14,6},{1,9},{3,11}... | collective-permute-start | bytes 1179656 | tf_op jit(solution)/shard_map/ppermute | solution.py:289
  231.7 37.8 %collective-permute-start.16 = (bf16[12,2,64,128]{3,2,1,0:T(8,128)(2,1)}, bf16[12,2,64,128]{3,2,1,0:T(8,128)(2,1)S(1)}, u32[]{:S(2)}, u32[]{:S(2)}) collective-permute-start(bf16[12,2,64,128]{3,2,1,0:T(8,128)(2,1)} %get-tuple-element.92), channel_id=1, source_target_pairs={{0,10},{2,12},{4,14},{6,0},{8,2},{10,4},{12,6},{14,8},{1,11},{3,13... | collective-permute-start | bytes 1179656 | tf_op jit(solution)/shard_map/ppermute | solution.py:289
  231.7 46.7 %all-to-all-start.3 = ((f32[8,96,128]{2,1,0:T(8,128)}), f32[8,96,128]{2,1,0:T(8,128)S(1)}, u32[]{:S(2)}, u32[]{:S(2)}) async-start(f32[8,96,128]{2,1,0:T(8,128)} %bitcast.16), calls=%async_computation.3 | async-start | bytes 786432 | tf_op jit(solution)/shard_map/all_to_all | solution.py:278
  239.6 66.0 %collective-permute-start.17 = (bf16[12,2,64,128]{3,2,1,0:T(8,128)(2,1)}, bf16[12,2,64,128]{3,2,1,0:T(8,128)(2,1)S(1)}, u32[]{:S(2)}, u32[]{:S(2)}) collective-permute-start(bf16[12,2,64,128]{3,2,1,0:T(8,128)(2,1)} %get-tuple-element.93), channel_id=1, source_target_pairs={{0,6},{2,8},{4,10},{6,12},{8,14},{10,0},{12,2},{14,4},{1,7},{3,9},... | collective-permute-start | bytes 1179656 | tf_op jit(solution)/shard_map/ppermute | solution.py:289
  243.4 62.2 %collective-permute-start.18 = (bf16[12,2,64,128]{3,2,1,0:T(8,128)(2,1)}, bf16[12,2,64,128]{3,2,1,0:T(8,128)(2,1)S(1)}, u32[]{:S(2)}, u32[]{:S(2)}) collective-permute-start(bf16[12,2,64,128]{3,2,1,0:T(8,128)(2,1)} %get-tuple-element.94), channel_id=1, source_target_pairs={{0,12},{2,14},{4,0},{6,2},{8,4},{10,6},{12,8},{14,10},{1,13},{3,15... | collective-permute-start | bytes 1179656 | tf_op jit(solution)/shard_map/ppermute | solution.py:289
  245.2 60.4 %collective-permute-start.19 = (bf16[12,2,64,128]{3,2,1,0:T(8,128)(2,1)}, bf16[12,2,64,128]{3,2,1,0:T(8,128)(2,1)S(1)}, u32[]{:S(2)}, u32[]{:S(2)}) collective-permute-start(bf16[12,2,64,128]{3,2,1,0:T(8,128)(2,1)} %get-tuple-element.95), channel_id=1, source_target_pairs={{0,4},{2,6},{4,8},{6,10},{8,12},{10,14},{12,0},{14,2},{1,5},{3,7},... | collective-permute-start | bytes 1179656 | tf_op jit(solution)/shard_map/ppermute | solution.py:289
  254.0 51.6 %collective-permute-start.20 = (bf16[12,2,64,128]{3,2,1,0:T(8,128)(2,1)}, bf16[12,2,64,128]{3,2,1,0:T(8,128)(2,1)S(1)}, u32[]{:S(2)}, u32[]{:S(2)}) collective-permute-start(bf16[12,2,64,128]{3,2,1,0:T(8,128)(2,1)} %get-tuple-element.96), channel_id=1, source_target_pairs={{0,14},{2,0},{4,2},{6,4},{8,6},{10,8},{12,10},{14,12},{1,15},{3,1}... | collective-permute-start | bytes 1179656 | tf_op jit(solution)/shard_map/ppermute | solution.py:289
  269.4 36.8 %collective-permute-start.21 = (bf16[12,2,64,128]{3,2,1,0:T(8,128)(2,1)}, bf16[12,2,64,128]{3,2,1,0:T(8,128)(2,1)S(1)}, u32[]{:S(2)}, u32[]{:S(2)}) collective-permute-start(bf16[12,2,64,128]{3,2,1,0:T(8,128)(2,1)} %get-tuple-element.97), channel_id=1, source_target_pairs={{0,2},{2,4},{4,6},{6,8},{8,10},{10,12},{12,14},{14,0},{1,3},{3,5},... | collective-permute-start | bytes 1179656 | tf_op jit(solution)/shard_map/ppermute | solution.py:289
  310.9 84.4 %all-to-all-start.4 = ((bf16[16,2,128,128]{3,2,1,0:T(8,128)(2,1)}), bf16[16,2,128,128]{3,2,1,0:T(8,128)(2,1)S(1)}, u32[]{:S(2)}, u32[]{:S(2)}) async-start(bf16[16,2,128,128]{3,2,1,0:T(8,128)(2,1)} %unpack.2), calls=%async_computation.4 | async-start | bytes 2097152 | tf_op jit(solution)/shard_map/all_to_all | solution.py:278
  318.6 26.3 %collective-permute-start.22 = (bf16[12,2,64,128]{3,2,1,0:T(8,128)(2,1)}, bf16[12,2,64,128]{3,2,1,0:T(8,128)(2,1)S(1)}, u32[]{:S(2)}, u32[]{:S(2)}) collective-permute-start(bf16[12,2,64,128]{3,2,1,0:T(8,128)(2,1)} %get-tuple-element.100), channel_id=1, source_target_pairs={{0,8},{2,10},{4,12},{6,14},{8,0},{10,2},{12,4},{14,6},{1,9},{3,11}... | collective-permute-start | bytes 1179656 | tf_op jit(solution)/shard_map/ppermute | solution.py:289
  323.0 38.7 %collective-permute-start.23 = (bf16[12,2,64,128]{3,2,1,0:T(8,128)(2,1)S(1)}, bf16[12,2,64,128]{3,2,1,0:T(8,128)(2,1)S(1)}, u32[]{:S(2)}, u32[]{:S(2)}) collective-permute-start(bf16[12,2,64,128]{3,2,1,0:T(8,128)(2,1)S(1)} %copy-done.37), channel_id=1, source_target_pairs={{0,10},{2,12},{4,14},{6,0},{8,2},{10,4},{12,6},{14,8},{1,11},{3,13... | collective-permute-start | bytes 1179656 | tf_op jit(solution)/shard_map/ppermute | solution.py:289
  327.7 42.4 %collective-permute-start.24 = (bf16[12,2,64,128]{3,2,1,0:T(8,128)(2,1)}, bf16[12,2,64,128]{3,2,1,0:T(8,128)(2,1)S(1)}, u32[]{:S(2)}, u32[]{:S(2)}) collective-permute-start(bf16[12,2,64,128]{3,2,1,0:T(8,128)(2,1)} %get-tuple-element.102), channel_id=1, source_target_pairs={{0,6},{2,8},{4,10},{6,12},{8,14},{10,0},{12,2},{14,4},{1,7},{3,9},... | collective-permute-start | bytes 1179656 | tf_op jit(solution)/shard_map/ppermute | solution.py:289
  328.1 57.9 %collective-permute-start.25 = (bf16[12,2,64,128]{3,2,1,0:T(8,128)(2,1)}, bf16[12,2,64,128]{3,2,1,0:T(8,128)(2,1)S(1)}, u32[]{:S(2)}, u32[]{:S(2)}) collective-permute-start(bf16[12,2,64,128]{3,2,1,0:T(8,128)(2,1)} %get-tuple-element.103), channel_id=1, source_target_pairs={{0,12},{2,14},{4,0},{6,2},{8,4},{10,6},{12,8},{14,10},{1,13},{3,15... | collective-permute-start | bytes 1179656 | tf_op jit(solution)/shard_map/ppermute | solution.py:289
  330.8 55.2 %collective-permute-start.26 = (bf16[12,2,64,128]{3,2,1,0:T(8,128)(2,1)}, bf16[12,2,64,128]{3,2,1,0:T(8,128)(2,1)S(1)}, u32[]{:S(2)}, u32[]{:S(2)}) collective-permute-start(bf16[12,2,64,128]{3,2,1,0:T(8,128)(2,1)} %get-tuple-element.104), channel_id=1, source_target_pairs={{0,4},{2,6},{4,8},{6,10},{8,12},{10,14},{12,0},{14,2},{1,5},{3,7},... | collective-permute-start | bytes 1179656 | tf_op jit(solution)/shard_map/ppermute | solution.py:289
  344.9 44.5 %collective-permute-start.27 = (bf16[12,2,64,128]{3,2,1,0:T(8,128)(2,1)}, bf16[12,2,64,128]{3,2,1,0:T(8,128)(2,1)S(1)}, u32[]{:S(2)}, u32[]{:S(2)}) collective-permute-start(bf16[12,2,64,128]{3,2,1,0:T(8,128)(2,1)} %get-tuple-element.105), channel_id=1, source_target_pairs={{0,14},{2,0},{4,2},{6,4},{8,6},{10,8},{12,10},{14,12},{1,15},{3,1}... | collective-permute-start | bytes 1179656 | tf_op jit(solution)/shard_map/ppermute | solution.py:289
  361.7 28.8 %collective-permute-start.28 = (bf16[12,2,64,128]{3,2,1,0:T(8,128)(2,1)}, bf16[12,2,64,128]{3,2,1,0:T(8,128)(2,1)S(1)}, u32[]{:S(2)}, u32[]{:S(2)}) collective-permute-start(bf16[12,2,64,128]{3,2,1,0:T(8,128)(2,1)} %get-tuple-element.106), channel_id=1, source_target_pairs={{0,2},{2,4},{4,6},{6,8},{8,10},{10,12},{12,14},{14,0},{1,3},{3,5},... | collective-permute-start | bytes 1179656 | tf_op jit(solution)/shard_map/ppermute | solution.py:289
  370.2 32.5 %collective-permute-start.29 = (bf16[16,2,128,128]{3,2,1,0:T(8,128)(2,1)}, bf16[16,2,128,128]{3,2,1,0:T(8,128)(2,1)}, u32[]{:S(2)}, u32[]{:S(2)}) collective-permute-start(bf16[16,2,128,128]{3,2,1,0:T(8,128)(2,1)} %get-tuple-element.107), channel_id=1, source_target_pairs={{0,1},{1,0},{2,3},{3,2},{4,5},{5,4},{6,7},{7,6},{8,9},{9,8},{10,11... | collective-permute-start | bytes 3145736 | tf_op jit(solution)/shard_map/ppermute | solution.py:395
  (43 other events, 472.2 us)

commit v5 on v4

--- a/solution.py
+++ b/solution.py
@@ -19,6 +19,7 @@
 SPANS = INST // 2
 BLK = 16
 UNROLL = 4
+UNROLL_STATS = 8
 COST = 1 << 10
 LIST = 104
 SCALE = 1.0 / math.sqrt(DH)
@@ -153,8 +154,8 @@
         copy.wait()
 
     def step(it, carry):
-        for u in range(UNROLL):
-            n = it * UNROLL + u
+        for u in range(UNROLL_STATS):
+            n = it * UNROLL_STATS + u
             row, srow, block = table[n], table[R_STAT + n], table[R_BLK + n]
             score = dot(store[block, 0], stage[row, 0], NT) * SCALE
             gprob = dot(store[block, 1], stage[row, 1], NT)
@@ -165,7 +166,7 @@
             stats[pl.ds(srow, 1), :] = jnp.concatenate([top + jnp.log(total), delta], axis=1)
         return carry
 
-    lax.fori_loop(0, (table[R_COUNT] + UNROLL - 1) // UNROLL, step, 0)
+    lax.fori_loop(0, (table[R_COUNT] + UNROLL_STATS - 1) // UNROLL_STATS, step, 0)
     for chip in range(RING):
         out[pl.ds(chip * STAT_ROWS, STAT_ROWS), :] = stats[:STAT_ROWS]
 
@@ -270,7 +271,8 @@
 SEMS = pltpu.SemaphoreType.DMA((RING + 2,))
 
 
-EARLY, LATE = (3, 5, 4, 1, 7), (2, 6)
+EARLY = (4, 3, 5, 2, 6)
+LIGHT, HEAVY = (2, 6, 1, 7), (4, 3, 5)
 ORDER = (0, 4, 3, 5, 2, 6, 1, 7)
 
 
@@ -278,11 +280,7 @@
     return lax.all_to_all(rows, axis, split_axis=0, concat_axis=0, tiled=True)
 
 
-def ring_send(parts, sign, gated=(), after=()):
-    parts = list(parts)
-    if gated:
-        for d, part in zip(gated, gate([parts[d] for d in gated], after)):
-            parts[d] = part
+def ring_send(parts, sign):
     got = list(parts)
     for d in sorted(range(1, RING), key=ORDER.index):
         pairs = [(i, (i + sign * d) % RING) for i in range(RING)]
@@ -311,19 +309,19 @@
     place = jnp.stack([lax.axis_index("grp"), core]).astype(jnp.int32)
     names = jnp.concatenate([nbr_owner.reshape(INST), nbr_block.reshape(INST)])
     swap = [(0, 1), (1, 0)]
-    kv_other = lax.ppermute(
-        lax.dynamic_index_in_dim(kv_store, 1 - core, 2, keepdims=False), "store", swap
-    )
     query_rows = query.reshape(SEQ, 2, 128, DH)
     grad_rows = d_out.reshape(SEQ, 2, 128, DH)
+    first = jnp.stack([query_rows[:, 0], grad_rows[:, 0]], axis=1)
+    first, half = lax.optimization_barrier((first, 1 - core))
+    kv_other = lax.ppermute(
+        lax.dynamic_index_in_dim(kv_store, half, 2, keepdims=False), "store", swap
+    )
 
     arrived = []
     all_names = lax.all_gather(names.reshape(1, 2 * INST), "grp", tiled=True)
     after = [kv_other, all_names]
     for pair in range(2):
-        rows = jnp.stack([query_rows[:, pair], grad_rows[:, pair]], axis=1)
-        if pair == 1:
-            (rows,) = gate([rows], [recv_table] + after)
+        rows = first if pair == 0 else jnp.stack([query_rows[:, 1], grad_rows[:, 1]], axis=1)
         rows = exchange(rows, "seq")
         outs = pl.pallas_call(
             pack_kernel,
@@ -354,8 +352,8 @@
                 cost_estimate=cost(0, COST),
                 name="recv_table",
             )(place, all_names)
-            arrived.append(ring_send(outs[:RING], 1, LATE, [recv_table]))
-            after = [arrived[0][d] for d in EARLY]
+            arrived.append(ring_send(outs[:RING], 1))
+            after = [recv_table] + [arrived[0][d] for d in EARLY]
     bulk = outs[:RING]
 
     after = [send_table]
@@ -373,7 +371,11 @@
             name="stats",
         )(place, recv_table, *ordered(arrived[pair]), kv_store, kv_other, *after)
         given = exchange(stats, "grp")
-        moved = ring_send(bulk, 1 - 2 * pair, range(1, RING), [stats])
+        bulk = list(bulk)
+        for some, ready in ((LIGHT, stats), (HEAVY, given)):
+            for d, part in zip(some, gate([bulk[d] for d in some], [ready])):
+                bulk[d] = part
+        moved = ring_send(bulk, 1 - 2 * pair)
         if pair == 0:
             arrived.append(moved)
         else:
@@ -381,7 +383,7 @@
         outs = pl.pallas_call(
             functools.partial(grad_kernel, pair),
             out_shape=[shape(PART)] * RING + [shape((BLK, 2, 128, DH))] * 2,
-            in_specs=[SMEM, SMEM, VMEM] + [ANY] * (RING + 2),
+            in_specs=[SMEM, SMEM, VMEM] + [ANY] * (RING + 2 + len(LIGHT)),
             out_specs=[ANY] * RING + [VMEM] * 2,
             scratch_shapes=[STAGE, STORE, STAGE]
             + [pltpu.VMEM((LIST, DH), F32)] * 3
@@ -389,11 +391,20 @@
             compiler_params=PARAMS,
             cost_estimate=cost(COST, COST),
             name="grads",
-        )(place, recv_table, given, *ordered(arrived[pair]), kv_store, kv_other)
+        )(
+            place,
+            recv_table,
+            given,
+            *ordered(arrived[pair]),
+            kv_store,
+            kv_other,
+            *(moved[d] for d in LIGHT),
+        )
         bulk = outs[:RING]
         after = [outs[RING]]
         kv_grads.append((outs[RING], lax.ppermute(outs[RING + 1], "store", swap)))
-    returned.append(ring_send(bulk, -1))
+    later = [returned[0][d] for d in LIGHT + HEAVY[:1]]
+    returned.append(ring_send([bulk[0], *gate(bulk[1:], later)], -1))
 
     results = []
     for pair in range(2):

time: 425 us -> 411 us (0.967)
  Pallas kernels: 110 us -> 96.2 us
  waiting for transfers between devices: 159 us -> 151 us
    pallas_call x2, Pallas kernels: 52.7 us -> 44.4 us  [on_device(): pl.pallas_call(functools.partial(grad_kernel, pair), out_shape=[shape(PAR...]
    all_to_all x6, waiting for transfers between devices: 25.8 us -> 18 us  [exchange(): return lax.all_to_all(rows, axis, split_axis=0, concat_axis=0, tiled=True)]
    all_to_all x6, starting transfers between devices: 43 us -> 49.4 us  [exchange(): return lax.all_to_all(rows, axis, split_axis=0, concat_axis=0, tiled=True)]
    pallas_call x2, Pallas kernels: 21.6 us -> 15.6 us  [on_device(): pl.pallas_call(functools.partial(stat_kernel, pair), out_shape=shape((RIN...]
    ppermute x28, starting transfers between devices: 66.9 us -> 62.5 us  [ring_send(): got[d] = lax.ppermute(parts[d], 'grp', pairs)]
    unnamed x78 -> x66, local copies, waits for them, and re-layouts: 8.73 us -> 10.5 us
  transfers between devices with their start and end apart: 37 -> 37, of which waited for: 20 -> 19; matrix products, arithmetic and copies ran while one was open for 1% -> 1% of each run, Pallas kernels for 19% -> 19%
where the time goes in v5:
time: 411 us; the launch traced here: 404 us
  waiting for transfers between devices  151 us (37%)
  starting transfers between devices  112 us (27%)
  Pallas kernels  96.2 us (23%)
  blocking collectives  19.6 us (5%)
  local copies, waits for them, and re-layouts  16.8 us (4%)
  other arithmetic  6.83 us (2%)
    ppermute x28, waiting for transfers between devices, ring_send(): got[d] = lax.ppermute(parts[d], 'grp', pairs)  133 us
    ppermute x28, starting transfers between devices, ring_send(): got[d] = lax.ppermute(parts[d], 'grp', pairs)  62.5 us
    all_to_all x6, starting transfers between devices, exchange(): return lax.all_to_all(rows, axis, split_axis=0, concat_axis=0, tiled=True)  49.4 us
    pallas_call x2, Pallas kernels, on_device(): pl.pallas_call(functools.partial(grad_kernel, pair), out_shape=[shape(PAR...  44.4 us
    all_gather x1, blocking collectives, on_device(): all_names = lax.all_gather(names.reshape(1, 2 * INST), 'grp', tiled=True)  19.6 us
    all_to_all x6, waiting for transfers between devices, exchange(): return lax.all_to_all(rows, axis, split_axis=0, concat_axis=0, tiled=True)  18 us
    pallas_call x2, Pallas kernels, on_device(): pl.pallas_call(functools.partial(stat_kernel, pair), out_shape=shape((RIN...  15.6 us
    unnamed x66, local copies, waits for them, and re-layouts  10.5 us
  transfers between devices with their start and end apart: 37, of which 19 were waited for; matrix products, arithmetic and copies ran while one was open for 1% of the time, Pallas kernels for 19%

profile of v5, /device:TPU:2, one launch (start us, length us, event | category | flops | bytes accessed | tf_op | source)
XLA Modules:
  0.0 403.7 jit_solution(50071873621435643)
XLA Ops:
  7.6 7.5 %all-to-all-start.1 = ((bf16[16,2,128,128]{3,2,1,0:T(8,128)(2,1)}), bf16[16,2,128,128]{3,2,1,0:T(8,128)(2,1)S(1)}, u32[]{:S(2)}, u32[]{:S(2)}) async-start(bf16[16,2,128,128]{3,2,1,0:T(8,128)(2,1)} %pad_maximum_fusion.1), calls=%async_computation.1 | async-start | bytes 2097152 | tf_op jit(solution)/shard_map/all_to_all | solution.py:280
  15.5 19.6 %all-gather.1 = s32[8,1,128]{2,1,0:T(1,128)} all-gather(s32[1,1,128]{2,1,0:T(1,128)S(1)} %fusion.4), channel_id=2, replica_groups=mesh['seq'=16,'grp'=8,'store'=2] {'grp'}, dimensions={0}, use_global_device_ids=true | all-gather | bytes 4608 | tf_op jit(solution)/shard_map/all_gather | solution.py:321
  37.4 7.2 %all-to-all-start = ((bf16[16,2,128,128]{3,2,1,0:T(8,128)(2,1)}), bf16[16,2,128,128]{3,2,1,0:T(8,128)(2,1)}, u32[]{:S(2)}, u32[]{:S(2)}) async-start(bf16[16,2,128,128]{3,2,1,0:T(8,128)(2,1)} %pad_maximum_fusion), calls=%async_computation | async-start | bytes 2097152 | tf_op jit(solution)/shard_map/all_to_all | solution.py:280
  47.3 4.0 pack.2
  62.8 14.9 %collective-permute-done.1.refs_1_ = bf16[12,2,64,128]{3,2,1,0:T(8,128)(2,1)S(1)} collective-permute-done((bf16[12,2,64,128]{3,2,1,0:T(8,128)(2,1)}, bf16[12,2,64,128]{3,2,1,0:T(8,128)(2,1)S(1)}, u32[]{:S(2)}, u32[]{:S(2)}) %collective-permute-start.1) | collective-permute-done | bytes 393248 | tf_op jit(solution)/shard_map/ppermute | solution.py:287
  77.7 23.4 %collective-permute-done.2.refs_2_ = bf16[12,2,64,128]{3,2,1,0:T(8,128)(2,1)S(1)} collective-permute-done((bf16[12,2,64,128]{3,2,1,0:T(8,128)(2,1)}, bf16[12,2,64,128]{3,2,1,0:T(8,128)(2,1)S(1)}, u32[]{:S(2)}, u32[]{:S(2)}) %collective-permute-start.2) | collective-permute-done | bytes 393248 | tf_op jit(solution)/shard_map/ppermute | solution.py:287
  101.0 10.2 %recv_table.1.refs_0_.table = s32[640]{0:T(1024)} custom-call(s32[2]{0:T(128)} %pad_add_fusion.place, s32[8,128]{1,0:T(8,128)} %bitcast.26), custom_call_target="tpu_custom_call" | custom-call | bytes 1024 | tf_op jit(solution)/shard_map/recv_table/pallas_call | solution.py:343
  114.9 4.0 %pack.3 = (bf16[12,2,64,128]{3,2,1,0:T(8,128)(2,1)}, bf16[12,2,64,128]{3,2,1,0:T(8,128)(2,1)}, bf16[12,2,64,128]{3,2,1,0:T(8,128)(2,1)}, bf16[12,2,64,128]{3,2,1...) custom-call(s32[2]{0:T(128)} %pad_add_fusion.place, ...), custom_call_target="tpu_custom_call" | custom-call | bytes 1024 | tf_op jit(solution)/shard_map/pack/pallas_call | solution.py:326
  120.9 7.8 %stats.2.refs_0_ = f32[768,128]{1,0:T(8,128)} custom-call(s32[2]{0:T(128)} %pad_add_fusion.place, s32[640]{0:T(1024)} %recv_table.1.refs_0_.table, bf16[12,2,64,128]{3,2,1,0:T(8,128)(2,1)} %get-tuple-element.71.refs_0_, bf16[12,2,64,128]{3,2,1,0:T(8,128)(2,1)} %copy-done.2, bf16[12,2,64,128]{3,2,1,0:T(8,128)(2,1)} %copy-done.3, ...), custom_call_target="tpu_custom_call" | custom-call | flops 1024 | bytes 1024 | tf_op jit(solution)/shard_map/stats/pallas_call | solution.py:363
  128.7 7.1 %all-to-all-start.2 = ((f32[8,96,128]{2,1,0:T(8,128)}), f32[8,96,128]{2,1,0:T(8,128)S(1)}, u32[]{:S(2)}, u32[]{:S(2)}) async-start(f32[8,96,128]{2,1,0:T(8,128)} %bitcast.15), calls=%async_computation.2 | async-start | bytes 786432 | tf_op jit(solution)/shard_map/all_to_all | solution.py:280
  143.2 7.8 %all-to-all-done.2 = f32[8,96,128]{2,1,0:T(8,128)S(1)} async-done(((f32[8,96,128]{2,1,0:T(8,128)}), f32[8,96,128]{2,1,0:T(8,128)S(1)}, u32[]{:S(2)}, u32[]{:S(2)}) %all-to-all-start.2) | async-done | bytes 393248 | tf_op jit(solution)/shard_map/all_to_all | solution.py:280
  153.4 12.8 %collective-permute-done.8.refs_10_.refs_4_ = bf16[12,2,64,128]{3,2,1,0:T(8,128)(2,1)S(1)} collective-permute-done((bf16[12,2,64,128]{3,2,1,0:T(8,128)(2,1)}, bf16[12,2,64,128]{3,2,1,0:T(8,128)(2,1)S(1)}, u32[]{:S(2)}, u32[]{:S(2)}) %collective-permute-start.8) | collective-permute-done | bytes 393248 | tf_op jit(solution)/shard_map/ppermute | solution.py:287
  166.2 5.0 %collective-permute-start.14 = (bf16[12,2,64,128]{3,2,1,0:T(8,128)(2,1)}, bf16[12,2,64,128]{3,2,1,0:T(8,128)(2,1)S(1)}, u32[]{:S(2)}, u32[]{:S(2)}) collective-permute-start(bf16[12,2,64,128]{3,2,1,0:T(8,128)(2,1)} %get-tuple-element.89), channel_id=1, source_target_pairs={{0,10},{2,12},{4,14},{6,0},{8,2},{10,4},{12,6},{14,8},{1,11},{3,13... | collective-permute-start | bytes 1179656 | tf_op jit(solution)/shard_map/ppermute | solution.py:287
  171.2 19.4 %collective-permute-done.10.refs_12_.refs_6_ = bf16[12,2,64,128]{3,2,1,0:T(8,128)(2,1)S(1)} collective-permute-done((bf16[12,2,64,128]{3,2,1,0:T(8,128)(2,1)}, bf16[12,2,64,128]{3,2,1,0:T(8,128)(2,1)S(1)}, u32[]{:S(2)}, u32[]{:S(2)}) %collective-permute-start.10) | collective-permute-done | bytes 393248 | tf_op jit(solution)/shard_map/ppermute | solution.py:287
  192.1 22.2 %grads.2 = (bf16[12,2,64,128]{3,2,1,0:T(8,128)(2,1)}, bf16[12,2,64,128]{3,2,1,0:T(8,128)(2,1)}, bf16[12,2,64,128]{3,2,1,0:T(8,128)(2,1)}, bf16[12,2,64,128]{3,2,...) custom-call(s32[2]{0:T(128)} %pad_add_fusion.place, ...), custom_call_target="tpu_custom_call" | custom-call | flops 1024 | bytes 1024 | tf_op jit(solution)/shard_map/grads/pallas_call | solution.py:383
  217.8 7.8 %stats.3.refs_0_ = f32[768,128]{1,0:T(8,128)} custom-call(s32[2]{0:T(128)} %pad_add_fusion.place, s32[640]{0:T(1024)} %recv_table.1.refs_0_.table, bf16[12,2,64,128]{3,2,1,0:T(8,128)(2,1)} %get-tuple-element.83.refs_0_, bf16[12,2,64,128]{3,2,1,0:T(8,128)(2,1)} %copy-done.17, bf16[12,2,64,128]{3,2,1,0:T(8,128)(2,1)} %copy-done.18, ...), custom_call_target="tpu_custom_call" | custom-call | flops 1024 | bytes 1024 | tf_op jit(solution)/shard_map/stats/pallas_call | solution.py:363
  225.6 13.1 %all-to-all-start.3 = ((f32[8,96,128]{2,1,0:T(8,128)}), f32[8,96,128]{2,1,0:T(8,128)S(1)}, u32[]{:S(2)}, u32[]{:S(2)}) async-start(f32[8,96,128]{2,1,0:T(8,128)} %bitcast.16), calls=%async_computation.3 | async-start | bytes 786432 | tf_op jit(solution)/shard_map/all_to_all | solution.py:280
  238.7 4.1 %collective-permute-start.18 = (bf16[12,2,64,128]{3,2,1,0:T(8,128)(2,1)}, bf16[12,2,64,128]{3,2,1,0:T(8,128)(2,1)S(1)}, u32[]{:S(2)}, u32[]{:S(2)}) collective-permute-start(bf16[12,2,64,128]{3,2,1,0:T(8,128)(2,1)} %get-tuple-element.101), channel_id=1, source_target_pairs={{0,12},{2,14},{4,0},{6,2},{8,4},{10,6},{12,8},{14,10},{1,13},{3,15... | collective-permute-start | bytes 1179656 | tf_op jit(solution)/shard_map/ppermute | solution.py:287
  246.1 9.5 %all-to-all-done.3 = f32[8,96,128]{2,1,0:T(8,128)S(1)} async-done(((f32[8,96,128]{2,1,0:T(8,128)}), f32[8,96,128]{2,1,0:T(8,128)S(1)}, u32[]{:S(2)}, u32[]{:S(2)}) %all-to-all-start.3) | async-done | bytes 393248 | tf_op jit(solution)/shard_map/all_to_all | solution.py:280
  256.3 10.6 %collective-permute-done.18.refs_10_.refs_4_.refs_0_ = bf16[12,2,64,128]{3,2,1,0:T(8,128)(2,1)S(1)} collective-permute-done((bf16[12,2,64,128]{3,2,1,0:T(8,128)(2,1)}, bf16[12,2,64,128]{3,2,1,0:T(8,128)(2,1)S(1)}, u32[]{:S(2)}, u32[]{:S(2)}) %collective-permute-start.18) | collective-permute-done | bytes 393248 | tf_op jit(solution)/shard_map/ppermute | solution.py:287
  270.8 12.6 %collective-permute-done.20.refs_12_.refs_6_.refs_2_ = bf16[12,2,64,128]{3,2,1,0:T(8,128)(2,1)S(1)} collective-permute-done((bf16[12,2,64,128]{3,2,1,0:T(8,128)(2,1)}, bf16[12,2,64,128]{3,2,1,0:T(8,128)(2,1)S(1)}, u32[]{:S(2)}, u32[]{:S(2)}) %collective-permute-start.20) | collective-permute-done | bytes 393248 | tf_op jit(solution)/shard_map/ppermute | solution.py:287
  283.4 6.3 %collective-permute-done.21.refs_13_.refs_7_.refs_3_ = bf16[12,2,64,128]{3,2,1,0:T(8,128)(2,1)S(1)} collective-permute-done((bf16[12,2,64,128]{3,2,1,0:T(8,128)(2,1)}, bf16[12,2,64,128]{3,2,1,0:T(8,128)(2,1)S(1)}, u32[]{:S(2)}, u32[]{:S(2)}) %collective-permute-start.21) | collective-permute-done | bytes 393248 | tf_op jit(solution)/shard_map/ppermute | solution.py:287
  290.5 22.2 %grads.3 = (bf16[12,2,64,128]{3,2,1,0:T(8,128)(2,1)}, bf16[12,2,64,128]{3,2,1,0:T(8,128)(2,1)}, bf16[12,2,64,128]{3,2,1,0:T(8,128)(2,1)}, bf16[12,2,64,128]{3,2,...) custom-call(s32[2]{0:T(128)} %pad_add_fusion.place, ...), custom_call_target="tpu_custom_call" | custom-call | flops 1024 | bytes 1024 | tf_op jit(solution)/shard_map/grads/pallas_call | solution.py:383
  317.7 7.3 %all-to-all-start.4 = ((bf16[16,2,128,128]{3,2,1,0:T(8,128)(2,1)}), bf16[16,2,128,128]{3,2,1,0:T(8,128)(2,1)S(1)}, u32[]{:S(2)}, u32[]{:S(2)}) async-start(bf16[16,2,128,128]{3,2,1,0:T(8,128)(2,1)} %unpack.2), calls=%async_computation.4 | async-start | bytes 2097152 | tf_op jit(solution)/shard_map/all_to_all | solution.py:280
  325.0 16.4 %collective-permute-start.22 = (bf16[12,2,64,128]{3,2,1,0:T(8,128)(2,1)}, bf16[12,2,64,128]{3,2,1,0:T(8,128)(2,1)S(1)}, u32[]{:S(2)}, u32[]{:S(2)}) collective-permute-start(bf16[12,2,64,128]{3,2,1,0:T(8,128)(2,1)} %get-tuple-element.114), channel_id=1, source_target_pairs={{0,8},{2,10},{4,12},{6,14},{8,0},{10,2},{12,4},{14,6},{1,9},{3,11}... | collective-permute-start | bytes 1179656 | tf_op jit(solution)/shard_map/ppermute | solution.py:287
  348.2 7.5 %collective-permute-done.22.refs_1_ = bf16[12,2,64,128]{3,2,1,0:T(8,128)(2,1)S(1)} collective-permute-done((bf16[12,2,64,128]{3,2,1,0:T(8,128)(2,1)}, bf16[12,2,64,128]{3,2,1,0:T(8,128)(2,1)S(1)}, u32[]{:S(2)}, u32[]{:S(2)}) %collective-permute-start.22) | collective-permute-done | bytes 393248 | tf_op jit(solution)/shard_map/ppermute | solution.py:287
  355.7 5.4 %collective-permute-done.23.refs_2_ = bf16[12,2,64,128]{3,2,1,0:T(8,128)(2,1)S(1)} collective-permute-done((bf16[12,2,64,128]{3,2,1,0:T(8,128)(2,1)}, bf16[12,2,64,128]{3,2,1,0:T(8,128)(2,1)S(1)}, u32[]{:S(2)}, u32[]{:S(2)}) %collective-permute-start.23) | collective-permute-done | bytes 393248 | tf_op jit(solution)/shard_map/ppermute | solution.py:287
  363.7 5.9 %collective-permute-done.24.refs_3_ = bf16[12,2,64,128]{3,2,1,0:T(8,128)(2,1)S(1)} collective-permute-done((bf16[12,2,64,128]{3,2,1,0:T(8,128)(2,1)}, bf16[12,2,64,128]{3,2,1,0:T(8,128)(2,1)S(1)}, u32[]{:S(2)}, u32[]{:S(2)}) %collective-permute-start.24) | collective-permute-done | bytes 393248 | tf_op jit(solution)/shard_map/ppermute | solution.py:287
  372.1 4.2 %collective-permute-done.27.refs_6_ = bf16[12,2,64,128]{3,2,1,0:T(8,128)(2,1)} collective-permute-done((bf16[12,2,64,128]{3,2,1,0:T(8,128)(2,1)}, bf16[12,2,64,128]{3,2,1,0:T(8,128)(2,1)}, u32[]{:S(2)}, u32[]{:S(2)}) %collective-permute-start.27) | collective-permute-done | bytes 393248 | tf_op jit(solution)/shard_map/ppermute | solution.py:287
  378.4 3.9 unpack.3
  382.3 7.2 %all-to-all-start.5 = ((bf16[16,2,128,128]{3,2,1,0:T(8,128)(2,1)}), bf16[16,2,128,128]{3,2,1,0:T(8,128)(2,1)S(1)}, u32[]{:S(2)}, u32[]{:S(2)}) async-start(bf16[16,2,128,128]{3,2,1,0:T(8,128)(2,1)} %unpack.3), calls=%async_computation.5 | async-start | bytes 2097152 | tf_op jit(solution)/shard_map/all_to_all | solution.py:280
  390.5 10.1 %join.1 = bf16[16,2,2,2,128,128]{5,4,3,2,1,0:T(8,128)(2,1)} custom-call(s32[2]{0:T(128)} %pad_add_fusion.place, bf16[16,2,128,128]{3,2,1,0:T(8,128)(2,1)} %get-tuple-element.90.refs_10_.keep0, bf16[16,2,128,128]{3,2,1,0:T(8,128)(2,1)} %get-tuple-element.105.refs_8_.keep1, bf16[16,2,128,128]{3,2,1,0:T(8,128)(2,1)} %copy-done.23, ...), custom_call_target="tpu_custom_call" | custom-call | bytes 1024 | tf_op jit(solution)/shard_map/join/pallas_call | solution.py:426
  (137 shorter events, 75.4 us)
Async XLA Ops:
  7.6 38.4 %collective-permute-start = (bf16[16,2,2,128,128]{4,3,2,1,0:T(8,128)(2,1)}, bf16[16,2,2,128,128]{4,3,2,1,0:T(8,128)(2,1)S(1)}, u32[]{:S(2)}, u32[]{:S(2)}) collective-permute-start(bf16[16,2,2,128,128]{4,3,2,1,0:T(8,128)(2,1)} %dynamic-slice_bitcast_fusion), channel_id=1, source_target_pairs={{0,1},{1,0},{2,3},{3,2},{4,5},{5,4},{6,7},{7,6},{8,9},{9,8},{10,11... | collective-permute-start | bytes 6291464 | tf_op jit(solution)/shard_map/ppermute | solution.py:316
  7.6 29.9 %all-to-all-start.1 = ((bf16[16,2,128,128]{3,2,1,0:T(8,128)(2,1)}), bf16[16,2,128,128]{3,2,1,0:T(8,128)(2,1)S(1)}, u32[]{:S(2)}, u32[]{:S(2)}) async-start(bf16[16,2,128,128]{3,2,1,0:T(8,128)(2,1)} %pad_maximum_fusion.1), calls=%async_computation.1 | async-start | bytes 2097152 | tf_op jit(solution)/shard_map/all_to_all | solution.py:280
  37.4 73.8 %all-to-all-start = ((bf16[16,2,128,128]{3,2,1,0:T(8,128)(2,1)}), bf16[16,2,128,128]{3,2,1,0:T(8,128)(2,1)}, u32[]{:S(2)}, u32[]{:S(2)}) async-start(bf16[16,2,128,128]{3,2,1,0:T(8,128)(2,1)} %pad_maximum_fusion), calls=%async_computation | async-start | bytes 2097152 | tf_op jit(solution)/shard_map/all_to_all | solution.py:280
  51.3 26.4 %collective-permute-start.1 = (bf16[12,2,64,128]{3,2,1,0:T(8,128)(2,1)}, bf16[12,2,64,128]{3,2,1,0:T(8,128)(2,1)S(1)}, u32[]{:S(2)}, u32[]{:S(2)}) collective-permute-start(bf16[12,2,64,128]{3,2,1,0:T(8,128)(2,1)} %get-tuple-element.65), channel_id=1, source_target_pairs={{0,8},{2,10},{4,12},{6,14},{8,0},{10,2},{12,4},{14,6},{1,9},{3,11}... | collective-permute-start | bytes 1179656 | tf_op jit(solution)/shard_map/ppermute | solution.py:287
  53.6 47.5 %collective-permute-start.2 = (bf16[12,2,64,128]{3,2,1,0:T(8,128)(2,1)}, bf16[12,2,64,128]{3,2,1,0:T(8,128)(2,1)S(1)}, u32[]{:S(2)}, u32[]{:S(2)}) collective-permute-start(bf16[12,2,64,128]{3,2,1,0:T(8,128)(2,1)} %get-tuple-element.66), channel_id=1, source_target_pairs={{0,6},{2,8},{4,10},{6,12},{8,14},{10,0},{12,2},{14,4},{1,7},{3,9},... | collective-permute-start | bytes 1179656 | tf_op jit(solution)/shard_map/ppermute | solution.py:287
  54.9 56.3 %collective-permute-start.3 = (bf16[12,2,64,128]{3,2,1,0:T(8,128)(2,1)}, bf16[12,2,64,128]{3,2,1,0:T(8,128)(2,1)S(1)}, u32[]{:S(2)}, u32[]{:S(2)}) collective-permute-start(bf16[12,2,64,128]{3,2,1,0:T(8,128)(2,1)} %get-tuple-element.67), channel_id=1, source_target_pairs={{0,10},{2,12},{4,14},{6,0},{8,2},{10,4},{12,6},{14,8},{1,11},{3,13... | collective-permute-start | bytes 1179656 | tf_op jit(solution)/shard_map/ppermute | solution.py:287
  58.6 54.8 %collective-permute-start.4 = (bf16[12,2,64,128]{3,2,1,0:T(8,128)(2,1)}, bf16[12,2,64,128]{3,2,1,0:T(8,128)(2,1)S(1)}, u32[]{:S(2)}, u32[]{:S(2)}) collective-permute-start(bf16[12,2,64,128]{3,2,1,0:T(8,128)(2,1)} %get-tuple-element.68), channel_id=1, source_target_pairs={{0,4},{2,6},{4,8},{6,10},{8,12},{10,14},{12,0},{14,2},{1,5},{3,7},... | collective-permute-start | bytes 1179656 | tf_op jit(solution)/shard_map/ppermute | solution.py:287
  59.5 53.9 %collective-permute-start.5 = (bf16[12,2,64,128]{3,2,1,0:T(8,128)(2,1)}, bf16[12,2,64,128]{3,2,1,0:T(8,128)(2,1)S(1)}, u32[]{:S(2)}, u32[]{:S(2)}) collective-permute-start(bf16[12,2,64,128]{3,2,1,0:T(8,128)(2,1)} %get-tuple-element.69), channel_id=1, source_target_pairs={{0,12},{2,14},{4,0},{6,2},{8,4},{10,6},{12,8},{14,10},{1,13},{3,15... | collective-permute-start | bytes 1179656 | tf_op jit(solution)/shard_map/ppermute | solution.py:287
  77.7 42.3 %collective-permute-start.6 = (bf16[12,2,64,128]{3,2,1,0:T(8,128)(2,1)}, bf16[12,2,64,128]{3,2,1,0:T(8,128)(2,1)S(1)}, u32[]{:S(2)}, u32[]{:S(2)}) collective-permute-start(bf16[12,2,64,128]{3,2,1,0:T(8,128)(2,1)} %get-tuple-element.72), channel_id=1, source_target_pairs={{0,2},{2,4},{4,6},{6,8},{8,10},{10,12},{12,14},{14,0},{1,3},{3,5},... | collective-permute-start | bytes 1179656 | tf_op jit(solution)/shard_map/ppermute | solution.py:287
  128.7 22.4 %all-to-all-start.2 = ((f32[8,96,128]{2,1,0:T(8,128)}), f32[8,96,128]{2,1,0:T(8,128)S(1)}, u32[]{:S(2)}, u32[]{:S(2)}) async-start(f32[8,96,128]{2,1,0:T(8,128)} %bitcast.15), calls=%async_computation.2 | async-start | bytes 786432 | tf_op jit(solution)/shard_map/all_to_all | solution.py:280
  135.8 30.4 %collective-permute-start.8 = (bf16[12,2,64,128]{3,2,1,0:T(8,128)(2,1)}, bf16[12,2,64,128]{3,2,1,0:T(8,128)(2,1)S(1)}, u32[]{:S(2)}, u32[]{:S(2)}) collective-permute-start(bf16[12,2,64,128]{3,2,1,0:T(8,128)(2,1)} %get-tuple-element.78), channel_id=1, source_target_pairs={{0,4},{2,6},{4,8},{6,10},{8,12},{10,14},{12,0},{14,2},{1,5},{3,7},... | collective-permute-start | bytes 1179656 | tf_op jit(solution)/shard_map/ppermute | solution.py:287
  138.7 27.5 %collective-permute-start.9 = (bf16[12,2,64,128]{3,2,1,0:T(8,128)(2,1)}, bf16[12,2,64,128]{3,2,1,0:T(8,128)(2,1)S(1)}, u32[]{:S(2)}, u32[]{:S(2)}) collective-permute-start(bf16[12,2,64,128]{3,2,1,0:T(8,128)(2,1)} %get-tuple-element.79), channel_id=1, source_target_pairs={{0,12},{2,14},{4,0},{6,2},{8,4},{10,6},{12,8},{14,10},{1,13},{3,15... | collective-permute-start | bytes 1179656 | tf_op jit(solution)/shard_map/ppermute | solution.py:287
  140.0 50.6 %collective-permute-start.10 = (bf16[12,2,64,128]{3,2,1,0:T(8,128)(2,1)}, bf16[12,2,64,128]{3,2,1,0:T(8,128)(2,1)S(1)}, u32[]{:S(2)}, u32[]{:S(2)}) collective-permute-start(bf16[12,2,64,128]{3,2,1,0:T(8,128)(2,1)} %get-tuple-element.80), channel_id=1, source_target_pairs={{0,2},{2,4},{4,6},{6,8},{8,10},{10,12},{12,14},{14,0},{1,3},{3,5},... | collective-permute-start | bytes 1179656 | tf_op jit(solution)/shard_map/ppermute | solution.py:287
  141.9 48.6 %collective-permute-start.11 = (bf16[12,2,64,128]{3,2,1,0:T(8,128)(2,1)}, bf16[12,2,64,128]{3,2,1,0:T(8,128)(2,1)S(1)}, u32[]{:S(2)}, u32[]{:S(2)}) collective-permute-start(bf16[12,2,64,128]{3,2,1,0:T(8,128)(2,1)} %get-tuple-element.81), channel_id=1, source_target_pairs={{0,14},{2,0},{4,2},{6,4},{8,6},{10,8},{12,10},{14,12},{1,15},{3,1}... | collective-permute-start | bytes 1179656 | tf_op jit(solution)/shard_map/ppermute | solution.py:287
  151.8 62.5 %collective-permute-start.12 = (bf16[12,2,64,128]{3,2,1,0:T(8,128)(2,1)}, bf16[12,2,64,128]{3,2,1,0:T(8,128)(2,1)S(1)}, u32[]{:S(2)}, u32[]{:S(2)}) collective-permute-start(bf16[12,2,64,128]{3,2,1,0:T(8,128)(2,1)} %get-tuple-element.87), channel_id=1, source_target_pairs={{0,8},{2,10},{4,12},{6,14},{8,0},{10,2},{12,4},{14,6},{1,9},{3,11}... | collective-permute-start | bytes 1179656 | tf_op jit(solution)/shard_map/ppermute | solution.py:287
  166.2 50.7 %collective-permute-start.13 = (bf16[12,2,64,128]{3,2,1,0:T(8,128)(2,1)}, bf16[12,2,64,128]{3,2,1,0:T(8,128)(2,1)S(1)}, u32[]{:S(2)}, u32[]{:S(2)}) collective-permute-start(bf16[12,2,64,128]{3,2,1,0:T(8,128)(2,1)} %get-tuple-element.88), channel_id=1, source_target_pairs={{0,6},{2,8},{4,10},{6,12},{8,14},{10,0},{12,2},{14,4},{1,7},{3,9},... | collective-permute-start | bytes 1179656 | tf_op jit(solution)/shard_map/ppermute | solution.py:287
  166.2 50.7 %collective-permute-start.14 = (bf16[12,2,64,128]{3,2,1,0:T(8,128)(2,1)}, bf16[12,2,64,128]{3,2,1,0:T(8,128)(2,1)S(1)}, u32[]{:S(2)}, u32[]{:S(2)}) collective-permute-start(bf16[12,2,64,128]{3,2,1,0:T(8,128)(2,1)} %get-tuple-element.89), channel_id=1, source_target_pairs={{0,10},{2,12},{4,14},{6,0},{8,2},{10,4},{12,6},{14,8},{1,11},{3,13... | collective-permute-start | bytes 1179656 | tf_op jit(solution)/shard_map/ppermute | solution.py:287
  225.6 29.9 %all-to-all-start.3 = ((f32[8,96,128]{2,1,0:T(8,128)}), f32[8,96,128]{2,1,0:T(8,128)S(1)}, u32[]{:S(2)}, u32[]{:S(2)}) async-start(f32[8,96,128]{2,1,0:T(8,128)} %bitcast.16), calls=%async_computation.3 | async-start | bytes 786432 | tf_op jit(solution)/shard_map/all_to_all | solution.py:280
  238.7 28.2 %collective-permute-start.18 = (bf16[12,2,64,128]{3,2,1,0:T(8,128)(2,1)}, bf16[12,2,64,128]{3,2,1,0:T(8,128)(2,1)S(1)}, u32[]{:S(2)}, u32[]{:S(2)}) collective-permute-start(bf16[12,2,64,128]{3,2,1,0:T(8,128)(2,1)} %get-tuple-element.101), channel_id=1, source_target_pairs={{0,12},{2,14},{4,0},{6,2},{8,4},{10,6},{12,8},{14,10},{1,13},{3,15... | collective-permute-start | bytes 1179656 | tf_op jit(solution)/shard_map/ppermute | solution.py:287
  242.8 26.3 %collective-permute-start.19 = (bf16[12,2,64,128]{3,2,1,0:T(8,128)(2,1)}, bf16[12,2,64,128]{3,2,1,0:T(8,128)(2,1)S(1)}, u32[]{:S(2)}, u32[]{:S(2)}) collective-permute-start(bf16[12,2,64,128]{3,2,1,0:T(8,128)(2,1)} %get-tuple-element.102), channel_id=1, source_target_pairs={{0,4},{2,6},{4,8},{6,10},{8,12},{10,14},{12,0},{14,2},{1,5},{3,7},... | collective-permute-start | bytes 1179656 | tf_op jit(solution)/shard_map/ppermute | solution.py:287
  242.8 40.6 %collective-permute-start.20 = (bf16[12,2,64,128]{3,2,1,0:T(8,128)(2,1)}, bf16[12,2,64,128]{3,2,1,0:T(8,128)(2,1)S(1)}, u32[]{:S(2)}, u32[]{:S(2)}) collective-permute-start(bf16[12,2,64,128]{3,2,1,0:T(8,128)(2,1)} %get-tuple-element.103), channel_id=1, source_target_pairs={{0,14},{2,0},{4,2},{6,4},{8,6},{10,8},{12,10},{14,12},{1,15},{3,1}... | collective-permute-start | bytes 1179656 | tf_op jit(solution)/shard_map/ppermute | solution.py:287
  246.1 43.7 %collective-permute-start.21 = (bf16[12,2,64,128]{3,2,1,0:T(8,128)(2,1)}, bf16[12,2,64,128]{3,2,1,0:T(8,128)(2,1)S(1)}, u32[]{:S(2)}, u32[]{:S(2)}) collective-permute-start(bf16[12,2,64,128]{3,2,1,0:T(8,128)(2,1)} %get-tuple-element.104), channel_id=1, source_target_pairs={{0,2},{2,4},{4,6},{6,8},{8,10},{10,12},{12,14},{14,0},{1,3},{3,5},... | collective-permute-start | bytes 1179656 | tf_op jit(solution)/shard_map/ppermute | solution.py:287
  256.3 56.5 %collective-permute-start.15 = (bf16[12,2,64,128]{3,2,1,0:T(8,128)(2,1)}, bf16[12,2,64,128]{3,2,1,0:T(8,128)(2,1)S(1)}, u32[]{:S(2)}, u32[]{:S(2)}) collective-permute-start(bf16[12,2,64,128]{3,2,1,0:T(8,128)(2,1)} %get-tuple-element.94), channel_id=1, source_target_pairs={{0,8},{2,10},{4,12},{6,14},{8,0},{10,2},{12,4},{14,6},{1,9},{3,11}... | collective-permute-start | bytes 1179656 | tf_op jit(solution)/shard_map/ppermute | solution.py:287
  266.9 45.8 %collective-permute-start.16 = (bf16[12,2,64,128]{3,2,1,0:T(8,128)(2,1)}, bf16[12,2,64,128]{3,2,1,0:T(8,128)(2,1)S(1)}, u32[]{:S(2)}, u32[]{:S(2)}) collective-permute-start(bf16[12,2,64,128]{3,2,1,0:T(8,128)(2,1)} %get-tuple-element.95), channel_id=1, source_target_pairs={{0,10},{2,12},{4,14},{6,0},{8,2},{10,4},{12,6},{14,8},{1,11},{3,13... | collective-permute-start | bytes 1179656 | tf_op jit(solution)/shard_map/ppermute | solution.py:287
  269.2 43.6 %collective-permute-start.17 = (bf16[12,2,64,128]{3,2,1,0:T(8,128)(2,1)}, bf16[12,2,64,128]{3,2,1,0:T(8,128)(2,1)S(1)}, u32[]{:S(2)}, u32[]{:S(2)}) collective-permute-start(bf16[12,2,64,128]{3,2,1,0:T(8,128)(2,1)} %get-tuple-element.96), channel_id=1, source_target_pairs={{0,6},{2,8},{4,10},{6,12},{8,14},{10,0},{12,2},{14,4},{1,7},{3,9},... | collective-permute-start | bytes 1179656 | tf_op jit(solution)/shard_map/ppermute | solution.py:287
  317.7 64.6 %all-to-all-start.4 = ((bf16[16,2,128,128]{3,2,1,0:T(8,128)(2,1)}), bf16[16,2,128,128]{3,2,1,0:T(8,128)(2,1)S(1)}, u32[]{:S(2)}, u32[]{:S(2)}) async-start(bf16[16,2,128,128]{3,2,1,0:T(8,128)(2,1)} %unpack.2), calls=%async_computation.4 | async-start | bytes 2097152 | tf_op jit(solution)/shard_map/all_to_all | solution.py:280
  325.0 30.7 %collective-permute-start.22 = (bf16[12,2,64,128]{3,2,1,0:T(8,128)(2,1)}, bf16[12,2,64,128]{3,2,1,0:T(8,128)(2,1)S(1)}, u32[]{:S(2)}, u32[]{:S(2)}) collective-permute-start(bf16[12,2,64,128]{3,2,1,0:T(8,128)(2,1)} %get-tuple-element.114), channel_id=1, source_target_pairs={{0,8},{2,10},{4,12},{6,14},{8,0},{10,2},{12,4},{14,6},{1,9},{3,11}... | collective-permute-start | bytes 1179656 | tf_op jit(solution)/shard_map/ppermute | solution.py:287
  341.4 28.2 %collective-permute-start.24 = (bf16[12,2,64,128]{3,2,1,0:T(8,128)(2,1)}, bf16[12,2,64,128]{3,2,1,0:T(8,128)(2,1)S(1)}, u32[]{:S(2)}, u32[]{:S(2)}) collective-permute-start(bf16[12,2,64,128]{3,2,1,0:T(8,128)(2,1)} %get-tuple-element.116), channel_id=1, source_target_pairs={{0,6},{2,8},{4,10},{6,12},{8,14},{10,0},{12,2},{14,4},{1,7},{3,9},... | collective-permute-start | bytes 1179656 | tf_op jit(solution)/shard_map/ppermute | solution.py:287
  345.2 26.8 %collective-permute-start.25 = (bf16[12,2,64,128]{3,2,1,0:T(8,128)(2,1)}, bf16[12,2,64,128]{3,2,1,0:T(8,128)(2,1)S(1)}, u32[]{:S(2)}, u32[]{:S(2)}) collective-permute-start(bf16[12,2,64,128]{3,2,1,0:T(8,128)(2,1)} %get-tuple-element.117), channel_id=1, source_target_pairs={{0,12},{2,14},{4,0},{6,2},{8,4},{10,6},{12,8},{14,10},{1,13},{3,15... | collective-permute-start | bytes 1179656 | tf_op jit(solution)/shard_map/ppermute | solution.py:287
  345.3 26.8 %collective-permute-start.26 = (bf16[12,2,64,128]{3,2,1,0:T(8,128)(2,1)}, bf16[12,2,64,128]{3,2,1,0:T(8,128)(2,1)}, u32[]{:S(2)}, u32[]{:S(2)}) collective-permute-start(bf16[12,2,64,128]{3,2,1,0:T(8,128)(2,1)} %get-tuple-element.118), channel_id=1, source_target_pairs={{0,4},{2,6},{4,8},{6,10},{8,12},{10,14},{12,0},{14,2},{1,5},{3,7},... | collective-permute-start | bytes 1179656 | tf_op jit(solution)/shard_map/ppermute | solution.py:287
  355.7 20.6 %collective-permute-start.27 = (bf16[12,2,64,128]{3,2,1,0:T(8,128)(2,1)}, bf16[12,2,64,128]{3,2,1,0:T(8,128)(2,1)}, u32[]{:S(2)}, u32[]{:S(2)}) collective-permute-start(bf16[12,2,64,128]{3,2,1,0:T(8,128)(2,1)} %get-tuple-element.119), channel_id=1, source_target_pairs={{0,14},{2,0},{4,2},{6,4},{8,6},{10,8},{12,10},{14,12},{1,15},{3,1}... | collective-permute-start | bytes 1179656 | tf_op jit(solution)/shard_map/ppermute | solution.py:287
  369.6 19.9 %collective-permute-start.29 = (bf16[16,2,128,128]{3,2,1,0:T(8,128)(2,1)}, bf16[16,2,128,128]{3,2,1,0:T(8,128)(2,1)S(1)}, u32[]{:S(2)}, u32[]{:S(2)}) collective-permute-start(bf16[16,2,128,128]{3,2,1,0:T(8,128)(2,1)} %get-tuple-element.121), channel_id=1, source_target_pairs={{0,1},{1,0},{2,3},{3,2},{4,5},{5,4},{6,7},{7,6},{8,9},{9,8},{10,11... | collective-permute-start | bytes 3145736 | tf_op jit(solution)/shard_map/ppermute | solution.py:405
  (37 other events, 344.6 us)

commit v6 on v5

--- a/solution.py
+++ b/solution.py
@@ -18,7 +18,7 @@
 INST = 64
 SPANS = INST // 2
 BLK = 16
-UNROLL = 4
+UNROLL = 8
 UNROLL_STATS = 8
 COST = 1 << 10
 LIST = 104

time: 411 us -> 411 us (level); the launches traced: 404 us -> 411 us
  waiting for transfers between devices: 151 us -> 174 us
  Pallas kernels: 96.2 us -> 86.6 us
  starting transfers between devices: 112 us -> 106 us
    ppermute x28, waiting for transfers between devices: 133 us -> 154 us  [ring_send(): got[d] = lax.ppermute(parts[d], 'grp', pairs)]
    pallas_call x2, Pallas kernels: 44.4 us -> 36.6 us  [on_device(): pl.pallas_call(functools.partial(grad_kernel, pair), out_shape=[shape(PAR...]
  transfers between devices with their start and end apart: 37 -> 37, of which waited for: 19 -> 21; matrix products, arithmetic and copies ran while one was open for 1% -> 1% of each run, Pallas kernels for 19% -> 17%
where the time goes in v6:
time: 411 us
  waiting for transfers between devices  174 us (42%)
  starting transfers between devices  106 us (26%)
  Pallas kernels  86.6 us (21%)
  blocking collectives  19.6 us (5%)
  local copies, waits for them, and re-layouts  16.5 us (4%)
  other arithmetic  6.83 us (2%)
    ppermute x28, waiting for transfers between devices, ring_send(): got[d] = lax.ppermute(parts[d], 'grp', pairs)  154 us
    ppermute x28, starting transfers between devices, ring_send(): got[d] = lax.ppermute(parts[d], 'grp', pairs)  59.5 us
    all_to_all x6, starting transfers between devices, exchange(): return lax.all_to_all(rows, axis, split_axis=0, concat_axis=0, tiled=True)  46.7 us
    pallas_call x2, Pallas kernels, on_device(): pl.pallas_call(functools.partial(grad_kernel, pair), out_shape=[shape(PAR...  36.6 us
    all_to_all x6, waiting for transfers between devices, exchange(): return lax.all_to_all(rows, axis, split_axis=0, concat_axis=0, tiled=True)  20.2 us
    all_gather x1, blocking collectives, on_device(): all_names = lax.all_gather(names.reshape(1, 2 * INST), 'grp', tiled=True)  19.6 us
    pallas_call x2, Pallas kernels, on_device(): pl.pallas_call(functools.partial(stat_kernel, pair), out_shape=shape((RIN...  13.7 us
    unnamed x66, local copies, waits for them, and re-layouts  10.3 us
  transfers between devices with their start and end apart: 37, of which 21 were waited for; matrix products, arithmetic and copies ran while one was open for 1% of the time, Pallas kernels for 17%

profile of v6, /device:TPU:2, one launch (start us, length us, event | category | flops | bytes accessed | tf_op | source)
XLA Modules:
  0.0 411.3 jit_solution(291665304791175582)
XLA Ops:
  7.6 7.5 %all-to-all-start.1 = ((bf16[16,2,128,128]{3,2,1,0:T(8,128)(2,1)}), bf16[16,2,128,128]{3,2,1,0:T(8,128)(2,1)S(1)}, u32[]{:S(2)}, u32[]{:S(2)}) async-start(bf16[16,2,128,128]{3,2,1,0:T(8,128)(2,1)} %pad_maximum_fusion.1), calls=%async_computation.1 | async-start | bytes 2097152 | tf_op jit(solution)/shard_map/all_to_all | solution.py:280
  15.5 19.6 %all-gather.1 = s32[8,1,128]{2,1,0:T(1,128)} all-gather(s32[1,1,128]{2,1,0:T(1,128)S(1)} %fusion.4), channel_id=2, replica_groups=mesh['seq'=16,'grp'=8,'store'=2] {'grp'}, dimensions={0}, use_global_device_ids=true | all-gather | bytes 4608 | tf_op jit(solution)/shard_map/all_gather | solution.py:321
  37.4 7.2 %all-to-all-start = ((bf16[16,2,128,128]{3,2,1,0:T(8,128)(2,1)}), bf16[16,2,128,128]{3,2,1,0:T(8,128)(2,1)}, u32[]{:S(2)}, u32[]{:S(2)}) async-start(bf16[16,2,128,128]{3,2,1,0:T(8,128)(2,1)} %pad_maximum_fusion), calls=%async_computation | async-start | bytes 2097152 | tf_op jit(solution)/shard_map/all_to_all | solution.py:280
  47.3 4.0 pack.2
  62.8 14.9 %collective-permute-done.1.refs_1_ = bf16[12,2,64,128]{3,2,1,0:T(8,128)(2,1)S(1)} collective-permute-done((bf16[12,2,64,128]{3,2,1,0:T(8,128)(2,1)}, bf16[12,2,64,128]{3,2,1,0:T(8,128)(2,1)S(1)}, u32[]{:S(2)}, u32[]{:S(2)}) %collective-permute-start.1) | collective-permute-done | bytes 393248 | tf_op jit(solution)/shard_map/ppermute | solution.py:287
  77.7 23.4 %collective-permute-done.2.refs_2_ = bf16[12,2,64,128]{3,2,1,0:T(8,128)(2,1)S(1)} collective-permute-done((bf16[12,2,64,128]{3,2,1,0:T(8,128)(2,1)}, bf16[12,2,64,128]{3,2,1,0:T(8,128)(2,1)S(1)}, u32[]{:S(2)}, u32[]{:S(2)}) %collective-permute-start.2) | collective-permute-done | bytes 393248 | tf_op jit(solution)/shard_map/ppermute | solution.py:287
  101.0 10.3 %recv_table.1.refs_0_.table = s32[640]{0:T(1024)} custom-call(s32[2]{0:T(128)} %pad_add_fusion.place, s32[8,128]{1,0:T(8,128)} %bitcast.26), custom_call_target="tpu_custom_call" | custom-call | bytes 1024 | tf_op jit(solution)/shard_map/recv_table/pallas_call | solution.py:343
  114.9 4.0 pack.3
  120.9 6.9 %stats.2.refs_0_ = f32[768,128]{1,0:T(8,128)} custom-call(s32[2]{0:T(128)} %pad_add_fusion.place, s32[640]{0:T(1024)} %recv_table.1.refs_0_.table, bf16[12,2,64,128]{3,2,1,0:T(8,128)(2,1)} %get-tuple-element.71.refs_0_, bf16[12,2,64,128]{3,2,1,0:T(8,128)(2,1)} %copy-done.2, bf16[12,2,64,128]{3,2,1,0:T(8,128)(2,1)} %copy-done.3, ...), custom_call_target="tpu_custom_call" | custom-call | flops 1024 | bytes 1024 | tf_op jit(solution)/shard_map/stats/pallas_call | solution.py:363
  127.7 7.1 %all-to-all-start.2 = ((f32[8,96,128]{2,1,0:T(8,128)}), f32[8,96,128]{2,1,0:T(8,128)S(1)}, u32[]{:S(2)}, u32[]{:S(2)}) async-start(f32[8,96,128]{2,1,0:T(8,128)} %bitcast.15), calls=%async_computation.2 | async-start | bytes 786432 | tf_op jit(solution)/shard_map/all_to_all | solution.py:280
  142.3 7.8 %all-to-all-done.2 = f32[8,96,128]{2,1,0:T(8,128)S(1)} async-done(((f32[8,96,128]{2,1,0:T(8,128)}), f32[8,96,128]{2,1,0:T(8,128)S(1)}, u32[]{:S(2)}, u32[]{:S(2)}) %all-to-all-start.2) | async-done | bytes 393248 | tf_op jit(solution)/shard_map/all_to_all | solution.py:280
  152.4 12.8 %collective-permute-done.8.refs_10_.refs_4_ = bf16[12,2,64,128]{3,2,1,0:T(8,128)(2,1)S(1)} collective-permute-done((bf16[12,2,64,128]{3,2,1,0:T(8,128)(2,1)}, bf16[12,2,64,128]{3,2,1,0:T(8,128)(2,1)S(1)}, u32[]{:S(2)}, u32[]{:S(2)}) %collective-permute-start.8) | collective-permute-done | bytes 393248 | tf_op jit(solution)/shard_map/ppermute | solution.py:287
  165.3 5.0 %collective-permute-start.14 = (bf16[12,2,64,128]{3,2,1,0:T(8,128)(2,1)}, bf16[12,2,64,128]{3,2,1,0:T(8,128)(2,1)S(1)}, u32[]{:S(2)}, u32[]{:S(2)}) collective-permute-start(bf16[12,2,64,128]{3,2,1,0:T(8,128)(2,1)} %get-tuple-element.89), channel_id=1, source_target_pairs={{0,10},{2,12},{4,14},{6,0},{8,2},{10,4},{12,6},{14,8},{1,11},{3,13... | collective-permute-start | bytes 1179656 | tf_op jit(solution)/shard_map/ppermute | solution.py:287
  170.3 19.4 %collective-permute-done.10.refs_12_.refs_6_ = bf16[12,2,64,128]{3,2,1,0:T(8,128)(2,1)S(1)} collective-permute-done((bf16[12,2,64,128]{3,2,1,0:T(8,128)(2,1)}, bf16[12,2,64,128]{3,2,1,0:T(8,128)(2,1)S(1)}, u32[]{:S(2)}, u32[]{:S(2)}) %collective-permute-start.10) | collective-permute-done | bytes 393248 | tf_op jit(solution)/shard_map/ppermute | solution.py:287
  191.2 18.3 %grads.2 = (bf16[12,2,64,128]{3,2,1,0:T(8,128)(2,1)}, bf16[12,2,64,128]{3,2,1,0:T(8,128)(2,1)}, bf16[12,2,64,128]{3,2,1,0:T(8,128)(2,1)}, bf16[12,2,64,128]{3,2,...) custom-call(s32[2]{0:T(128)} %pad_add_fusion.place, ...), custom_call_target="tpu_custom_call" | custom-call | flops 1024 | bytes 1024 | tf_op jit(solution)/shard_map/grads/pallas_call | solution.py:383
  209.4 6.5 %collective-permute-done.13.refs_2_ = bf16[12,2,64,128]{3,2,1,0:T(8,128)(2,1)S(1)} collective-permute-done((bf16[12,2,64,128]{3,2,1,0:T(8,128)(2,1)}, bf16[12,2,64,128]{3,2,1,0:T(8,128)(2,1)S(1)}, u32[]{:S(2)}, u32[]{:S(2)}) %collective-permute-start.13) | collective-permute-done | bytes 393248 | tf_op jit(solution)/shard_map/ppermute | solution.py:287
  216.9 6.9 %stats.3.refs_0_ = f32[768,128]{1,0:T(8,128)} custom-call(s32[2]{0:T(128)} %pad_add_fusion.place, s32[640]{0:T(1024)} %recv_table.1.refs_0_.table, bf16[12,2,64,128]{3,2,1,0:T(8,128)(2,1)} %get-tuple-element.83.refs_0_, bf16[12,2,64,128]{3,2,1,0:T(8,128)(2,1)} %copy-done.17, bf16[12,2,64,128]{3,2,1,0:T(8,128)(2,1)} %copy-done.18, ...), custom_call_target="tpu_custom_call" | custom-call | flops 1024 | bytes 1024 | tf_op jit(solution)/shard_map/stats/pallas_call | solution.py:363
  223.7 10.3 %all-to-all-start.3 = ((f32[8,96,128]{2,1,0:T(8,128)}), f32[8,96,128]{2,1,0:T(8,128)S(1)}, u32[]{:S(2)}, u32[]{:S(2)}) async-start(f32[8,96,128]{2,1,0:T(8,128)} %bitcast.16), calls=%async_computation.3 | async-start | bytes 786432 | tf_op jit(solution)/shard_map/all_to_all | solution.py:280
  234.1 4.1 %collective-permute-start.18 = (bf16[12,2,64,128]{3,2,1,0:T(8,128)(2,1)}, bf16[12,2,64,128]{3,2,1,0:T(8,128)(2,1)S(1)}, u32[]{:S(2)}, u32[]{:S(2)}) collective-permute-start(bf16[12,2,64,128]{3,2,1,0:T(8,128)(2,1)} %get-tuple-element.101), channel_id=1, source_target_pairs={{0,12},{2,14},{4,0},{6,2},{8,4},{10,6},{12,8},{14,10},{1,13},{3,15... | collective-permute-start | bytes 1179656 | tf_op jit(solution)/shard_map/ppermute | solution.py:287
  241.5 10.9 %all-to-all-done.3 = f32[8,96,128]{2,1,0:T(8,128)S(1)} async-done(((f32[8,96,128]{2,1,0:T(8,128)}), f32[8,96,128]{2,1,0:T(8,128)S(1)}, u32[]{:S(2)}, u32[]{:S(2)}) %all-to-all-start.3) | async-done | bytes 393248 | tf_op jit(solution)/shard_map/all_to_all | solution.py:280
  253.1 4.1 %collective-permute-done.18.refs_10_.refs_4_.refs_0_ = bf16[12,2,64,128]{3,2,1,0:T(8,128)(2,1)S(1)} collective-permute-done((bf16[12,2,64,128]{3,2,1,0:T(8,128)(2,1)}, bf16[12,2,64,128]{3,2,1,0:T(8,128)(2,1)S(1)}, u32[]{:S(2)}, u32[]{:S(2)}) %collective-permute-start.18) | collective-permute-done | bytes 393248 | tf_op jit(solution)/shard_map/ppermute | solution.py:287
  257.2 6.2 %collective-permute-start.16 = (bf16[12,2,64,128]{3,2,1,0:T(8,128)(2,1)}, bf16[12,2,64,128]{3,2,1,0:T(8,128)(2,1)S(1)}, u32[]{:S(2)}, u32[]{:S(2)}) collective-permute-start(bf16[12,2,64,128]{3,2,1,0:T(8,128)(2,1)} %get-tuple-element.95), channel_id=1, source_target_pairs={{0,10},{2,12},{4,14},{6,0},{8,2},{10,4},{12,6},{14,8},{1,11},{3,13... | collective-permute-start | bytes 1179656 | tf_op jit(solution)/shard_map/ppermute | solution.py:287
  264.5 14.7 %collective-permute-done.20.refs_12_.refs_6_.refs_2_ = bf16[12,2,64,128]{3,2,1,0:T(8,128)(2,1)S(1)} collective-permute-done((bf16[12,2,64,128]{3,2,1,0:T(8,128)(2,1)}, bf16[12,2,64,128]{3,2,1,0:T(8,128)(2,1)S(1)}, u32[]{:S(2)}, u32[]{:S(2)}) %collective-permute-start.20) | collective-permute-done | bytes 393248 | tf_op jit(solution)/shard_map/ppermute | solution.py:287
  279.2 6.4 %collective-permute-done.21.refs_13_.refs_7_.refs_3_ = bf16[12,2,64,128]{3,2,1,0:T(8,128)(2,1)S(1)} collective-permute-done((bf16[12,2,64,128]{3,2,1,0:T(8,128)(2,1)}, bf16[12,2,64,128]{3,2,1,0:T(8,128)(2,1)S(1)}, u32[]{:S(2)}, u32[]{:S(2)}) %collective-permute-start.21) | collective-permute-done | bytes 393248 | tf_op jit(solution)/shard_map/ppermute | solution.py:287
  286.4 18.3 %grads.3 = (bf16[12,2,64,128]{3,2,1,0:T(8,128)(2,1)}, bf16[12,2,64,128]{3,2,1,0:T(8,128)(2,1)}, bf16[12,2,64,128]{3,2,1,0:T(8,128)(2,1)}, bf16[12,2,64,128]{3,2,...) custom-call(s32[2]{0:T(128)} %pad_add_fusion.place, ...), custom_call_target="tpu_custom_call" | custom-call | flops 1024 | bytes 1024 | tf_op jit(solution)/shard_map/grads/pallas_call | solution.py:383
  312.9 7.3 %all-to-all-start.4 = ((bf16[16,2,128,128]{3,2,1,0:T(8,128)(2,1)}), bf16[16,2,128,128]{3,2,1,0:T(8,128)(2,1)S(1)}, u32[]{:S(2)}, u32[]{:S(2)}) async-start(bf16[16,2,128,128]{3,2,1,0:T(8,128)(2,1)} %unpack.2), calls=%async_computation.4 | async-start | bytes 2097152 | tf_op jit(solution)/shard_map/all_to_all | solution.py:280
  320.2 8.9 %collective-permute-start.22 = (bf16[12,2,64,128]{3,2,1,0:T(8,128)(2,1)}, bf16[12,2,64,128]{3,2,1,0:T(8,128)(2,1)S(1)}, u32[]{:S(2)}, u32[]{:S(2)}) collective-permute-start(bf16[12,2,64,128]{3,2,1,0:T(8,128)(2,1)} %get-tuple-element.114), channel_id=1, source_target_pairs={{0,8},{2,10},{4,12},{6,14},{8,0},{10,2},{12,4},{14,6},{1,9},{3,11}... | collective-permute-start | bytes 1179656 | tf_op jit(solution)/shard_map/ppermute | solution.py:287
  336.6 10.7 %collective-permute-done.22.refs_1_ = bf16[12,2,64,128]{3,2,1,0:T(8,128)(2,1)S(1)} collective-permute-done((bf16[12,2,64,128]{3,2,1,0:T(8,128)(2,1)}, bf16[12,2,64,128]{3,2,1,0:T(8,128)(2,1)S(1)}, u32[]{:S(2)}, u32[]{:S(2)}) %collective-permute-start.22) | collective-permute-done | bytes 393248 | tf_op jit(solution)/shard_map/ppermute | solution.py:287
  350.1 22.5 %collective-permute-done.23.refs_2_ = bf16[12,2,64,128]{3,2,1,0:T(8,128)(2,1)S(1)} collective-permute-done((bf16[12,2,64,128]{3,2,1,0:T(8,128)(2,1)}, bf16[12,2,64,128]{3,2,1,0:T(8,128)(2,1)S(1)}, u32[]{:S(2)}, u32[]{:S(2)}) %collective-permute-start.23) | collective-permute-done | bytes 393248 | tf_op jit(solution)/shard_map/ppermute | solution.py:287
  376.3 4.6 %collective-permute-done.26.refs_5_ = bf16[12,2,64,128]{3,2,1,0:T(8,128)(2,1)} collective-permute-done((bf16[12,2,64,128]{3,2,1,0:T(8,128)(2,1)}, bf16[12,2,64,128]{3,2,1,0:T(8,128)(2,1)}, u32[]{:S(2)}, u32[]{:S(2)}) %collective-permute-start.26) | collective-permute-done | bytes 393248 | tf_op jit(solution)/shard_map/ppermute | solution.py:287
  389.1 7.2 %all-to-all-start.5 = ((bf16[16,2,128,128]{3,2,1,0:T(8,128)(2,1)}), bf16[16,2,128,128]{3,2,1,0:T(8,128)(2,1)S(1)}, u32[]{:S(2)}, u32[]{:S(2)}) async-start(bf16[16,2,128,128]{3,2,1,0:T(8,128)(2,1)} %unpack.3), calls=%async_computation.5 | async-start | bytes 2097152 | tf_op jit(solution)/shard_map/all_to_all | solution.py:280
  397.3 10.1 %join.1 = bf16[16,2,2,2,128,128]{5,4,3,2,1,0:T(8,128)(2,1)} custom-call(s32[2]{0:T(128)} %pad_add_fusion.place, bf16[16,2,128,128]{3,2,1,0:T(8,128)(2,1)} %get-tuple-element.90.refs_10_.keep0, bf16[16,2,128,128]{3,2,1,0:T(8,128)(2,1)} %get-tuple-element.105.refs_8_.keep1, bf16[16,2,128,128]{3,2,1,0:T(8,128)(2,1)} %copy-done.23, ...), custom_call_target="tpu_custom_call" | custom-call | bytes 1024 | tf_op jit(solution)/shard_map/join/pallas_call | solution.py:426
  (137 shorter events, 82.3 us)
Async XLA Ops:
  7.6 38.4 %collective-permute-start = (bf16[16,2,2,128,128]{4,3,2,1,0:T(8,128)(2,1)}, bf16[16,2,2,128,128]{4,3,2,1,0:T(8,128)(2,1)S(1)}, u32[]{:S(2)}, u32[]{:S(2)}) collective-permute-start(bf16[16,2,2,128,128]{4,3,2,1,0:T(8,128)(2,1)} %dynamic-slice_bitcast_fusion), channel_id=1, source_target_pairs={{0,1},{1,0},{2,3},{3,2},{4,5},{5,4},{6,7},{7,6},{8,9},{9,8},{10,11... | collective-permute-start | bytes 6291464 | tf_op jit(solution)/shard_map/ppermute | solution.py:316
  7.6 29.9 %all-to-all-start.1 = ((bf16[16,2,128,128]{3,2,1,0:T(8,128)(2,1)}), bf16[16,2,128,128]{3,2,1,0:T(8,128)(2,1)S(1)}, u32[]{:S(2)}, u32[]{:S(2)}) async-start(bf16[16,2,128,128]{3,2,1,0:T(8,128)(2,1)} %pad_maximum_fusion.1), calls=%async_computation.1 | async-start | bytes 2097152 | tf_op jit(solution)/shard_map/all_to_all | solution.py:280
  37.4 73.9 %all-to-all-start = ((bf16[16,2,128,128]{3,2,1,0:T(8,128)(2,1)}), bf16[16,2,128,128]{3,2,1,0:T(8,128)(2,1)}, u32[]{:S(2)}, u32[]{:S(2)}) async-start(bf16[16,2,128,128]{3,2,1,0:T(8,128)(2,1)} %pad_maximum_fusion), calls=%async_computation | async-start | bytes 2097152 | tf_op jit(solution)/shard_map/all_to_all | solution.py:280
  51.3 26.4 %collective-permute-start.1 = (bf16[12,2,64,128]{3,2,1,0:T(8,128)(2,1)}, bf16[12,2,64,128]{3,2,1,0:T(8,128)(2,1)S(1)}, u32[]{:S(2)}, u32[]{:S(2)}) collective-permute-start(bf16[12,2,64,128]{3,2,1,0:T(8,128)(2,1)} %get-tuple-element.65), channel_id=1, source_target_pairs={{0,8},{2,10},{4,12},{6,14},{8,0},{10,2},{12,4},{14,6},{1,9},{3,11}... | collective-permute-start | bytes 1179656 | tf_op jit(solution)/shard_map/ppermute | solution.py:287
  53.6 47.5 %collective-permute-start.2 = (bf16[12,2,64,128]{3,2,1,0:T(8,128)(2,1)}, bf16[12,2,64,128]{3,2,1,0:T(8,128)(2,1)S(1)}, u32[]{:S(2)}, u32[]{:S(2)}) collective-permute-start(bf16[12,2,64,128]{3,2,1,0:T(8,128)(2,1)} %get-tuple-element.66), channel_id=1, source_target_pairs={{0,6},{2,8},{4,10},{6,12},{8,14},{10,0},{12,2},{14,4},{1,7},{3,9},... | collective-permute-start | bytes 1179656 | tf_op jit(solution)/shard_map/ppermute | solution.py:287
  54.9 56.4 %collective-permute-start.3 = (bf16[12,2,64,128]{3,2,1,0:T(8,128)(2,1)}, bf16[12,2,64,128]{3,2,1,0:T(8,128)(2,1)S(1)}, u32[]{:S(2)}, u32[]{:S(2)}) collective-permute-start(bf16[12,2,64,128]{3,2,1,0:T(8,128)(2,1)} %get-tuple-element.67), channel_id=1, source_target_pairs={{0,10},{2,12},{4,14},{6,0},{8,2},{10,4},{12,6},{14,8},{1,11},{3,13... | collective-permute-start | bytes 1179656 | tf_op jit(solution)/shard_map/ppermute | solution.py:287
  58.6 54.8 %collective-permute-start.4 = (bf16[12,2,64,128]{3,2,1,0:T(8,128)(2,1)}, bf16[12,2,64,128]{3,2,1,0:T(8,128)(2,1)S(1)}, u32[]{:S(2)}, u32[]{:S(2)}) collective-permute-start(bf16[12,2,64,128]{3,2,1,0:T(8,128)(2,1)} %get-tuple-element.68), channel_id=1, source_target_pairs={{0,4},{2,6},{4,8},{6,10},{8,12},{10,14},{12,0},{14,2},{1,5},{3,7},... | collective-permute-start | bytes 1179656 | tf_op jit(solution)/shard_map/ppermute | solution.py:287
  59.5 53.9 %collective-permute-start.5 = (bf16[12,2,64,128]{3,2,1,0:T(8,128)(2,1)}, bf16[12,2,64,128]{3,2,1,0:T(8,128)(2,1)S(1)}, u32[]{:S(2)}, u32[]{:S(2)}) collective-permute-start(bf16[12,2,64,128]{3,2,1,0:T(8,128)(2,1)} %get-tuple-element.69), channel_id=1, source_target_pairs={{0,12},{2,14},{4,0},{6,2},{8,4},{10,6},{12,8},{14,10},{1,13},{3,15... | collective-permute-start | bytes 1179656 | tf_op jit(solution)/shard_map/ppermute | solution.py:287
  77.7 42.3 %collective-permute-start.6 = (bf16[12,2,64,128]{3,2,1,0:T(8,128)(2,1)}, bf16[12,2,64,128]{3,2,1,0:T(8,128)(2,1)S(1)}, u32[]{:S(2)}, u32[]{:S(2)}) collective-permute-start(bf16[12,2,64,128]{3,2,1,0:T(8,128)(2,1)} %get-tuple-element.72), channel_id=1, source_target_pairs={{0,2},{2,4},{4,6},{6,8},{8,10},{10,12},{12,14},{14,0},{1,3},{3,5},... | collective-permute-start | bytes 1179656 | tf_op jit(solution)/shard_map/ppermute | solution.py:287
  134.8 30.4 %collective-permute-start.8 = (bf16[12,2,64,128]{3,2,1,0:T(8,128)(2,1)}, bf16[12,2,64,128]{3,2,1,0:T(8,128)(2,1)S(1)}, u32[]{:S(2)}, u32[]{:S(2)}) collective-permute-start(bf16[12,2,64,128]{3,2,1,0:T(8,128)(2,1)} %get-tuple-element.78), channel_id=1, source_target_pairs={{0,4},{2,6},{4,8},{6,10},{8,12},{10,14},{12,0},{14,2},{1,5},{3,7},... | collective-permute-start | bytes 1179656 | tf_op jit(solution)/shard_map/ppermute | solution.py:287
  137.8 27.5 %collective-permute-start.9 = (bf16[12,2,64,128]{3,2,1,0:T(8,128)(2,1)}, bf16[12,2,64,128]{3,2,1,0:T(8,128)(2,1)S(1)}, u32[]{:S(2)}, u32[]{:S(2)}) collective-permute-start(bf16[12,2,64,128]{3,2,1,0:T(8,128)(2,1)} %get-tuple-element.79), channel_id=1, source_target_pairs={{0,12},{2,14},{4,0},{6,2},{8,4},{10,6},{12,8},{14,10},{1,13},{3,15... | collective-permute-start | bytes 1179656 | tf_op jit(solution)/shard_map/ppermute | solution.py:287
  139.1 50.6 %collective-permute-start.10 = (bf16[12,2,64,128]{3,2,1,0:T(8,128)(2,1)}, bf16[12,2,64,128]{3,2,1,0:T(8,128)(2,1)S(1)}, u32[]{:S(2)}, u32[]{:S(2)}) collective-permute-start(bf16[12,2,64,128]{3,2,1,0:T(8,128)(2,1)} %get-tuple-element.80), channel_id=1, source_target_pairs={{0,2},{2,4},{4,6},{6,8},{8,10},{10,12},{12,14},{14,0},{1,3},{3,5},... | collective-permute-start | bytes 1179656 | tf_op jit(solution)/shard_map/ppermute | solution.py:287
  141.0 48.6 %collective-permute-start.11 = (bf16[12,2,64,128]{3,2,1,0:T(8,128)(2,1)}, bf16[12,2,64,128]{3,2,1,0:T(8,128)(2,1)S(1)}, u32[]{:S(2)}, u32[]{:S(2)}) collective-permute-start(bf16[12,2,64,128]{3,2,1,0:T(8,128)(2,1)} %get-tuple-element.81), channel_id=1, source_target_pairs={{0,14},{2,0},{4,2},{6,4},{8,6},{10,8},{12,10},{14,12},{1,15},{3,1}... | collective-permute-start | bytes 1179656 | tf_op jit(solution)/shard_map/ppermute | solution.py:287
  150.9 58.5 %collective-permute-start.12 = (bf16[12,2,64,128]{3,2,1,0:T(8,128)(2,1)}, bf16[12,2,64,128]{3,2,1,0:T(8,128)(2,1)S(1)}, u32[]{:S(2)}, u32[]{:S(2)}) collective-permute-start(bf16[12,2,64,128]{3,2,1,0:T(8,128)(2,1)} %get-tuple-element.87), channel_id=1, source_target_pairs={{0,8},{2,10},{4,12},{6,14},{8,0},{10,2},{12,4},{14,6},{1,9},{3,11}... | collective-permute-start | bytes 1179656 | tf_op jit(solution)/shard_map/ppermute | solution.py:287
  165.2 50.7 %collective-permute-start.13 = (bf16[12,2,64,128]{3,2,1,0:T(8,128)(2,1)}, bf16[12,2,64,128]{3,2,1,0:T(8,128)(2,1)S(1)}, u32[]{:S(2)}, u32[]{:S(2)}) collective-permute-start(bf16[12,2,64,128]{3,2,1,0:T(8,128)(2,1)} %get-tuple-element.88), channel_id=1, source_target_pairs={{0,6},{2,8},{4,10},{6,12},{8,14},{10,0},{12,2},{14,4},{1,7},{3,9},... | collective-permute-start | bytes 1179656 | tf_op jit(solution)/shard_map/ppermute | solution.py:287
  165.3 50.7 %collective-permute-start.14 = (bf16[12,2,64,128]{3,2,1,0:T(8,128)(2,1)}, bf16[12,2,64,128]{3,2,1,0:T(8,128)(2,1)S(1)}, u32[]{:S(2)}, u32[]{:S(2)}) collective-permute-start(bf16[12,2,64,128]{3,2,1,0:T(8,128)(2,1)} %get-tuple-element.89), channel_id=1, source_target_pairs={{0,10},{2,12},{4,14},{6,0},{8,2},{10,4},{12,6},{14,8},{1,11},{3,13... | collective-permute-start | bytes 1179656 | tf_op jit(solution)/shard_map/ppermute | solution.py:287
  223.7 28.6 %all-to-all-start.3 = ((f32[8,96,128]{2,1,0:T(8,128)}), f32[8,96,128]{2,1,0:T(8,128)S(1)}, u32[]{:S(2)}, u32[]{:S(2)}) async-start(f32[8,96,128]{2,1,0:T(8,128)} %bitcast.16), calls=%async_computation.3 | async-start | bytes 786432 | tf_op jit(solution)/shard_map/all_to_all | solution.py:280
  234.1 23.1 %collective-permute-start.18 = (bf16[12,2,64,128]{3,2,1,0:T(8,128)(2,1)}, bf16[12,2,64,128]{3,2,1,0:T(8,128)(2,1)S(1)}, u32[]{:S(2)}, u32[]{:S(2)}) collective-permute-start(bf16[12,2,64,128]{3,2,1,0:T(8,128)(2,1)} %get-tuple-element.101), channel_id=1, source_target_pairs={{0,12},{2,14},{4,0},{6,2},{8,4},{10,6},{12,8},{14,10},{1,13},{3,15... | collective-permute-start | bytes 1179656 | tf_op jit(solution)/shard_map/ppermute | solution.py:287
  238.2 25.2 %collective-permute-start.19 = (bf16[12,2,64,128]{3,2,1,0:T(8,128)(2,1)}, bf16[12,2,64,128]{3,2,1,0:T(8,128)(2,1)S(1)}, u32[]{:S(2)}, u32[]{:S(2)}) collective-permute-start(bf16[12,2,64,128]{3,2,1,0:T(8,128)(2,1)} %get-tuple-element.102), channel_id=1, source_target_pairs={{0,4},{2,6},{4,8},{6,10},{8,12},{10,14},{12,0},{14,2},{1,5},{3,7},... | collective-permute-start | bytes 1179656 | tf_op jit(solution)/shard_map/ppermute | solution.py:287
  238.2 41.0 %collective-permute-start.20 = (bf16[12,2,64,128]{3,2,1,0:T(8,128)(2,1)}, bf16[12,2,64,128]{3,2,1,0:T(8,128)(2,1)S(1)}, u32[]{:S(2)}, u32[]{:S(2)}) collective-permute-start(bf16[12,2,64,128]{3,2,1,0:T(8,128)(2,1)} %get-tuple-element.103), channel_id=1, source_target_pairs={{0,14},{2,0},{4,2},{6,4},{8,6},{10,8},{12,10},{14,12},{1,15},{3,1}... | collective-permute-start | bytes 1179656 | tf_op jit(solution)/shard_map/ppermute | solution.py:287
  241.4 44.1 %collective-permute-start.21 = (bf16[12,2,64,128]{3,2,1,0:T(8,128)(2,1)}, bf16[12,2,64,128]{3,2,1,0:T(8,128)(2,1)S(1)}, u32[]{:S(2)}, u32[]{:S(2)}) collective-permute-start(bf16[12,2,64,128]{3,2,1,0:T(8,128)(2,1)} %get-tuple-element.104), channel_id=1, source_target_pairs={{0,2},{2,4},{4,6},{6,8},{8,10},{10,12},{12,14},{14,0},{1,3},{3,5},... | collective-permute-start | bytes 1179656 | tf_op jit(solution)/shard_map/ppermute | solution.py:287
  253.1 51.6 %collective-permute-start.15 = (bf16[12,2,64,128]{3,2,1,0:T(8,128)(2,1)}, bf16[12,2,64,128]{3,2,1,0:T(8,128)(2,1)S(1)}, u32[]{:S(2)}, u32[]{:S(2)}) collective-permute-start(bf16[12,2,64,128]{3,2,1,0:T(8,128)(2,1)} %get-tuple-element.94), channel_id=1, source_target_pairs={{0,8},{2,10},{4,12},{6,14},{8,0},{10,2},{12,4},{14,6},{1,9},{3,11}... | collective-permute-start | bytes 1179656 | tf_op jit(solution)/shard_map/ppermute | solution.py:287
  257.2 48.4 %collective-permute-start.16 = (bf16[12,2,64,128]{3,2,1,0:T(8,128)(2,1)}, bf16[12,2,64,128]{3,2,1,0:T(8,128)(2,1)S(1)}, u32[]{:S(2)}, u32[]{:S(2)}) collective-permute-start(bf16[12,2,64,128]{3,2,1,0:T(8,128)(2,1)} %get-tuple-element.95), channel_id=1, source_target_pairs={{0,10},{2,12},{4,14},{6,0},{8,2},{10,4},{12,6},{14,8},{1,11},{3,13... | collective-permute-start | bytes 1179656 | tf_op jit(solution)/shard_map/ppermute | solution.py:287
  263.4 44.8 %collective-permute-start.17 = (bf16[12,2,64,128]{3,2,1,0:T(8,128)(2,1)}, bf16[12,2,64,128]{3,2,1,0:T(8,128)(2,1)S(1)}, u32[]{:S(2)}, u32[]{:S(2)}) collective-permute-start(bf16[12,2,64,128]{3,2,1,0:T(8,128)(2,1)} %get-tuple-element.96), channel_id=1, source_target_pairs={{0,6},{2,8},{4,10},{6,12},{8,14},{10,0},{12,2},{14,4},{1,7},{3,9},... | collective-permute-start | bytes 1179656 | tf_op jit(solution)/shard_map/ppermute | solution.py:287
  312.9 76.2 %all-to-all-start.4 = ((bf16[16,2,128,128]{3,2,1,0:T(8,128)(2,1)}), bf16[16,2,128,128]{3,2,1,0:T(8,128)(2,1)S(1)}, u32[]{:S(2)}, u32[]{:S(2)}) async-start(bf16[16,2,128,128]{3,2,1,0:T(8,128)(2,1)} %unpack.2), calls=%async_computation.4 | async-start | bytes 2097152 | tf_op jit(solution)/shard_map/all_to_all | solution.py:280
  320.2 27.2 %collective-permute-start.22 = (bf16[12,2,64,128]{3,2,1,0:T(8,128)(2,1)}, bf16[12,2,64,128]{3,2,1,0:T(8,128)(2,1)S(1)}, u32[]{:S(2)}, u32[]{:S(2)}) collective-permute-start(bf16[12,2,64,128]{3,2,1,0:T(8,128)(2,1)} %get-tuple-element.114), channel_id=1, source_target_pairs={{0,8},{2,10},{4,12},{6,14},{8,0},{10,2},{12,4},{14,6},{1,9},{3,11}... | collective-permute-start | bytes 1179656 | tf_op jit(solution)/shard_map/ppermute | solution.py:287
  329.1 43.5 %collective-permute-start.23 = (bf16[12,2,64,128]{3,2,1,0:T(8,128)(2,1)}, bf16[12,2,64,128]{3,2,1,0:T(8,128)(2,1)S(1)}, u32[]{:S(2)}, u32[]{:S(2)}) collective-permute-start(bf16[12,2,64,128]{3,2,1,0:T(8,128)(2,1)} %get-tuple-element.115), channel_id=1, source_target_pairs={{0,10},{2,12},{4,14},{6,0},{8,2},{10,4},{12,6},{14,8},{1,11},{3,13... | collective-permute-start | bytes 1179656 | tf_op jit(solution)/shard_map/ppermute | solution.py:287
  332.3 40.3 %collective-permute-start.24 = (bf16[12,2,64,128]{3,2,1,0:T(8,128)(2,1)}, bf16[12,2,64,128]{3,2,1,0:T(8,128)(2,1)S(1)}, u32[]{:S(2)}, u32[]{:S(2)}) collective-permute-start(bf16[12,2,64,128]{3,2,1,0:T(8,128)(2,1)} %get-tuple-element.116), channel_id=1, source_target_pairs={{0,6},{2,8},{4,10},{6,12},{8,14},{10,0},{12,2},{14,4},{1,7},{3,9},... | collective-permute-start | bytes 1179656 | tf_op jit(solution)/shard_map/ppermute | solution.py:287
  332.9 43.4 %collective-permute-start.25 = (bf16[12,2,64,128]{3,2,1,0:T(8,128)(2,1)}, bf16[12,2,64,128]{3,2,1,0:T(8,128)(2,1)S(1)}, u32[]{:S(2)}, u32[]{:S(2)}) collective-permute-start(bf16[12,2,64,128]{3,2,1,0:T(8,128)(2,1)} %get-tuple-element.117), channel_id=1, source_target_pairs={{0,12},{2,14},{4,0},{6,2},{8,4},{10,6},{12,8},{14,10},{1,13},{3,15... | collective-permute-start | bytes 1179656 | tf_op jit(solution)/shard_map/ppermute | solution.py:287
  336.6 44.3 %collective-permute-start.26 = (bf16[12,2,64,128]{3,2,1,0:T(8,128)(2,1)}, bf16[12,2,64,128]{3,2,1,0:T(8,128)(2,1)}, u32[]{:S(2)}, u32[]{:S(2)}) collective-permute-start(bf16[12,2,64,128]{3,2,1,0:T(8,128)(2,1)} %get-tuple-element.118), channel_id=1, source_target_pairs={{0,4},{2,6},{4,8},{6,10},{8,12},{10,14},{12,0},{14,2},{1,5},{3,7},... | collective-permute-start | bytes 1179656 | tf_op jit(solution)/shard_map/ppermute | solution.py:287
  347.3 34.5 %collective-permute-start.27 = (bf16[12,2,64,128]{3,2,1,0:T(8,128)(2,1)}, bf16[12,2,64,128]{3,2,1,0:T(8,128)(2,1)}, u32[]{:S(2)}, u32[]{:S(2)}) collective-permute-start(bf16[12,2,64,128]{3,2,1,0:T(8,128)(2,1)} %get-tuple-element.119), channel_id=1, source_target_pairs={{0,14},{2,0},{4,2},{6,4},{8,6},{10,8},{12,10},{14,12},{1,15},{3,1}... | collective-permute-start | bytes 1179656 | tf_op jit(solution)/shard_map/ppermute | solution.py:287
  372.6 23.7 %collective-permute-start.29 = (bf16[16,2,128,128]{3,2,1,0:T(8,128)(2,1)}, bf16[16,2,128,128]{3,2,1,0:T(8,128)(2,1)S(1)}, u32[]{:S(2)}, u32[]{:S(2)}) collective-permute-start(bf16[16,2,128,128]{3,2,1,0:T(8,128)(2,1)} %get-tuple-element.121), channel_id=1, source_target_pairs={{0,1},{1,0},{2,3},{3,2},{4,5},{5,4},{6,7},{7,6},{8,9},{9,8},{10,11... | collective-permute-start | bytes 3145736 | tf_op jit(solution)/shard_map/ppermute | solution.py:405
  (37 other events, 377.9 us)
